TPU v7x, 128 devices: a whole 4x4x4 slice. The times are simulated.
128 devices in a mesh: tile: 8 (over x, core), tm: 16 (over y, z).
Axes of the slice: x: 4, y: 4, z: 4, core: 2. Of those that a mesh axis runs over, the one named last changes fastest.
Arguments:
- movie: bfloat16 [256, 256, 1024], P('tile', None, 'tm'), may hold values from -6 to 6
- footprints: bfloat16 [64, 4, 32, 32, 128], P('tile'), may hold values from -0.5 to 0.5
- support: int32 [64, 4], P('tile'), may hold values from -1 to 31, as said below
- cycle_offsets: int32 [48, 2], replicated, may hold values from -8 to 8, as said below
- cycle_weights: float32 [48, 256, 256], P(None, 'tile'), may hold values from -0.875 to 0.875
- owner_map: int32 [32], replicated, may hold values from 0 to 31, each once
- traces_old: bfloat16 [4096, 1024], P(('tile', 'tm')), may hold values from 0 to 2
- taps: float32 [129], replicated, may hold values from -0.5 to 0.5
Outputs:
- residual: bfloat16 [256, 256, 1024], P('tile', None, 'tm')
- traces_new: bfloat16 [4096, 1024], P(('tile', 'tm'))
Inputs may be any that keep to these rules, and one draw needn't show every extreme that they name: `support`: in every row the live slots come first and name distinct blocks; -1 marks the empty slots. Every tile has 1 to 4 live slots, and every tile row (the 8 tiles t with equal t // 8) has exactly 20 live slots in all. `cycle_offsets`: rows are distinct (row offset, column offset) pairs; each has max(|row offset|, |column offset|) between 6 and 8; one row offset is 8 and one is -8. `owner_map`: each block has its own position.
All inputs are finite; a program needn't handle non-finite values.
Results may differ from a plain program's by a relative error of at most 0.0075.
Values may be sent and summed in bfloat16 or wider, within the bound.
A program may use at most 128 MiB of HBM per device.

v0:
```python
import jax
import jax.numpy as jnp
from jax import lax
from jax.sharding import PartitionSpec as P

TILE = 32
BLOCK = 128
NBLK = 32
RAD = 8
TBLK = 256


ridge_term = 1.0
highest = lax.Precision.HIGHEST


def padded_2(array, sides, width):
    for axis, dim in sides:
        peers, length = (lax.axis_size(axis), array.shape[dim])
        up = [(i, (i + 1) % peers) for i in range(peers - 1)]
        down = [(j, i) for i, j in up]
        last = lax.slice_in_dim(array, length - width, length, axis=dim)
        initial = lax.slice_in_dim(array, 0, width, axis=dim)
        before = lax.ppermute(last, axis, up)
        after = lax.ppermute(initial, axis, down)
        array = jnp.concatenate([before, array, after], axis=dim)
    return array


def cycle_sum(padded, weights, cycle_offsets, out_rows, col_count):
    frames = padded.shape[2]
    running = jnp.zeros((out_rows, col_count, frames), jnp.float32)
    for cycle_index in range(cycle_offsets.shape[0]):
        start_row = RAD + cycle_offsets[cycle_index, 0]
        start_col = RAD + cycle_offsets[cycle_index, 1]
        shifted = lax.dynamic_slice(
            padded, (start_row, start_col, jnp.zeros((), jnp.int32)), (out_rows, col_count, frames)
        )
        running = running + weights[cycle_index][:, :, None] * shifted.astype(jnp.float32)
    return running


def widen_cols(field_in):
    return jnp.pad(field_in, ((0, 0), (RAD, RAD), (0, 0)))


def clean_rows(field_in, weights, cycle_offsets):
    extended = padded_2(field_in, (("tile", 0),), RAD)
    backdrop = cycle_sum(
        widen_cols(extended), weights, cycle_offsets, field_in.shape[0], field_in.shape[1]
    )
    return (field_in.astype(jnp.float32) - backdrop).astype(jnp.bfloat16)


def to_tiles(owned):
    group_traces = lax.all_to_all(owned, "tm", split_axis=1, concat_axis=0, tiled=True)
    return lax.all_gather(group_traces, "tile", axis=0, tiled=True)


def neural_part(footprints, live_slot, position, traces_full, row_count, col_count):
    frame_count = traces_full.shape[1]
    blocks = traces_full.reshape(NBLK, BLOCK, frame_count)
    picked = jnp.take(blocks, jnp.maximum(position, 0), axis=0)
    picked = jnp.where(live_slot[:, :, None, None], picked, jnp.zeros((), jnp.bfloat16))
    neural_image = jnp.einsum(
        "tkrcn,tknf->rtcf", footprints, picked, preferred_element_type=jnp.float32
    )
    return neural_image.reshape(row_count, col_count, frame_count)


def band_tables(taps):
    half_taps = (taps.shape[0] - 1) // 2
    source_pos = jnp.arange(TBLK, dtype=jnp.int32)[:, None]
    target_pos = jnp.arange(TBLK, dtype=jnp.int32)[None, :]
    matrices = []
    for block_shift in (-1, 0, 1):
        tap_ids = target_pos - source_pos - block_shift * TBLK + half_taps
        inside = (tap_ids >= 0) & (tap_ids <= 2 * half_taps)
        matrices.append(jnp.where(inside, taps[jnp.clip(tap_ids, 0, 2 * half_taps)], 0.0))
    return matrices


def wiener_blocks(update, taps):
    owned_count, frames = update.shape
    block_total = frames // TBLK
    blocks = update.reshape(owned_count, block_total, TBLK)
    empty_block = jnp.zeros((owned_count, 1, TBLK), jnp.float32)
    before = jnp.concatenate([empty_block, blocks[:, :-1]], axis=1)
    after_blocks = jnp.concatenate([blocks[:, 1:], empty_block], axis=1)
    matrices = band_tables(taps)
    running = jnp.einsum("nbs,st->nbt", before, matrices[0], precision=highest)
    running = running + jnp.einsum("nbs,st->nbt", blocks, matrices[1], precision=highest)
    running = running + jnp.einsum("nbs,st->nbt", after_blocks, matrices[2], precision=highest)
    return running.reshape(owned_count, frames)


def body(movie, footprints, support, cycle_offsets, cycle_weights, owner_map, traces_old, taps):
    row_count, col_count, frames = movie.shape
    tile_count = lax.axis_size("tile")
    time_count = lax.axis_size("tm")
    owned_count = traces_old.shape[0]
    tiles_here, slot_count = support.shape
    live_slot = support >= 0
    block_ids = jnp.arange(NBLK, dtype=jnp.int32)
    matches = jnp.maximum(support, 0)[:, :, None] == block_ids
    position = jnp.sum(jnp.where(matches, owner_map, 0), axis=2)
    neural_old = neural_part(
        footprints, live_slot, position, to_tiles(traces_old), row_count, col_count
    )
    first_res = (movie.astype(jnp.float32) - neural_old).astype(jnp.bfloat16)
    second_res = clean_rows(first_res, cycle_weights, cycle_offsets)
    third_res = clean_rows(second_res, cycle_weights, cycle_offsets)
    tile_view = third_res.reshape(row_count, tiles_here, TILE, frames)
    slot_proj = jnp.einsum(
        "tkrcn,rtcf->tknf", footprints, tile_view, preferred_element_type=jnp.float32
    )
    selector = (
        (position.reshape(-1)[None, :] == block_ids[:, None]) & live_slot.reshape(-1)[None, :]
    ).astype(jnp.float32)
    partial_sums = jnp.einsum(
        "bs,snf->bnf",
        selector,
        slot_proj.reshape(tiles_here * slot_count, BLOCK, frames),
        precision=highest,
    ).reshape(NBLK * BLOCK, frames)
    footprint_f = footprints.astype(jnp.float32)
    squares = jnp.sum(footprint_f * footprint_f, axis=(2, 3)).reshape(
        tiles_here * slot_count, BLOCK
    )
    partial_norms = jnp.dot(selector, squares, precision=highest).reshape(NBLK * BLOCK)
    tile_here = lax.axis_index("tile")
    time_here = lax.axis_index("tm")
    delivered = lax.all_to_all(
        partial_sums, ("tile", "tm"), split_axis=0, concat_axis=1, tiled=True
    )
    owned_sums = jnp.sum(
        delivered.reshape(owned_count, tile_count, time_count, frames), axis=1
    ).reshape(owned_count, time_count * frames)
    total_norms = lax.psum(partial_norms, "tile")
    owned_norms = lax.dynamic_slice_in_dim(
        total_norms, (tile_here * time_count + time_here) * owned_count, owned_count
    )
    update = traces_old.astype(jnp.float32) + owned_sums / (owned_norms[:, None] + ridge_term)
    filtered = wiener_blocks(update, taps)
    fresh_traces = jnp.maximum(filtered, 0.0).astype(jnp.bfloat16)
    neural_new = neural_part(
        footprints, live_slot, position, to_tiles(fresh_traces), row_count, col_count
    )
    residual = (third_res.astype(jnp.float32) + neural_old - neural_new).astype(jnp.bfloat16)
    return (residual, fresh_traces)


def solution(mesh):
    return jax.shard_map(
        body,
        mesh=mesh,
        in_specs=(
            P("tile", None, "tm"),
            P("tile", None, None, None, None),
            P("tile", None),
            P(),
            P(None, "tile", None),
            P(),
            P(("tile", "tm"), None),
            P(),
        ),
        out_specs=(P("tile", None, "tm"), P(("tile", "tm"), None)),
        check_vma=False,
    )
```

profile of v0, /device:TPU:1, one launch (start us, length us, event | category | flops | bytes accessed | tf_op | source)
XLA Modules:
  0.0 1705.5 jit_solution(5099692638520922296)
XLA Ops:
  0.7 1.1 all_to_all.38
  2.6 8.6 all-to-all-start
  11.8 0.9 select_reduce_fusion
  13.4 1.3 slice.738
  14.7 2.1 fusion.89
  41.8 2.1 fusion.90
  67.8 2.1 fusion.87
  93.8 2.1 fusion.88
  119.5 2.1 fusion.91
  124.2 0.9 slice_bitcast_fusion.45
  125.2 1.9 slice_bitcast_fusion.47
  128.4 1.8 copy.133
  130.3 14.8 all_gather.6
  146.2 5.8 convolution_bitcast_fusion.1
  152.6 0.9 copy-done.7
  154.2 1.6 fusion.86
  155.9 3.1 collective-permute-start
  159.1 2.1 collective-permute-start.1
  183.5 1.1 slice_bitcast_fusion.46
  184.9 2.5 select_maximum_fusion.2
  187.6 83.5 %subtract_convert_fusion.1 = bf16[32,256,64]{2,1,0:T(8,128)(2,1)S(1)} fusion(bf16[32,256,64]{2,1,0:T(8,128)(2,1)S(1)} %fusion.2, bf16[48,272,64]{2,1,0:T(8,128)(2,1)S(1)} %select_maximum_fusion.2, s32[]{:T(128)S(6)} %select_n.541, s32[]{:T(128)S(6)} %select_n.542, f32[32,256]{1,0:T(8,128)S(1)} %get-tuple-element.63, s32[]{:T(128)S(6)} %select_n.539, ...), kind=kLoop, calls=%fused_computation.15 | loop fusion | flops 76546048 | bytes 54002048 | tf_op jit(solution)/shard_map/convert_element_type | solution.py:52
  271.3 1.3 copy-done.3
  272.6 1.1 fusion.85
  273.8 3.8 collective-permute-start.2
  277.6 2.1 collective-permute-start.3
  281.1 2.9 collective-permute-done.2
  284.0 4.4 collective-permute-done.3
  288.4 3.0 select_maximum_fusion
  291.7 87.4 %subtract_convert_fusion = bf16[32,256,64]{2,1,0:T(8,128)(2,1)S(1)} fusion(bf16[32,256,64]{2,1,0:T(8,128)(2,1)S(1)} %copy-done.4, bf16[48,272,64]{2,1,0:T(8,128)(2,1)S(1)} %select_maximum_fusion, s32[]{:T(128)S(6)} %select_n.541, s32[]{:T(128)S(6)} %select_n.542, s32[]{:T(128)S(6)} %select_n.539, s32[]{:T(128)S(6)} %select_n.540, s32[]{:T(128)S(6)} %select_n.537, ...), kind=kLoop, calls=%fused_computation.14 | loop fusion | flops 76546048 | bytes 54002048 | tf_op jit(solution)/shard_map/convert_element_type | solution.py:52
  379.1 1.6 fusion.4
  380.7 1.3 fusion.9
  382.8 2.3 reshape.653
  385.0 9.4 all-to-all-start.1
  395.2 408.0 %gather_fusion.2 = f32[65536]{0:T(1024)S(1)} fusion(f32[129]{0:T(256)S(1)} %copy-done, s32[65536]{0:T(1024)S(1)} %copy-done.12), kind=kCustom, calls=%fused_computation.4 | custom fusion | bytes 786432 | tf_op jit(solution)/shard_map/gather | solution.py:79
  803.2 0.8 reshape.619
  804.0 408.0 %gather_fusion.1 = f32[65536]{0:T(1024)S(1)} fusion(f32[129]{0:T(256)S(1)} %copy-done, s32[65536]{0:T(1024)S(1)} %copy-done.13), kind=kCustom, calls=%fused_computation.3 | custom fusion | bytes 786432 | tf_op jit(solution)/shard_map/gather | solution.py:79
  1212.7 408.0 %gather_fusion = f32[65536]{0:T(1024)S(1)} fusion(f32[129]{0:T(256)S(1)} %copy-done, s32[65536]{0:T(1024)S(1)} %copy-done.14), kind=kCustom, calls=%fused_computation.2 | custom fusion | bytes 786432 | tf_op jit(solution)/shard_map/gather | solution.py:79
  1621.5 5.0 multiply_reduce_fusion
  1626.7 22.9 %psum.7 = f32[4096]{0:T(1024)S(1)} all-reduce(f32[4096]{0:T(1024)S(1)} %convolution_bitcast_fusion.2), channel_id=1, replica_groups=mesh['tile'=8,'tm'=16] {'tile'}, use_global_device_ids=true, to_apply=%region_3.5 | all-reduce | flops 4096 | bytes 32768 | tf_op jit(solution)/shard_map/psum | solution.py:139
  1650.1 4.5 reduce
  1654.6 0.8 reshape.654
  1658.1 7.0 all-to-all-start.2
  1665.7 5.9 all-to-all-done.2
  1671.8 19.0 %all_gather.7 = bf16[4096,64]{1,0:T(8,128)(2,1)S(1)} all-gather(bf16[512,64]{1,0:T(8,128)(2,1)S(1)} %bitcast.415), channel_id=1, replica_groups=mesh['tile'=8,'tm'=16] {'tile'}, dimensions={0}, use_global_device_ids=true | all-gather | bytes 589824 | tf_op jit(solution)/shard_map/all_gather | solution.py:57
  1691.9 5.8 convolution_bitcast_fusion
  1698.2 1.7 copy-done.2
  1700.6 2.3 fusion.1
  1702.9 2.7 copy.160
  (250 shorter events, 17.0 us)
Async XLA Ops:
  0.6 394.5 %copy-start = (f32[129]{0:T(256)S(1)}, f32[129]{0:T(256)}, u32[]{:S(2)}) copy-start(f32[129]{0:T(256)} %param.17) | copy-start | bytes 1552
  0.6 127.7 %copy-start.8 = (bf16[32,256,64]{1,2,0:T(8,128)(2,1)S(1)}, bf16[32,256,64]{1,2,0:T(8,128)(2,1)}, u32[]{:S(2)}) copy-start(bf16[32,256,64]{1,2,0:T(8,128)(2,1)} %param.10) | copy-start | bytes 3145732
  2.6 127.6 %all-to-all-start = ((bf16[16,2,1024]{2,1,0:T(2,128)(2,1)}), bf16[16,2,1024]{2,1,0:T(2,128)(2,1)S(1)}, u32[]{:S(2)}, u32[]{:S(2)}) async-start(bf16[16,2,1024]{2,1,0:T(2,128)(2,1)} %reshape.651), calls=%async_computation | async-start | bytes 131072 | tf_op jit(solution)/shard_map/all_to_all | solution.py:56
  125.1 62.2 %copy-start.15 = (f32[32,256]{1,0:T(8,128)}, f32[32,256]{1,0:T(8,128)S(1)}, u32[]{:S(2)}) copy-start(f32[32,256]{1,0:T(8,128)S(1)} %get-tuple-element.59) | copy-start | bytes 98308
  125.2 62.2 %copy-start.17 = (f32[32,256]{1,0:T(8,128)}, f32[32,256]{1,0:T(8,128)S(1)}, u32[]{:S(2)}) copy-start(f32[32,256]{1,0:T(8,128)S(1)} %get-tuple-element.60) | copy-start | bytes 98308
  125.2 62.2 %copy-start.19 = (f32[32,256]{1,0:T(8,128)}, f32[32,256]{1,0:T(8,128)S(1)}, u32[]{:S(2)}) copy-start(f32[32,256]{1,0:T(8,128)S(1)} %get-tuple-element.61) | copy-start | bytes 98308
  125.2 62.2 %copy-start.21 = (f32[32,256]{1,0:T(8,128)}, f32[32,256]{1,0:T(8,128)S(1)}, u32[]{:S(2)}) copy-start(f32[32,256]{1,0:T(8,128)S(1)} %get-tuple-element.62) | copy-start | bytes 98308
  125.2 62.2 %copy-start.23 = (f32[32,256]{1,0:T(8,128)}, f32[32,256]{1,0:T(8,128)S(1)}, u32[]{:S(2)}) copy-start(f32[32,256]{1,0:T(8,128)S(1)} %get-tuple-element.63) | copy-start | bytes 98308
  125.2 62.2 %copy-start.25 = (f32[32,256]{1,0:T(8,128)}, f32[32,256]{1,0:T(8,128)S(1)}, u32[]{:S(2)}) copy-start(f32[32,256]{1,0:T(8,128)S(1)} %get-tuple-element.64) | copy-start | bytes 98308
  127.1 60.3 %copy-start.27 = (f32[32,256]{1,0:T(8,128)}, f32[32,256]{1,0:T(8,128)S(1)}, u32[]{:S(2)}) copy-start(f32[32,256]{1,0:T(8,128)S(1)} %get-tuple-element.17) | copy-start | bytes 98308
  127.1 60.3 %copy-start.29 = (f32[32,256]{1,0:T(8,128)}, f32[32,256]{1,0:T(8,128)S(1)}, u32[]{:S(2)}) copy-start(f32[32,256]{1,0:T(8,128)S(1)} %get-tuple-element.18) | copy-start | bytes 98308
  127.2 19.0 %copy-start.87 = (pred[8,4]{1,0:T(8,128)(4,1)}, pred[8,4]{1,0:T(8,128)(4,1)S(1)}, u32[]{:S(2)}) copy-start(pred[8,4]{1,0:T(8,128)(4,1)S(1)} %copy.135) | copy-start | bytes 100
  127.3 153.2 %copy-start.89 = (pred[8,4]{1,0:T(8,128)(4,1)}, pred[8,4]{1,0:T(8,128)(4,1)S(1)}, u32[]{:S(2)}) copy-start(pred[8,4]{1,0:T(8,128)(4,1)S(1)} %copy.134) | copy-start | bytes 100
  130.1 21.8 %copy-start.91 = (s32[1024]{0:T(1024)}, s32[1024]{0:T(1024)S(1)}, u32[]{:S(2)}) copy-start(s32[1024]{0:T(1024)S(1)} %pad_clamp_fusion) | copy-start | bytes 12292
  155.9 28.9 %collective-permute-start = (bf16[8,256,64]{2,1,0:T(8,128)(2,1)}, bf16[8,256,64]{2,1,0:T(8,128)(2,1)S(1)}, u32[]{:S(2)}, u32[]{:S(2)}) collective-permute-start(bf16[8,256,64]{2,1,0:T(8,128)(2,1)} %get-tuple-element.15), channel_id=1, source_target_pairs={{0,16},{16,32},{32,48},{48,64},{64,80},{80,96},{96,112},{1,17},{17... | collective-permute-start | bytes 786440 | tf_op jit(solution)/shard_map/ppermute | solution.py:24
  159.1 25.8 %collective-permute-start.1 = (bf16[8,256,64]{2,1,0:T(8,128)(2,1)}, bf16[8,256,64]{2,1,0:T(8,128)(2,1)}, u32[]{:S(2)}, u32[]{:S(2)}) collective-permute-start(bf16[8,256,64]{2,1,0:T(8,128)(2,1)} %get-tuple-element.16), channel_id=1, source_target_pairs={{16,0},{32,16},{48,32},{64,48},{80,64},{96,80},{112,96},{17,1},{33... | collective-permute-start | bytes 786440 | tf_op jit(solution)/shard_map/ppermute | solution.py:25
  184.7 86.5 %copy-start.48 = (f32[32,256]{1,0:T(8,128)}, f32[32,256]{1,0:T(8,128)S(1)}, u32[]{:S(2)}) copy-start(f32[32,256]{1,0:T(8,128)S(1)} %get-tuple-element.36) | copy-start | bytes 98308
  184.7 86.5 %copy-start.50 = (f32[32,256]{1,0:T(8,128)}, f32[32,256]{1,0:T(8,128)S(1)}, u32[]{:S(2)}) copy-start(f32[32,256]{1,0:T(8,128)S(1)} %get-tuple-element.37) | copy-start | bytes 98308
  184.7 86.5 %copy-start.52 = (f32[32,256]{1,0:T(8,128)}, f32[32,256]{1,0:T(8,128)S(1)}, u32[]{:S(2)}) copy-start(f32[32,256]{1,0:T(8,128)S(1)} %get-tuple-element.38) | copy-start | bytes 98308
  184.7 86.5 %copy-start.54 = (f32[32,256]{1,0:T(8,128)}, f32[32,256]{1,0:T(8,128)S(1)}, u32[]{:S(2)}) copy-start(f32[32,256]{1,0:T(8,128)S(1)} %get-tuple-element.39) | copy-start | bytes 98308
  184.7 86.5 %copy-start.56 = (f32[32,256]{1,0:T(8,128)}, f32[32,256]{1,0:T(8,128)S(1)}, u32[]{:S(2)}) copy-start(f32[32,256]{1,0:T(8,128)S(1)} %get-tuple-element.40) | copy-start | bytes 98308
  184.7 86.5 %copy-start.58 = (f32[32,256]{1,0:T(8,128)}, f32[32,256]{1,0:T(8,128)S(1)}, u32[]{:S(2)}) copy-start(f32[32,256]{1,0:T(8,128)S(1)} %get-tuple-element.41) | copy-start | bytes 98308
  184.7 86.5 %copy-start.60 = (f32[32,256]{1,0:T(8,128)}, f32[32,256]{1,0:T(8,128)S(1)}, u32[]{:S(2)}) copy-start(f32[32,256]{1,0:T(8,128)S(1)} %get-tuple-element.42) | copy-start | bytes 98308
  184.7 86.5 %copy-start.62 = (f32[32,256]{1,0:T(8,128)}, f32[32,256]{1,0:T(8,128)S(1)}, u32[]{:S(2)}) copy-start(f32[32,256]{1,0:T(8,128)S(1)} %get-tuple-element.43) | copy-start | bytes 98308
  184.7 86.5 %copy-start.64 = (f32[32,256]{1,0:T(8,128)}, f32[32,256]{1,0:T(8,128)S(1)}, u32[]{:S(2)}) copy-start(f32[32,256]{1,0:T(8,128)S(1)} %get-tuple-element.44) | copy-start | bytes 98308
  184.8 86.5 %copy-start.66 = (f32[32,256]{1,0:T(8,128)}, f32[32,256]{1,0:T(8,128)S(1)}, u32[]{:S(2)}) copy-start(f32[32,256]{1,0:T(8,128)S(1)} %get-tuple-element.45) | copy-start | bytes 98308
  184.8 86.5 %copy-start.68 = (f32[32,256]{1,0:T(8,128)}, f32[32,256]{1,0:T(8,128)S(1)}, u32[]{:S(2)}) copy-start(f32[32,256]{1,0:T(8,128)S(1)} %get-tuple-element.46) | copy-start | bytes 98308
  184.8 86.5 %copy-start.70 = (f32[32,256]{1,0:T(8,128)}, f32[32,256]{1,0:T(8,128)S(1)}, u32[]{:S(2)}) copy-start(f32[32,256]{1,0:T(8,128)S(1)} %get-tuple-element.47) | copy-start | bytes 98308
  184.8 86.5 %copy-start.72 = (f32[32,256]{1,0:T(8,128)}, f32[32,256]{1,0:T(8,128)S(1)}, u32[]{:S(2)}) copy-start(f32[32,256]{1,0:T(8,128)S(1)} %get-tuple-element.48) | copy-start | bytes 98308
  184.8 86.5 %copy-start.74 = (f32[32,256]{1,0:T(8,128)}, f32[32,256]{1,0:T(8,128)S(1)}, u32[]{:S(2)}) copy-start(f32[32,256]{1,0:T(8,128)S(1)} %get-tuple-element.49) | copy-start | bytes 98308
  184.8 86.5 %copy-start.76 = (f32[32,256]{1,0:T(8,128)}, f32[32,256]{1,0:T(8,128)S(1)}, u32[]{:S(2)}) copy-start(f32[32,256]{1,0:T(8,128)S(1)} %get-tuple-element.50) | copy-start | bytes 98308
  184.8 86.5 %copy-start.78 = (f32[32,256]{1,0:T(8,128)}, f32[32,256]{1,0:T(8,128)S(1)}, u32[]{:S(2)}) copy-start(f32[32,256]{1,0:T(8,128)S(1)} %get-tuple-element.51) | copy-start | bytes 98308
  184.8 86.5 %copy-start.80 = (f32[32,256]{1,0:T(8,128)}, f32[32,256]{1,0:T(8,128)S(1)}, u32[]{:S(2)}) copy-start(f32[32,256]{1,0:T(8,128)S(1)} %get-tuple-element.52) | copy-start | bytes 98308
  184.8 86.5 %copy-start.82 = (f32[32,256]{1,0:T(8,128)}, f32[32,256]{1,0:T(8,128)S(1)}, u32[]{:S(2)}) copy-start(f32[32,256]{1,0:T(8,128)S(1)} %get-tuple-element.53) | copy-start | bytes 98308
  184.8 86.5 %copy-start.84 = (f32[32,256]{1,0:T(8,128)}, f32[32,256]{1,0:T(8,128)S(1)}, u32[]{:S(2)}) copy-start(f32[32,256]{1,0:T(8,128)S(1)} %get-tuple-element.54) | copy-start | bytes 98308
  273.8 10.2 collective-permute-start.2
  277.6 10.8 collective-permute-start.3
  280.7 100.0 %copy-start.95 = (pred[32]{0:T(512)(128)(4,1)}, pred[32]{0:T(512)(128)(4,1)S(1)}, u32[]{:S(2)}) copy-start(pred[32]{0:T(512)(128)(4,1)S(1)} %and.25) | copy-start | bytes 100
  280.8 99.9 %copy-start.93 = (s32[32]{0:T(128)}, s32[32]{0:T(128)S(1)}, u32[]{:S(2)}) copy-start(s32[32]{0:T(128)S(1)} %eq.31) | copy-start | bytes 388
  288.4 90.6 %slice-start = ((s8[8388608]{0:T(1024)(128)(4,1)}), s8[4194304]{0:T(1024)(128)(4,1)S(1)}, s32[]{:S(2)}) async-start(s8[8388608]{0:T(1024)(128)(4,1)} %bitcast.396), calls=%async_computation.3 | async-start | bytes 8388608
  291.7 87.4 %slice-start.1 = ((s8[8388608]{0:T(1024)(128)(4,1)}), s8[4194304]{0:T(1024)(128)(4,1)S(1)}, s32[]{:S(2)}) async-start(s8[8388608]{0:T(1024)(128)(4,1)} %bitcast.396), calls=%async_computation.4 | async-start | bytes 8388608
  385.0 1264.6 %all-to-all-start.1 = ((f32[128,1,2048]{2,1,0:T(1,128)}), f32[128,1,2048]{2,1,0:T(1,128)}, u32[]{:S(2)}, u32[]{:S(2)}) async-start(f32[128,1,2048]{2,1,0:T(1,128)} %reshape.653), calls=%async_computation.1 | async-start | bytes 2097152 | tf_op jit(solution)/shard_map/all_to_all | solution.py:133
  395.2 408.8 %copy-start.13 = (s32[65536]{0:T(1024)S(1)}, s32[65536]{0:T(1024)}, u32[]{:S(2)}) copy-start(s32[65536]{0:T(1024)} %broadcast_clamp_fusion.1) | copy-start | bytes 786436
  804.0 408.8 %copy-start.14 = (s32[65536]{0:T(1024)S(1)}, s32[65536]{0:T(1024)}, u32[]{:S(2)}) copy-start(s32[65536]{0:T(1024)} %broadcast_clamp_fusion.2) | copy-start | bytes 786436
  1655.7 35.5 %copy-start.92 = (s32[1024]{0:T(1024)S(1)}, s32[1024]{0:T(1024)}, u32[]{:S(2)}) copy-start(s32[1024]{0:T(1024)} %copy-done.91) | copy-start | bytes 12292
  1656.0 35.9 %copy-start.88 = (pred[8,4]{1,0:T(8,128)(4,1)S(1)}, pred[8,4]{1,0:T(8,128)(4,1)}, u32[]{:S(2)}) copy-start(pred[8,4]{1,0:T(8,128)(4,1)} %copy-done.87) | copy-start | bytes 100
  1656.0 35.9 %copy-start.90 = (pred[8,4]{1,0:T(8,128)(4,1)S(1)}, pred[8,4]{1,0:T(8,128)(4,1)}, u32[]{:S(2)}) copy-start(pred[8,4]{1,0:T(8,128)(4,1)} %copy-done.89) | copy-start | bytes 100
  1658.1 13.6 all-to-all-start.2
  (58 other events, 488.5 us)
where the time goes:
time: 1710 us
  local copies, waits for them, and re-layouts  1270 us (74%)
  other arithmetic  194 us (11%)
  between operations  123 us (7%)
  blocking collectives  56.7 us (3%)
  starting transfers between devices  36.2 us (2%)
    gather x6, local copies, waits for them, and re-layouts, band_tables(): taps[jnp.clip(tap_ids, 0, 2 * half_taps)]  1230 us
    convert_element_type x2, other arithmetic, clean_rows(): return (field_in.astype(jnp.float32) - backdrop).astype(jnp.bfloat16)  171 us
  transfers between devices with their start and end apart: 7, of which 3 were waited for; matrix products, arithmetic and copies ran while one was open for 74% of the time, Pallas kernels for 0%

commit v1 on v0

v1 whole, which is shorter than its diff:
```python
import functools

import jax
import jax.numpy as jnp
from jax import lax
from jax.experimental import pallas as pl
from jax.experimental.pallas import tpu as pltpu
from jax.sharding import PartitionSpec as P

TILE = 32
BLOCK = 128
NBLK = 32
RAD = 8
RIDGE = 1.0
LANES = 128
FCHUNK = 32

SMEM = pltpu.MemorySpace.SMEM


def whole(space=pltpu.MemorySpace.VMEM):
    return pl.BlockSpec(memory_space=space)


def params(limit=48):
    return pltpu.CompilerParams(vmem_limit_bytes=limit * 2**20)


def block_of(support_ref, owner_ref, tile, slot):
    held = support_ref[tile, slot]
    return held >= 0, owner_ref[jnp.maximum(held, 0)]


def first_kernel(support_ref, owner_ref, traces_ref, foot_ref, movie_ref, out_ref, image):
    group = pl.program_id(0)
    tiles, slots = foot_ref.shape[0], foot_ref.shape[1]
    rows, width, frames = movie_ref.shape

    def one_tile(tile, carry):
        columns = pl.ds(pl.multiple_of(tile * TILE, TILE), TILE)
        for slot in range(slots):
            live, position = block_of(support_ref, owner_ref, group * tiles + tile, slot)

            def add(slot=slot, position=position):
                start = pl.multiple_of(position * BLOCK, BLOCK)
                part = jnp.dot(
                    foot_ref[tile, slot],
                    traces_ref[pl.ds(start, BLOCK), :],
                    preferred_element_type=jnp.float32,
                ).reshape(rows, TILE, frames)
                if slot == 0:
                    image[:, columns, :] = part
                else:
                    image[:, columns, :] += part

            if slot == 0:
                add()
            else:
                pl.when(live)(add)
        return carry

    lax.fori_loop(0, tiles, one_tile, 0)

    def two_rows(half, carry):
        row = half * 2
        both = [movie_ref[row + k].astype(jnp.float32) - image[row + k] for k in range(2)]
        turned = jnp.concatenate(both, axis=1).T
        for k in range(2):
            out_ref[row + k] = turned[k * frames : (k + 1) * frames].astype(jnp.bfloat16)
        return carry

    lax.fori_loop(0, rows // 2, two_rows, 0)


def first_residual(support, owner_map, traces, foot, movie):
    tiles, slots = foot.shape[:2]
    rows, cols, frames = movie.shape
    group = LANES // TILE
    return pl.pallas_call(
        first_kernel,
        grid=(tiles // group,),
        out_shape=jax.ShapeDtypeStruct((rows, frames, cols), jnp.bfloat16),
        in_specs=[
            whole(SMEM),
            whole(SMEM),
            whole(),
            pl.BlockSpec((group,) + foot.shape[1:], lambda g: (g, 0, 0, 0)),
            pl.BlockSpec((rows, LANES, frames), lambda g: (0, g, 0)),
        ],
        out_specs=pl.BlockSpec((rows, frames, LANES), lambda g: (0, 0, g)),
        scratch_shapes=[pltpu.VMEM((rows, LANES, frames), jnp.float32)],
        compiler_params=params(),
        name="first_residual",
    )(support, owner_map, traces, foot, movie)


def cycle_kernel(offsets_ref, weights_ref, field_ref, top_ref, bottom_ref, out_ref, padded):
    rows, frames, cols = field_ref.shape
    count = weights_ref.shape[1]
    padded[0:RAD] = top_ref[...].astype(jnp.float32)
    padded[RAD : RAD + rows] = field_ref[...].astype(jnp.float32)
    padded[RAD + rows : rows + 2 * RAD] = bottom_ref[...].astype(jnp.float32)
    lane = lax.broadcasted_iota(jnp.int32, (FCHUNK, LANES), 1)

    def one_row(row, carry):
        def one_chunk(chunk, inner):
            at = pl.ds(pl.multiple_of(chunk * FCHUNK, FCHUNK), FCHUNK)
            low = jnp.zeros((FCHUNK, LANES), jnp.float32)
            high = jnp.zeros((FCHUNK, LANES), jnp.float32)
            for j in range(count):
                down, right = offsets_ref[j, 0], offsets_ref[j, 1]
                source = RAD + row + down
                turn = lax.rem(LANES - right, LANES)
                first = pltpu.roll(padded[source, at, 0:LANES], turn, 1)
                second = pltpu.roll(padded[source, at, LANES : 2 * LANES], turn, 1)
                shifted = lane + right
                stays = (shifted >= 0) & (shifted < LANES)
                weight = weights_ref[row, j : j + 1, :]
                low += weight[:, :LANES] * jnp.where(stays, first, second)
                high += weight[:, LANES:] * jnp.where(stays, second, first)
            mine = padded[RAD + row, at, :]
            out_ref[row, at, 0:LANES] = (mine[:, :LANES] - low).astype(jnp.bfloat16)
            out_ref[row, at, LANES : 2 * LANES] = (mine[:, LANES:] - high).astype(jnp.bfloat16)
            return inner

        return lax.fori_loop(0, frames // FCHUNK, one_chunk, carry)

    lax.fori_loop(0, rows, one_row, 0)


def cycle_pass(offsets, weights, field, top, bottom):
    rows, frames, cols = field.shape
    return pl.pallas_call(
        cycle_kernel,
        out_shape=jax.ShapeDtypeStruct(field.shape, jnp.bfloat16),
        in_specs=[whole(SMEM)] + [whole()] * 4,
        out_specs=whole(),
        scratch_shapes=[pltpu.VMEM((rows + 2 * RAD, frames, cols), jnp.float32)],
        compiler_params=params(),
        name="cycle_pass",
    )(offsets, weights, field, top, bottom)


def project_kernel(support_ref, owner_ref, foot_ref, field_ref, third_ref, sums_ref, norms_ref):
    group = pl.program_id(0)
    tiles, slots, pixels, _ = foot_ref.shape
    rows, frames, width = field_ref.shape

    @pl.when(group == 0)
    def _():
        sums_ref[...] = jnp.zeros_like(sums_ref)
        norms_ref[...] = jnp.zeros_like(norms_ref)

    def two_rows(half, carry):
        row = half * 2
        both = field_ref[pl.ds(row, 2)].reshape(2 * frames, width).astype(jnp.float32)
        turned = both.T.astype(jnp.bfloat16)
        for k in range(2):
            third_ref[row + k] = turned[:, k * frames : (k + 1) * frames]
        return carry

    lax.fori_loop(0, rows // 2, two_rows, 0)

    def one_tile(tile, carry):
        columns = pl.ds(pl.multiple_of(tile * TILE, TILE), TILE)
        view = third_ref[:, columns, :].reshape(pixels, frames)
        for slot in range(slots):
            live, position = block_of(support_ref, owner_ref, group * tiles + tile, slot)

            def add(slot=slot, position=position):
                values = foot_ref[tile, slot]
                sums_ref[position] += lax.dot_general(
                    values, view, (((0,), (0,)), ((), ())), preferred_element_type=jnp.float32
                )
                wide = values.astype(jnp.float32)
                square = jnp.sum((wide * wide).reshape(pixels // 8, 8, BLOCK), axis=0)
                norms_ref[position] += square

            if slot == 0:
                add()
            else:
                pl.when(live)(add)
        return carry

    lax.fori_loop(0, tiles, one_tile, 0)


def project(support, owner_map, foot, field):
    tiles, slots = foot.shape[:2]
    rows, frames, cols = field.shape
    group = LANES // TILE
    return pl.pallas_call(
        project_kernel,
        grid=(tiles // group,),
        out_shape=[
            jax.ShapeDtypeStruct((rows, cols, frames), jnp.bfloat16),
            jax.ShapeDtypeStruct((NBLK, BLOCK, frames), jnp.float32),
            jax.ShapeDtypeStruct((NBLK, 8, BLOCK), jnp.float32),
        ],
        in_specs=[
            whole(SMEM),
            whole(SMEM),
            pl.BlockSpec((group,) + foot.shape[1:], lambda g: (g, 0, 0, 0)),
            pl.BlockSpec((rows, frames, LANES), lambda g: (0, 0, g)),
        ],
        out_specs=[
            pl.BlockSpec((rows, LANES, frames), lambda g: (0, g, 0)),
            pl.BlockSpec((NBLK, BLOCK, frames), lambda g: (0, 0, 0)),
            pl.BlockSpec((NBLK, 8, BLOCK), lambda g: (0, 0, 0)),
        ],
        compiler_params=params(),
        name="project",
    )(support, owner_map, foot, field)


def final_kernel(support_ref, owner_ref, old_ref, new_ref, foot_ref, third_ref, out_ref, change):
    tile = pl.program_id(0)
    slots = foot_ref.shape[1]
    rows, width, frames = third_ref.shape

    @pl.when(tile == 0)
    def _():
        change[...] = (
            old_ref[...].astype(jnp.float32) - new_ref[...].astype(jnp.float32)
        ).astype(jnp.bfloat16)

    def product(slot):
        live, position = block_of(support_ref, owner_ref, tile, slot)
        start = pl.multiple_of(position * BLOCK, BLOCK)
        part = change[pl.ds(start, BLOCK), :]
        part = jnp.where(live, part, jnp.zeros_like(part))
        return jnp.dot(foot_ref[0, slot], part, preferred_element_type=jnp.float32)

    total = product(0)
    for slot in range(1, slots):
        total += product(slot)
    out_ref[...] = (third_ref[...].astype(jnp.float32) + total.reshape(rows, width, frames)).astype(
        jnp.bfloat16
    )


def final_residual(support, owner_map, old, new, foot, third):
    tiles, slots = foot.shape[:2]
    rows, cols, frames = third.shape
    return pl.pallas_call(
        final_kernel,
        grid=(tiles,),
        out_shape=jax.ShapeDtypeStruct(third.shape, jnp.bfloat16),
        in_specs=[
            whole(SMEM),
            whole(SMEM),
            whole(),
            whole(),
            pl.BlockSpec((1,) + foot.shape[1:], lambda t: (t, 0, 0, 0)),
            pl.BlockSpec((rows, TILE, frames), lambda t: (0, t, 0)),
        ],
        out_specs=pl.BlockSpec((rows, TILE, frames), lambda t: (0, t, 0)),
        scratch_shapes=[pltpu.VMEM(old.shape, jnp.bfloat16)],
        compiler_params=params(),
        name="final_residual",
    )(support, owner_map, old, new, foot, third)


def filter_kernel(taps_ref, norms_ref, old_ref, sums_ref, out_ref, stacked):
    owned, frames = old_ref.shape
    update = old_ref[...].astype(jnp.float32) + sums_ref[...] / (norms_ref[...] + RIDGE)
    half = LANES // 2
    edge = jnp.zeros((owned, half), jnp.float32)
    padded = jnp.concatenate([edge, update, edge], axis=1)
    parts = frames // LANES
    for i in range(parts):
        stacked[i * owned : (i + 1) * owned] = padded[:, i * LANES : (i + 2) * LANES]
    table = pltpu.roll(
        jnp.broadcast_to(taps_ref[...], (LANES, 2 * LANES)), 0, 1, stride=1, stride_axis=0
    )
    made = lax.dot_general(
        stacked[...],
        table,
        (((1,), (1,)), ((), ())),
        precision=lax.Precision.HIGHEST,
        preferred_element_type=jnp.float32,
    )
    for i in range(parts):
        out_ref[:, i * LANES : (i + 1) * LANES] = jnp.maximum(
            made[i * owned : (i + 1) * owned], 0.0
        ).astype(jnp.bfloat16)


def filter_traces(taps, norms, old, sums):
    owned, frames = old.shape
    reversed_taps = jnp.pad(taps[::-1], (0, 2 * LANES - taps.shape[0]))[None, :]
    return pl.pallas_call(
        filter_kernel,
        out_shape=jax.ShapeDtypeStruct(old.shape, jnp.bfloat16),
        in_specs=[whole()] * 4,
        out_specs=whole(),
        scratch_shapes=[pltpu.VMEM((owned * frames // LANES, 2 * LANES), jnp.float32)],
        compiler_params=params(),
        name="filter_traces",
    )(reversed_taps, norms, old, sums)


def to_tiles(owned):
    group_traces = lax.all_to_all(owned, "tm", split_axis=1, concat_axis=0, tiled=True)
    return lax.all_gather(group_traces, "tile", axis=0, tiled=True)


def halos(field):
    peers = lax.axis_size("tile")
    up = [(i, i + 1) for i in range(peers - 1)]
    down = [(i + 1, i) for i in range(peers - 1)]
    return lax.ppermute(field[-RAD:], "tile", up), lax.ppermute(field[:RAD], "tile", down)


def body(movie, footprints, support, cycle_offsets, cycle_weights, owner_map, traces_old, taps):
    tiles, slots = support.shape
    time_count = lax.axis_size("tm")
    tile_count = lax.axis_size("tile")
    owned, frames_all = traces_old.shape
    frames = movie.shape[2]
    cols = movie.shape[1]
    foot = footprints.reshape(tiles, slots, TILE * TILE, BLOCK)
    place = jnp.arange(cols, dtype=jnp.int32)[None, :] + cycle_offsets[:, 1:2]
    inside = (place >= 0) & (place < cols)
    weights = jnp.where(inside[:, None, :], cycle_weights, 0.0).transpose(1, 0, 2)

    old_full = to_tiles(traces_old)
    first = first_residual(support, owner_map, old_full, foot, movie)
    second = cycle_pass(cycle_offsets, weights, first, *halos(first))
    third_turned = cycle_pass(cycle_offsets, weights, second, *halos(second))
    third, sums, squares = project(support, owner_map, foot, third_turned)
    norms = jnp.sum(squares, axis=1).reshape(NBLK * BLOCK)
    mine = lax.psum_scatter(
        sums.reshape(NBLK * BLOCK, frames), "tile", scatter_dimension=0, tiled=True
    )
    mine_norms = lax.psum_scatter(norms, "tile", scatter_dimension=0, tiled=True)
    owned_sums = lax.all_to_all(mine, "tm", split_axis=0, concat_axis=1, tiled=True)
    owned_norms = lax.dynamic_slice_in_dim(mine_norms, lax.axis_index("tm") * owned, owned)
    fresh = filter_traces(taps, owned_norms[:, None], traces_old, owned_sums)
    residual = final_residual(support, owner_map, old_full, to_tiles(fresh), foot, third)
    return (residual, fresh)


def solution(mesh):
    return jax.shard_map(
        body,
        mesh=mesh,
        in_specs=(
            P("tile", None, "tm"),
            P("tile", None, None, None, None),
            P("tile", None),
            P(),
            P(None, "tile", None),
            P(),
            P(("tile", "tm"), None),
            P(),
        ),
        out_specs=(P("tile", None, "tm"), P(("tile", "tm"), None)),
        check_vma=False,
    )
```

time: 1710 us -> 270 us (0.16)
  local copies, waits for them, and re-layouts: 1270 us -> 14.8 us
  other arithmetic: 194 us -> 2.1 us
  between operations: 123 us -> 14.9 us
  Pallas kernels: 0 us -> 102 us
  waiting for transfers between devices: 13.2 us -> 38.2 us
    gather x8 -> x0, local copies, waits for them, and re-layouts: 1230 us -> none  [the longest x6 1230 us: band_tables(): taps[jnp.clip(tap_ids, 0, 2 * half_taps)]]
    convert_element_type x4 -> x0, other arithmetic: 174 us -> none  [the longest x2 171 us: clean_rows(): return (field_in.astype(jnp.float32) - backdrop).astype(jnp.bfloat16)]
    pallas_call x0 -> x6, Pallas kernels: none -> 102 us  [the longest x2 66 us: cycle_pass(): pl.pallas_call(cycle_kernel, out_shape=jax.ShapeDtypeStruct(field.shape,...]
    reduce_scatter x0 -> x1, waiting for transfers between devices: none -> 26.1 us  [body(): lax.psum_scatter(sums.reshape(NBLK * BLOCK, frames), 'tile', scatter_dime...]
    unnamed x0 -> x1, blocking collectives: none -> 24.1 us
    psum x1 -> x0, blocking collectives: 22.9 us -> none  [body(): total_norms = lax.psum(partial_norms, 'tile')]
  transfers between devices with their start and end apart: 7 -> 7, of which waited for: 3 -> 6; matrix products, arithmetic and copies ran while one was open for 74% -> 2% of each run, Pallas kernels for 0% -> 0%
where the time goes in v1:
time: 270 us; the launch traced here: 269 us
  Pallas kernels  102 us (38%)
  blocking collectives  71.9 us (27%)
  waiting for transfers between devices  38.2 us (14%)
  starting transfers between devices  24.7 us (9%)
  between operations  14.9 us (6%)
  local copies, waits for them, and re-layouts  14.8 us (5%)
    pallas_call x2, Pallas kernels, cycle_pass(): pl.pallas_call(cycle_kernel, out_shape=jax.ShapeDtypeStruct(field.shape,...  66 us
    all_gather x2, blocking collectives, to_tiles(): return lax.all_gather(group_traces, 'tile', axis=0, tiled=True)  34.9 us
    reduce_scatter x1, waiting for transfers between devices, body(): lax.psum_scatter(sums.reshape(NBLK * BLOCK, frames), 'tile', scatter_dime...  26.1 us
    unnamed x1, blocking collectives  24.1 us
    pallas_call x1, Pallas kernels, project(): pl.pallas_call(project_kernel, grid=(tiles // group,), out_shape=[jax.Sha...  14.9 us
    all_to_all x1, blocking collectives, to_tiles(): lax.all_to_all(owned, 'tm', split_axis=1, concat_axis=0, tiled=True)  12.9 us
    pallas_call x1, Pallas kernels, first_residual(): pl.pallas_call(first_kernel, grid=(tiles // group,), out_shape=jax.ShapeD...  12.2 us
    unnamed x25, local copies, waits for them, and re-layouts  11 us
  transfers between devices with their start and end apart: 7, of which 6 were waited for; matrix products, arithmetic and copies ran while one was open for 2% of the time, Pallas kernels for 0%

profile of v1, /device:TPU:1, one launch (start us, length us, event | category | flops | bytes accessed | tf_op | source)
XLA Modules:
  0.0 268.9 jit_solution(8919326095371342566)
XLA Ops:
  7.2 1.0 all_to_all.42
  8.2 0.8 reshape.47
  9.0 8.6 %all-to-all-start = ((bf16[16,2,1024]{2,1,0:T(2,128)(2,1)}), bf16[16,2,1024]{2,1,0:T(2,128)(2,1)S(1)}, u32[]{:S(2)}, u32[]{:S(2)}) async-start(bf16[16,2,1024]{2,1,0:T(2,128)(2,1)} %reshape.47), calls=%async_computation | async-start | bytes 131072 | tf_op jit(solution)/shard_map/all_to_all | solution.py:304
  17.6 0.7 slice_bitcast_fusion
  18.3 0.1 fusion.3
  18.4 0.8 copy.38.offsets_ref
  19.2 0.8 copy.43.support_ref
  19.9 2.0 copy.36.movie_ref
  22.0 2.1 all-to-all-done
  24.1 0.1 reshape.48
  24.2 16.2 %all_gather.6.traces_ref.old_ref = bf16[4096,64]{1,0:T(8,128)(2,1)S(1)} all-gather(bf16[512,64]{1,0:T(8,128)(2,1)S(1)} %bitcast.33), channel_id=1, replica_groups=mesh['tile'=8,'tm'=16] {'tile'}, dimensions={0}, use_global_device_ids=true | all-gather | bytes 589824 | tf_op jit(solution)/shard_map/all_gather | solution.py:305
  40.4 12.2 %first_residual.1.field_ref = bf16[32,64,256]{2,1,0:T(8,128)(2,1)S(1)} custom-call(s32[8,4]{1,0:T(8,128)S(1)} %copy.43.support_ref, s32[32]{0:T(128)S(1)} %copy-done.2, bf16[4096,64]{1,0:T(8,128)(2,1)S(1)} %all_gather.6.traces_ref.old_ref, bf16[8,4,1024,128]{3,2,1,0:T(8,128)(2,1)} %bitcast.29, bf16[32,256,64]{2,1,0:T(8,128)(2,1)S(1)} %copy.36.movie_ref), custom_call_target="tpu_custom_call" | custom-call | tf_op jit(solution)/shard_map/first_residual/pallas_call | solution.py:79
  52.7 2.9 %collective-permute-start = (bf16[8,64,256]{2,1,0:T(8,128)(2,1)S(1)}, bf16[8,64,256]{2,1,0:T(8,128)(2,1)S(1)}, u32[]{:S(2)}, u32[]{:S(2)}) collective-permute-start(bf16[8,64,256]{2,1,0:T(8,128)(2,1)S(1)} %get-tuple-element.17), channel_id=1, source_target_pairs={{0,16},{16,32},{32,48},{48,64},{64,80},{80,96},{96,112},{1,17},{17... | collective-permute-start | bytes 786440 | tf_op jit(solution)/shard_map/ppermute | solution.py:312
  55.7 1.9 collective-permute-start.1
  57.6 1.0 fusion.weights_ref
  58.6 0.3 collective-permute-done.top_ref
  59.0 4.4 %collective-permute-done.1.bottom_ref = bf16[8,64,256]{2,1,0:T(8,128)(2,1)S(1)} collective-permute-done((bf16[8,64,256]{2,1,0:T(8,128)(2,1)S(1)}, bf16[8,64,256]{2,1,0:T(8,128)(2,1)S(1)}, u32[]{:S(2)}, u32[]{:S(2)}) %collective-permute-start.1) | collective-permute-done | bytes 262176 | tf_op jit(solution)/shard_map/ppermute | solution.py:312
  63.4 33.0 %cycle_pass.2.field_ref = bf16[32,64,256]{2,1,0:T(8,128)(2,1)S(1)} custom-call(s32[48,2]{1,0:T(8,128)S(1)} %copy.38.offsets_ref, f32[32,48,256]{2,1,0:T(8,128)S(1)} %fusion.weights_ref, bf16[32,64,256]{2,1,0:T(8,128)(2,1)S(1)} %first_residual.1.field_ref, bf16[8,64,256]{2,1,0:T(8,128)(2,1)S(1)} %collective-permute-done.top_ref, ...), custom_call_target="tpu_custom_call" | custom-call | tf_op jit(solution)/shard_map/cycle_pass/pallas_call | solution.py:133
  96.4 1.9 collective-permute-start.2
  98.3 2.4 collective-permute-start.3
  100.8 0.9 collective-permute-done.2.top_ref
  101.6 4.4 %collective-permute-done.3.bottom_ref = bf16[8,64,256]{2,1,0:T(8,128)(2,1)S(1)} collective-permute-done((bf16[8,64,256]{2,1,0:T(8,128)(2,1)S(1)}, bf16[8,64,256]{2,1,0:T(8,128)(2,1)S(1)}, u32[]{:S(2)}, u32[]{:S(2)}) %collective-permute-start.3) | collective-permute-done | bytes 262176 | tf_op jit(solution)/shard_map/ppermute | solution.py:312
  106.0 33.0 %cycle_pass.3.field_ref = bf16[32,64,256]{2,1,0:T(8,128)(2,1)S(1)} custom-call(s32[48,2]{1,0:T(8,128)S(1)} %copy.38.offsets_ref, f32[32,48,256]{2,1,0:T(8,128)S(1)} %fusion.weights_ref, bf16[32,64,256]{2,1,0:T(8,128)(2,1)S(1)} %cycle_pass.2.field_ref, bf16[8,64,256]{2,1,0:T(8,128)(2,1)S(1)} %collective-permute-done.2.top_ref, ...), custom_call_target="tpu_custom_call" | custom-call | tf_op jit(solution)/shard_map/cycle_pass/pallas_call | solution.py:133
  139.0 14.9 %project.1 = (bf16[32,256,64]{2,1,0:T(8,128)(2,1)S(1)}, f32[32,128,64]{2,1,0:T(8,128)}, f32[32,8,128]{2,1,0:T(8,128)S(1)}) custom-call(s32[8,4]{1,0:T(8,128)S(1)} %copy.43.support_ref, s32[32]{0:T(128)S(1)} %copy-done.2, bf16[8,4,1024,128]{3,2,1,0:T(8,128)(2,1)} %bitcast.30, bf16[32,64,256]{2,1,0:T(8,128)(2,1)S(1)} %cycle_pass.3.field_ref), custom_call_target="tpu_custom_call" | custom-call | tf_op jit(solution)/shard_map/project/pallas_call | solution.py:192
  153.9 1.3 copy-done
  155.3 0.6 copy-done.5
  155.9 0.6 dynamic-slice
  157.2 0.1 reverse
  157.3 0.1 slice.25
  157.4 26.1 %reduce-scatter.2.cloned.1.call-done = f32[512,64]{1,0:T(8,128)} async-done(((f32[4096,64]{1,0:T(8,128)}), f32[512,64]{1,0:T(8,128)}) %reduce-scatter.2.cloned.1.call-update) | async-done | bytes 131088 | tf_op jit(solution)/shard_map/reduce_scatter | solution.py:333
  183.5 1.8 reshape.49
  185.3 6.9 %all-to-all-start.1 = ((f32[16,1,2048]{2,1,0:T(1,128)}), f32[16,1,2048]{2,1,0:T(1,128)S(1)}, u32[]{:S(2)}, u32[]{:S(2)}) async-start(f32[16,1,2048]{2,1,0:T(1,128)} %reshape.49), calls=%async_computation.2 | async-start | bytes 262144 | tf_op jit(solution)/shard_map/all_to_all | solution.py:337
  192.2 24.1 %all-reduce.1 = f32[4096]{0:T(1024)S(1)} all-reduce(f32[4096]{0:T(1024)S(1)} %bitcast.38), channel_id=2, replica_groups=mesh['tile'=8,'tm'=16] {'tile'}, use_global_device_ids=true, to_apply=%region_1.2.clone | all-reduce | flops 4096 | bytes 32768
  216.2 0.1 dynamic-slice_bitcast_fusion
  216.3 0.1 copy.41.norms_ref
  216.4 0.5 broadcast.19
  216.9 1.0 reduce
  217.9 0.1 reshape.50
  218.0 0.2 copy.40
  218.1 0.1 all_to_all.49.sums_ref
  218.3 1.1 filter_traces.1
  219.4 1.0 all_to_all.50
  220.4 0.1 reshape.51
  220.6 12.9 %all_to_all.57 = bf16[16,2,1024]{2,1,0:T(2,128)(2,1)S(1)} all-to-all(bf16[16,2,1024]{2,1,0:T(2,128)(2,1)S(1)} %reshape.51), channel_id=1, replica_groups=mesh['tile'=8,'tm'=16] {'tm'}, dimensions={0} | all-to-all | bytes 131072 | tf_op jit(solution)/shard_map/all_to_all | solution.py:304
  233.5 0.1 reshape.52
  233.7 18.7 %all_gather.7.new_ref = bf16[4096,64]{1,0:T(8,128)(2,1)S(1)} all-gather(bf16[512,64]{1,0:T(8,128)(2,1)S(1)} %bitcast.34), channel_id=1, replica_groups=mesh['tile'=8,'tm'=16] {'tile'}, dimensions={0}, use_global_device_ids=true | all-gather | bytes 589824 | tf_op jit(solution)/shard_map/all_gather | solution.py:305
  252.4 8.0 %final_residual.1 = bf16[32,256,64]{2,1,0:T(8,128)(2,1)S(1)} custom-call(s32[8,4]{1,0:T(8,128)S(1)} %copy.43.support_ref, s32[32]{0:T(128)S(1)} %copy-done.2, bf16[4096,64]{1,0:T(8,128)(2,1)S(1)} %all_gather.6.traces_ref.old_ref, bf16[4096,64]{1,0:T(8,128)(2,1)S(1)} %all_gather.7.new_ref, bf16[8,4,1024,128]{3,2,1,0:T(8,128)(2,1)} %bitcast.31, ...), custom_call_target="tpu_custom_call" | custom-call | tf_op jit(solution)/shard_map/final_residual/pallas_call | solution.py:245
  260.4 1.6 copy.44
  (19 shorter events, 0.3 us)
Async XLA Ops:
  9.0 15.1 %all-to-all-start = ((bf16[16,2,1024]{2,1,0:T(2,128)(2,1)}), bf16[16,2,1024]{2,1,0:T(2,128)(2,1)S(1)}, u32[]{:S(2)}, u32[]{:S(2)}) async-start(bf16[16,2,1024]{2,1,0:T(2,128)(2,1)} %reshape.47), calls=%async_computation | async-start | bytes 131072 | tf_op jit(solution)/shard_map/all_to_all | solution.py:304
  17.6 165.9 %reduce-scatter.2.cloned.1.call-start = ((), (), s32[]{:S(2)}) async-start(), calls=%async_computation.4 | async-start | bytes 2359296 | tf_op jit(solution)/shard_map/reduce_scatter | solution.py:333
  19.9 20.5 %copy-start.2 = (s32[32]{0:T(128)S(1)}, s32[32]{0:T(128)}, u32[]{:S(2)}) copy-start(s32[32]{0:T(128)} %owner_ref.5) | copy-start | bytes 388
  40.4 17.2 %copy-start.3 = (f32[48,32,256]{2,1,0:T(8,128)S(1)}, f32[48,32,256]{2,1,0:T(8,128)}, u32[]{:S(2)}) copy-start(f32[48,32,256]{2,1,0:T(8,128)} %param.12) | copy-start | bytes 4718596
  52.7 6.2 %collective-permute-start = (bf16[8,64,256]{2,1,0:T(8,128)(2,1)S(1)}, bf16[8,64,256]{2,1,0:T(8,128)(2,1)S(1)}, u32[]{:S(2)}, u32[]{:S(2)}) collective-permute-start(bf16[8,64,256]{2,1,0:T(8,128)(2,1)S(1)} %get-tuple-element.17), channel_id=1, source_target_pairs={{0,16},{16,32},{32,48},{48,64},{64,80},{80,96},{96,112},{1,17},{17... | collective-permute-start | bytes 786440 | tf_op jit(solution)/shard_map/ppermute | solution.py:312
  55.7 7.7 %collective-permute-start.1 = (bf16[8,64,256]{2,1,0:T(8,128)(2,1)S(1)}, bf16[8,64,256]{2,1,0:T(8,128)(2,1)S(1)}, u32[]{:S(2)}, u32[]{:S(2)}) collective-permute-start(bf16[8,64,256]{2,1,0:T(8,128)(2,1)S(1)} %get-tuple-element.16), channel_id=1, source_target_pairs={{16,0},{32,16},{48,32},{64,48},{80,64},{96,80},{112,96},{17,1},{33... | collective-permute-start | bytes 786440 | tf_op jit(solution)/shard_map/ppermute | solution.py:312
  96.4 5.2 %collective-permute-start.2 = (bf16[8,64,256]{2,1,0:T(8,128)(2,1)S(1)}, bf16[8,64,256]{2,1,0:T(8,128)(2,1)S(1)}, u32[]{:S(2)}, u32[]{:S(2)}) collective-permute-start(bf16[8,64,256]{2,1,0:T(8,128)(2,1)S(1)} %get-tuple-element.15), channel_id=1, source_target_pairs={{0,16},{16,32},{32,48},{48,64},{64,80},{80,96},{96,112},{1,17},{17... | collective-permute-start | bytes 786440 | tf_op jit(solution)/shard_map/ppermute | solution.py:312
  98.3 7.7 %collective-permute-start.3 = (bf16[8,64,256]{2,1,0:T(8,128)(2,1)S(1)}, bf16[8,64,256]{2,1,0:T(8,128)(2,1)S(1)}, u32[]{:S(2)}, u32[]{:S(2)}) collective-permute-start(bf16[8,64,256]{2,1,0:T(8,128)(2,1)S(1)} %get-tuple-element.14), channel_id=1, source_target_pairs={{16,0},{32,16},{48,32},{64,48},{80,64},{96,80},{112,96},{17,1},{33... | collective-permute-start | bytes 786440 | tf_op jit(solution)/shard_map/ppermute | solution.py:312
  153.9 1.3 copy-start
  155.3 0.7 copy-start.5
  155.3 1.9 copy-start.4
  155.3 63.0 %copy-start.1 = (bf16[32,1024]{1,0:T(8,128)(2,1)S(1)}, bf16[32,1024]{1,0:T(8,128)(2,1)}, u32[]{:S(2)}) copy-start(bf16[32,1024]{1,0:T(8,128)(2,1)} %old_ref.1) | copy-start | bytes 196612
  185.3 31.1 %all-to-all-start.1 = ((f32[16,1,2048]{2,1,0:T(1,128)}), f32[16,1,2048]{2,1,0:T(1,128)S(1)}, u32[]{:S(2)}, u32[]{:S(2)}) async-start(f32[16,1,2048]{2,1,0:T(1,128)} %reshape.49), calls=%async_computation.2 | async-start | bytes 262144 | tf_op jit(solution)/shard_map/all_to_all | solution.py:337
Sparse Core Ops, SparseCore 0:
  155.4 28.0 reduce-scatter.1

commit v2 on v1

--- a/solution.py
+++ b/solution.py
@@ -42,10 +42,10 @@
             live, position = block_of(support_ref, owner_ref, group * tiles + tile, slot)
 
             def add(slot=slot, position=position):
-                start = pl.multiple_of(position * BLOCK, BLOCK)
+                start = pl.multiple_of(position * (BLOCK // 2), BLOCK // 2)
                 part = jnp.dot(
                     foot_ref[tile, slot],
-                    traces_ref[pl.ds(start, BLOCK), :],
+                    unpack(traces_ref[pl.ds(start, BLOCK // 2), :]),
                     preferred_element_type=jnp.float32,
                 ).reshape(rows, TILE, frames)
                 if slot == 0:
@@ -141,7 +141,9 @@
     )(offsets, weights, field, top, bottom)
 
 
-def project_kernel(support_ref, owner_ref, foot_ref, field_ref, third_ref, sums_ref, norms_ref):
+def project_kernel(
+    support_ref, owner_ref, foot_ref, field_ref, third_ref, packed_ref, sums_ref, norms_ref
+):
     group = pl.program_id(0)
     tiles, slots, pixels, _ = foot_ref.shape
     rows, frames, width = field_ref.shape
@@ -184,18 +186,45 @@
 
     lax.fori_loop(0, tiles, one_tile, 0)
 
+    @pl.when(group == pl.num_programs(0) - 1)
+    def _():
+        each = packed_ref.shape[2] - PACK
+        per = each // (BLOCK // 2)
+        for core in range(packed_ref.shape[0]):
+
+            def one_chip(chip, carry, core=core):
+                base = (2 * chip + core) * per
+                for q in range(per):
+                    values = sums_ref[base + q]
+                    for k in range(BLOCK // (2 * PACK)):
+                        top = values[2 * k * PACK : (2 * k + 1) * PACK]
+                        bottom = values[(2 * k + 1) * PACK : (2 * k + 2) * PACK]
+                        packed_ref[
+                            core, chip, q * (BLOCK // 2) + k * PACK : q * (BLOCK // 2) + (k + 1) * PACK
+                        ] = jnp.concatenate([top, bottom], axis=1).astype(jnp.bfloat16)
+                lines = [jnp.sum(norms_ref[base + q], axis=0, keepdims=True) for q in range(per)]
+                fill = [jnp.zeros((PACK // 2 - per, BLOCK), jnp.float32)]
+                norms = jnp.concatenate(lines + fill, axis=0)
+                high = norms.astype(jnp.bfloat16).astype(jnp.float32)
+                packed_ref[core, chip, each : each + PACK] = jnp.concatenate(
+                    [high, norms - high], axis=0
+                ).astype(jnp.bfloat16)
+                return carry
+
+            lax.fori_loop(0, packed_ref.shape[1], one_chip, 0)
+
 
 def project(support, owner_map, foot, field):
     tiles, slots = foot.shape[:2]
     rows, frames, cols = field.shape
     group = LANES // TILE
+    packed = (2, lax.axis_size("tile") // 2, lax.axis_size("tm") * PACK + PACK, LANES)
     return pl.pallas_call(
         project_kernel,
         grid=(tiles // group,),
         out_shape=[
             jax.ShapeDtypeStruct((rows, cols, frames), jnp.bfloat16),
-            jax.ShapeDtypeStruct((NBLK, BLOCK, frames), jnp.float32),
-            jax.ShapeDtypeStruct((NBLK, 8, BLOCK), jnp.float32),
+            jax.ShapeDtypeStruct(packed, jnp.bfloat16),
         ],
         in_specs=[
             whole(SMEM),
@@ -205,8 +234,11 @@
         ],
         out_specs=[
             pl.BlockSpec((rows, LANES, frames), lambda g: (0, g, 0)),
-            pl.BlockSpec((NBLK, BLOCK, frames), lambda g: (0, 0, 0)),
-            pl.BlockSpec((NBLK, 8, BLOCK), lambda g: (0, 0, 0)),
+            pl.BlockSpec(packed, lambda g: (0, 0, 0, 0)),
+        ],
+        scratch_shapes=[
+            pltpu.VMEM((NBLK, BLOCK, frames), jnp.float32),
+            pltpu.VMEM((NBLK, 8, BLOCK), jnp.float32),
         ],
         compiler_params=params(),
         name="project",
@@ -226,8 +258,8 @@
 
     def product(slot):
         live, position = block_of(support_ref, owner_ref, tile, slot)
-        start = pl.multiple_of(position * BLOCK, BLOCK)
-        part = change[pl.ds(start, BLOCK), :]
+        start = pl.multiple_of(position * (BLOCK // 2), BLOCK // 2)
+        part = unpack(change[pl.ds(start, BLOCK // 2), :])
         part = jnp.where(live, part, jnp.zeros_like(part))
         return jnp.dot(foot_ref[0, slot], part, preferred_element_type=jnp.float32)
 
@@ -261,15 +293,237 @@
     )(support, owner_map, old, new, foot, third)
 
 
-def filter_kernel(taps_ref, norms_ref, old_ref, sums_ref, out_ref, stacked):
-    owned, frames = old_ref.shape
-    update = old_ref[...].astype(jnp.float32) + sums_ref[...] / (norms_ref[...] + RIDGE)
-    half = LANES // 2
-    edge = jnp.zeros((owned, half), jnp.float32)
-    padded = jnp.concatenate([edge, update, edge], axis=1)
-    parts = frames // LANES
-    for i in range(parts):
-        stacked[i * owned : (i + 1) * owned] = padded[:, i * LANES : (i + 2) * LANES]
+MESH = pl.DeviceIdType.MESH
+PACK = 16
+HALF_LANES = LANES // 2
+
+
+def low_lanes():
+    return lax.broadcasted_iota(jnp.int32, (PACK, LANES), 1) < HALF_LANES
+
+
+def join_low(left, right):
+    return jnp.where(low_lanes(), left, pltpu.roll(right, HALF_LANES, 1))
+
+
+def join_high(left, right):
+    return jnp.where(low_lanes(), pltpu.roll(left, HALF_LANES, 1), right)
+
+
+def chunks_of(top, bottom):
+    return join_low(top, bottom), join_high(top, bottom)
+
+
+def unpack(packed):
+    wide = packed.astype(jnp.float32)
+    turned = pltpu.roll(wide, HALF_LANES, 1)
+    parts = []
+    for k in range(packed.shape[0] // PACK):
+        rows = slice(k * PACK, (k + 1) * PACK)
+        parts += [wide[rows, :HALF_LANES], turned[rows, :HALF_LANES]]
+    return jnp.concatenate(parts, axis=0).astype(jnp.bfloat16)
+
+
+class Place:
+    def __init__(self, tiles, times):
+        self.chips, self.times = tiles // 2, times
+        self.tile, self.time = lax.axis_index("tile"), lax.axis_index("tm")
+        self.chip, self.core = self.tile // 2, lax.rem(self.tile, 2)
+        self.sibling = self.chip * 2 + 1 - self.core
+
+    def chip_at(self, step):
+        return lax.rem(self.chip + step + self.chips, self.chips)
+
+    def time_at(self, step):
+        return lax.rem(self.time + step + self.times, self.times)
+
+    def greet(self):
+        barrier = pltpu.get_barrier_semaphore()
+        peers = [(self.sibling, self.time)]
+        peers += [(self.chip_at(d) * 2 + self.core, self.time) for d in range(1, self.chips)]
+        peers += [(self.tile, self.time_at(d)) for d in range(1, self.times)]
+        for peer in peers:
+            pl.semaphore_signal(barrier, inc=1, device_id=peer, device_id_type=MESH)
+        pl.semaphore_wait(barrier, len(peers))
+
+
+def send(source, target, send_sem, recv_sem, device):
+    return pltpu.make_async_remote_copy(
+        src_ref=source,
+        dst_ref=target,
+        send_sem=send_sem,
+        recv_sem=recv_sem,
+        device_id=device,
+        device_id_type=MESH,
+    )
+
+
+def spread(place, chunks, full, sems):
+    (ts, tr), (xs, xr), (ss, sr) = sems
+    tile, time = place.tile, place.time
+
+    def rows(index):
+        return pl.ds(pl.multiple_of(index * PACK, PACK), PACK)
+
+    first = []
+    for d in range(1, place.times):
+        peer = place.time_at(d)
+        copy = send(
+            chunks.at[peer], full.at[tile, rows(time)], ts.at[d], tr.at[d], (tile, peer)
+        )
+        copy.start()
+        first.append(copy)
+    full[tile, rows(time)] = chunks[time]
+    for d, copy in enumerate(first, 1):
+        came = place.time_at(-d)
+        send(
+            chunks.at[time], full.at[tile, rows(came)], ts.at[d], tr.at[d], (tile, came)
+        ).wait_recv()
+    second = []
+    for d in range(1, place.chips):
+        copy = send(
+            full.at[tile],
+            full.at[tile],
+            xs.at[d],
+            xr.at[d],
+            (place.chip_at(d) * 2 + place.core, time),
+        )
+        copy.start()
+        second.append(copy)
+    third = []
+    for d in range(place.chips):
+        came = place.chip_at(-d) * 2 + place.core
+        if d:
+            send(full.at[came], full.at[came], xs.at[d], xr.at[d], (came, time)).wait_recv()
+        copy = send(
+            full.at[came], full.at[came], ss.at[d], sr.at[d], (place.sibling, time)
+        )
+        copy.start()
+        third.append(copy)
+    for d in range(place.chips):
+        came = place.chip_at(-d) * 2 + 1 - place.core
+        send(
+            full.at[came], full.at[came], ss.at[d], sr.at[d], (place.sibling, time)
+        ).wait_recv()
+    for copy in first + second + third:
+        copy.wait_send()
+
+
+def pair_sems(*counts):
+    return [pltpu.SemaphoreType.DMA((n,)) for n in counts for _ in range(2)]
+
+
+def pairs(sems):
+    return [(sems[2 * k], sems[2 * k + 1]) for k in range(len(sems) // 2)]
+
+
+def old_kernel(tiles, times, old_ref, full_ref, chunks, *sems):
+    place = Place(tiles, times)
+    for i in range(times // 2):
+        part = old_ref[:, i * LANES : (i + 1) * LANES].astype(jnp.float32)
+        even, odd = chunks_of(part[:PACK], part[PACK:])
+        chunks[2 * i] = even.astype(jnp.bfloat16)
+        chunks[2 * i + 1] = odd.astype(jnp.bfloat16)
+    place.greet()
+    spread(place, chunks, full_ref, pairs(sems))
+
+
+def remote_params(identity):
+    return pltpu.CompilerParams(
+        vmem_limit_bytes=48 * 2**20, collective_id=identity, has_side_effects=True
+    )
+
+
+def spread_old(traces_old):
+    tiles, times = lax.axis_size("tile"), lax.axis_size("tm")
+    return pl.pallas_call(
+        functools.partial(old_kernel, tiles, times),
+        out_shape=jax.ShapeDtypeStruct((tiles, times * PACK, LANES), jnp.bfloat16),
+        in_specs=[whole()],
+        out_specs=whole(),
+        scratch_shapes=[pltpu.VMEM((times, PACK, LANES), jnp.bfloat16)]
+        + pair_sems(times, tiles // 2, tiles // 2),
+        compiler_params=remote_params(0),
+        name="spread_old",
+    )(traces_old)
+
+
+def exchange_kernel(
+    tiles, times, taps_ref, old_ref, sums_ref, full_ref, fresh_ref,
+    pair_buf, x_send, x_buf, owner_send, owner_buf, stacked, chunks, *sems
+):
+    place = Place(tiles, times)
+    (ps, pr), (xs, xr), (ts, tr), *rest = pairs(sems)
+    chips, tile, time, core = place.chips, place.tile, place.time, place.core
+    rows = times * PACK
+    place.greet()
+    to_pair = []
+    for d in [*range(1, chips), 0]:
+        at = place.chip_at(d)
+        copy = send(
+            sums_ref.at[1 - core, at], pair_buf.at[at], ps.at[d], pr.at[d], (place.sibling, time)
+        )
+        copy.start()
+        to_pair.append((d, at, copy))
+    to_chip = []
+    mine = None
+    for d, at, copy in to_pair:
+        copy.wait_recv()
+        total = sums_ref[core, at].astype(jnp.float32) + pair_buf[at].astype(jnp.float32)
+        if d:
+            x_send[d] = total.astype(jnp.bfloat16)
+            out = send(x_send.at[d], x_buf.at[d], xs.at[d], xr.at[d], (at * 2 + core, time))
+            out.start()
+            to_chip.append(out)
+        else:
+            mine = total
+    for d, copy in enumerate(to_chip, 1):
+        copy.wait_recv()
+        mine += x_buf[d].astype(jnp.float32)
+    owner_send[...] = mine[:rows].reshape(times, PACK, LANES)
+    to_owner = []
+    for d in range(1, times):
+        peer = place.time_at(d)
+        copy = send(owner_send.at[peer], owner_buf.at[time], ts.at[d], tr.at[d], (tile, peer))
+        copy.start()
+        to_owner.append(copy)
+    owner_buf[time] = owner_send[time]
+
+    high = mine[rows : rows + PACK]
+    both = high + pltpu.roll(high, PACK - PACK // 2, 0)
+    block = lax.rem(time * 2 * PACK, BLOCK)
+    line = lax.broadcasted_iota(jnp.int32, (PACK, LANES), 0)
+    lane = lax.broadcasted_iota(jnp.int32, (PACK, LANES), 1)
+    row = jnp.sum(
+        jnp.where(line == time // (BLOCK // (2 * PACK)), both, 0.0), axis=0, keepdims=True
+    )
+    columns = [
+        jnp.sum(jnp.where(lane == line + block + k * PACK, row, 0.0), axis=1, keepdims=True)
+        for k in range(2)
+    ]
+    divisor = jnp.where(lane < HALF_LANES, columns[0], columns[1]) + RIDGE
+
+    for d in range(1, times):
+        came = place.time_at(-d)
+        send(
+            owner_send.at[came], owner_buf.at[came], ts.at[d], tr.at[d], (tile, came)
+        ).wait_recv()
+    update = [jnp.zeros((PACK, LANES), jnp.float32)]
+    for i in range(times // 2):
+        part = old_ref[:, i * LANES : (i + 1) * LANES].astype(jnp.float32)
+        for k, old in enumerate(chunks_of(part[:PACK], part[PACK:])):
+            update.append(old + owner_buf[2 * i + k] / divisor)
+    update.append(jnp.zeros((PACK, LANES), jnp.float32))
+    steps = times // 2
+    lines = [
+        (join_low(update[2 * i], update[2 * i + 1]), join_high(update[2 * i], update[2 * i + 1]))
+        for i in range(steps + 1)
+    ]
+    for i in range(steps):
+        for k in range(2):
+            at = slice((2 * i + k) * PACK, (2 * i + k + 1) * PACK)
+            stacked[at, :LANES] = lines[i][k]
+            stacked[at, LANES:] = lines[i + 1][k]
     table = pltpu.roll(
         jnp.broadcast_to(taps_ref[...], (LANES, 2 * LANES)), 0, 1, stride=1, stride_axis=0
     )
@@ -280,29 +534,45 @@
         precision=lax.Precision.HIGHEST,
         preferred_element_type=jnp.float32,
     )
-    for i in range(parts):
-        out_ref[:, i * LANES : (i + 1) * LANES] = jnp.maximum(
-            made[i * owned : (i + 1) * owned], 0.0
-        ).astype(jnp.bfloat16)
-
-
-def filter_traces(taps, norms, old, sums):
-    owned, frames = old.shape
+    made = jnp.maximum(made, 0.0)
+    for i in range(steps):
+        part = made[2 * i * PACK : (2 * i + 2) * PACK]
+        fresh_ref[:, i * LANES : (i + 1) * LANES] = part.astype(jnp.bfloat16)
+        even, odd = chunks_of(part[:PACK], part[PACK:])
+        chunks[2 * i] = even.astype(jnp.bfloat16)
+        chunks[2 * i + 1] = odd.astype(jnp.bfloat16)
+    spread(place, chunks, full_ref, rest)
+    for copy in [c for _, _, c in to_pair] + to_chip + to_owner:
+        copy.wait_send()
+
+
+def exchange(taps, traces_old, sums):
+    tiles, times = lax.axis_size("tile"), lax.axis_size("tm")
+    chips = tiles // 2
+    rows = times * PACK
+    group = (rows + PACK, LANES)
     reversed_taps = jnp.pad(taps[::-1], (0, 2 * LANES - taps.shape[0]))[None, :]
     return pl.pallas_call(
-        filter_kernel,
-        out_shape=jax.ShapeDtypeStruct(old.shape, jnp.bfloat16),
-        in_specs=[whole()] * 4,
-        out_specs=whole(),
-        scratch_shapes=[pltpu.VMEM((owned * frames // LANES, 2 * LANES), jnp.float32)],
-        compiler_params=params(),
-        name="filter_traces",
-    )(reversed_taps, norms, old, sums)
-
-
-def to_tiles(owned):
-    group_traces = lax.all_to_all(owned, "tm", split_axis=1, concat_axis=0, tiled=True)
-    return lax.all_gather(group_traces, "tile", axis=0, tiled=True)
+        functools.partial(exchange_kernel, tiles, times),
+        out_shape=[
+            jax.ShapeDtypeStruct((tiles, rows, LANES), jnp.bfloat16),
+            jax.ShapeDtypeStruct(traces_old.shape, jnp.bfloat16),
+        ],
+        in_specs=[whole()] * 3,
+        out_specs=[whole()] * 2,
+        scratch_shapes=[
+            pltpu.VMEM((chips,) + group, jnp.bfloat16),
+            pltpu.VMEM((chips,) + group, jnp.bfloat16),
+            pltpu.VMEM((chips,) + group, jnp.bfloat16),
+            pltpu.VMEM((times, PACK, LANES), jnp.float32),
+            pltpu.VMEM((times, PACK, LANES), jnp.float32),
+            pltpu.VMEM((times * PACK, 2 * LANES), jnp.float32),
+            pltpu.VMEM((times, PACK, LANES), jnp.bfloat16),
+        ]
+        + pair_sems(chips, chips, times, times, chips, chips),
+        compiler_params=remote_params(1),
+        name="exchange",
+    )(reversed_taps, traces_old, sums)
 
 
 def halos(field):
@@ -314,30 +584,21 @@
 
 def body(movie, footprints, support, cycle_offsets, cycle_weights, owner_map, traces_old, taps):
     tiles, slots = support.shape
-    time_count = lax.axis_size("tm")
-    tile_count = lax.axis_size("tile")
-    owned, frames_all = traces_old.shape
-    frames = movie.shape[2]
     cols = movie.shape[1]
     foot = footprints.reshape(tiles, slots, TILE * TILE, BLOCK)
     place = jnp.arange(cols, dtype=jnp.int32)[None, :] + cycle_offsets[:, 1:2]
     inside = (place >= 0) & (place < cols)
     weights = jnp.where(inside[:, None, :], cycle_weights, 0.0).transpose(1, 0, 2)
 
-    old_full = to_tiles(traces_old)
+    old_full = spread_old(traces_old).reshape(-1, LANES)
     first = first_residual(support, owner_map, old_full, foot, movie)
     second = cycle_pass(cycle_offsets, weights, first, *halos(first))
     third_turned = cycle_pass(cycle_offsets, weights, second, *halos(second))
-    third, sums, squares = project(support, owner_map, foot, third_turned)
-    norms = jnp.sum(squares, axis=1).reshape(NBLK * BLOCK)
-    mine = lax.psum_scatter(
-        sums.reshape(NBLK * BLOCK, frames), "tile", scatter_dimension=0, tiled=True
-    )
-    mine_norms = lax.psum_scatter(norms, "tile", scatter_dimension=0, tiled=True)
-    owned_sums = lax.all_to_all(mine, "tm", split_axis=0, concat_axis=1, tiled=True)
-    owned_norms = lax.dynamic_slice_in_dim(mine_norms, lax.axis_index("tm") * owned, owned)
-    fresh = filter_traces(taps, owned_norms[:, None], traces_old, owned_sums)
-    residual = final_residual(support, owner_map, old_full, to_tiles(fresh), foot, third)
+    third, sums = project(support, owner_map, foot, third_turned)
+    new_full, fresh = exchange(taps, traces_old, sums)
+    residual = final_residual(
+        support, owner_map, old_full, new_full.reshape(-1, LANES), foot, third
+    )
     return (residual, fresh)
 
 

time: 270 us -> 179 us (0.66)
  blocking collectives: 71.9 us -> 0 us
  Pallas kernels: 102 us -> 150 us
  waiting for transfers between devices: 38.2 us -> 3.97 us
  between operations: 14.9 us -> 0.84 us
  starting transfers between devices: 24.7 us -> 11.8 us
  local copies, waits for them, and re-layouts: 14.8 us -> 9.63 us
    pallas_call x1 -> x2, Pallas kernels: 1.12 us -> 47.7 us  [the longest x1 28.1 us: exchange(): pl.pallas_call(functools.partial(exchange_kernel, tiles, times), out_shap...]
    all_gather x2 -> x0, blocking collectives: 34.9 us -> none  [to_tiles(): return lax.all_gather(group_traces, 'tile', axis=0, tiled=True)]
    reduce_scatter x1 -> x0, waiting for transfers between devices: 26.1 us -> none  [body(): lax.psum_scatter(sums.reshape(NBLK * BLOCK, frames), 'tile', scatter_dime...]
    unnamed x1 -> x0, blocking collectives: 24.1 us -> none
    all_to_all x2 -> x0, starting transfers between devices: 15.5 us -> none  [the longest x1 8.6 us: to_tiles(): lax.all_to_all(owned, 'tm', split_axis=1, concat_axis=0, tiled=True)]
    all_to_all x1 -> x0, blocking collectives: 12.9 us -> none  [to_tiles(): lax.all_to_all(owned, 'tm', split_axis=1, concat_axis=0, tiled=True)]
    ppermute x2, waiting for transfers between devices: 8.79 us -> 2.14 us  [halos(): lax.ppermute(field[:RAD], 'tile', down)]
    ppermute x2, starting transfers between devices: 4.86 us -> 7.88 us  [halos(): lax.ppermute(field[-RAD:], 'tile', up)]
  transfers between devices with their start and end apart: 7 -> 4, of which waited for: 6 -> 3; matrix products, arithmetic and copies ran while one was open for 2% -> 2% of each run, Pallas kernels for 0% -> 0%
where the time goes in v2:
time: 179 us
  Pallas kernels  150 us (84%)
  starting transfers between devices  11.8 us (7%)
  local copies, waits for them, and re-layouts  9.63 us (5%)
  waiting for transfers between devices  3.97 us (2%)
  other arithmetic  2.59 us (1%)
    pallas_call x2, Pallas kernels, cycle_pass(): pl.pallas_call(cycle_kernel, out_shape=jax.ShapeDtypeStruct(field.shape,...  66.3 us
    pallas_call x1, Pallas kernels, exchange(): pl.pallas_call(functools.partial(exchange_kernel, tiles, times), out_shap...  28.1 us
    pallas_call x1, Pallas kernels, spread_old(): pl.pallas_call(functools.partial(old_kernel, tiles, times), out_shape=jax...  19.6 us
    pallas_call x1, Pallas kernels, project(): pl.pallas_call(project_kernel, grid=(tiles // group,), out_shape=[jax.Sha...  14.3 us
    pallas_call x1, Pallas kernels, first_residual(): pl.pallas_call(first_kernel, grid=(tiles // group,), out_shape=jax.ShapeD...  13.5 us
    unnamed x25, local copies, waits for them, and re-layouts  8.77 us
    pallas_call x1, Pallas kernels, final_residual(): pl.pallas_call(final_kernel, grid=(tiles,), out_shape=jax.ShapeDtypeStruc...  7.98 us
    ppermute x2, starting transfers between devices, halos(): lax.ppermute(field[-RAD:], 'tile', up)  7.88 us
  transfers between devices with their start and end apart: 4, of which 3 were waited for; matrix products, arithmetic and copies ran while one was open for 2% of the time, Pallas kernels for 0%

profile of v2, /device:TPU:1, one launch (start us, length us, event | category | flops | bytes accessed | tf_op | source)
XLA Modules:
  0.0 178.7 jit_solution(6485575100643896344)
XLA Ops:
  0.6 0.8 copy.16.support_ref
  1.4 0.0 copy-start.4
  1.4 0.8 copy-done.4
  2.2 19.6 %spread_old.1 = bf16[8,256,128]{2,1,0:T(8,128)(2,1)S(1)} custom-call(bf16[32,1024]{1,0:T(8,128)(2,1)S(1)} %copy-done.4), custom_call_target="tpu_custom_call" | custom-call | tf_op jit(solution)/shard_map/spread_old/pallas_call | solution.py:439
  21.9 0.0 copy-start.6
  21.9 2.0 %copy.12.movie_ref = bf16[32,256,64]{2,1,0:T(8,128)(2,1)S(1)} copy(bf16[32,256,64]{1,2,0:T(8,128)(2,1)} %param.8) | data formatting | bytes 2097152 | tf_op args[0]
  23.9 0.0 copy-done.6
  23.9 0.0 copy-start.7
  23.9 13.5 %first_residual.1.field_ref = bf16[32,64,256]{2,1,0:T(8,128)(2,1)S(1)} custom-call(s32[8,4]{1,0:T(8,128)S(1)} %copy.16.support_ref, s32[32]{0:T(128)S(1)} %copy-done.6, bf16[2048,128]{1,0:T(8,128)(2,1)S(1)} %bitcast.9, bf16[8,4,1024,128]{3,2,1,0:T(8,128)(2,1)} %bitcast.13, bf16[32,256,64]{2,1,0:T(8,128)(2,1)S(1)} %copy.12.movie_ref), custom_call_target="tpu_custom_call" | custom-call | tf_op jit(solution)/shard_map/first_residual/pallas_call | solution.py:79
  37.5 0.0 copy-start
  37.5 1.0 copy-done
  38.5 2.1 %collective-permute-start.1 = (bf16[8,64,256]{2,1,0:T(8,128)(2,1)S(1)}, bf16[8,64,256]{2,1,0:T(8,128)(2,1)S(1)}, u32[]{:S(2)}, u32[]{:S(2)}) collective-permute-start(bf16[8,64,256]{2,1,0:T(8,128)(2,1)S(1)} %get-tuple-element.14), channel_id=1, source_target_pairs={{16,0},{32,16},{48,32},{64,48},{80,64},{96,80},{112,96},{17,1},{33... | collective-permute-start | bytes 786440 | tf_op jit(solution)/shard_map/ppermute | solution.py:582
  40.5 3.5 %collective-permute-start = (bf16[8,64,256]{2,1,0:T(8,128)(2,1)S(1)}, bf16[8,64,256]{2,1,0:T(8,128)(2,1)S(1)}, u32[]{:S(2)}, u32[]{:S(2)}) collective-permute-start(bf16[8,64,256]{2,1,0:T(8,128)(2,1)S(1)} %get-tuple-element.15), channel_id=1, source_target_pairs={{0,16},{16,32},{32,48},{48,64},{64,80},{80,96},{96,112},{1,17},{17... | collective-permute-start | bytes 786440 | tf_op jit(solution)/shard_map/ppermute | solution.py:582
  44.0 0.0 copy-done.7
  44.1 0.1 copy.14.offsets_ref
  44.1 0.1 fusion.3
  44.2 0.0 copy-start.1
  44.2 0.0 copy-start.8
  44.3 2.5 %fusion.weights_ref = f32[32,48,256]{2,1,0:T(8,128)S(1)} fusion(f32[48,32,256]{2,1,0:T(8,128)} %param.12, pred[48,256]{1,0:T(8,128)(4,1)S(1)} %fusion.3), kind=kLoop, calls=%fused_computation.1 | loop fusion | flops 393216 | bytes 3158016 | tf_op jit(solution)/shard_map/transpose | solution.py:591
  46.8 0.0 collective-permute-done.1.bottom_ref
  46.8 0.5 collective-permute-done.top_ref
  47.3 0.0 copy-start.2
  47.3 0.7 copy-done.2
  48.0 0.0 copy-done.1
  48.0 0.0 copy-start.3
  48.0 0.9 copy-done.3
  49.0 33.1 %cycle_pass.2.field_ref = bf16[32,64,256]{2,1,0:T(8,128)(2,1)S(1)} custom-call(s32[48,2]{1,0:T(8,128)S(1)} %copy.14.offsets_ref, f32[32,48,256]{2,1,0:T(8,128)S(1)} %fusion.weights_ref, bf16[32,64,256]{2,1,0:T(8,128)(2,1)S(1)} %copy-done.1, bf16[8,64,256]{2,1,0:T(8,128)(2,1)S(1)} %copy-done.3, bf16[8,64,256]{2,1,0:T(8,128)(2,1)S(1)} %collective-permute-done.1.bottom_ref), custom_call_target="tpu_custom_call" | custom-call | tf_op jit(solution)/shard_map/cycle_pass/pallas_call | solution.py:133
  82.1 0.8 fusion.4
  82.9 1.9 %collective-permute-start.3 = (bf16[8,64,256]{2,1,0:T(8,128)(2,1)}, bf16[8,64,256]{2,1,0:T(8,128)(2,1)S(1)}, u32[]{:S(2)}, u32[]{:S(2)}) collective-permute-start(bf16[8,64,256]{2,1,0:T(8,128)(2,1)} %get-tuple-element.12), channel_id=1, source_target_pairs={{16,0},{32,16},{48,32},{64,48},{80,64},{96,80},{112,96},{17,1},{33... | collective-permute-start | bytes 786440 | tf_op jit(solution)/shard_map/ppermute | solution.py:582
  84.9 4.4 %collective-permute-start.2 = (bf16[8,64,256]{2,1,0:T(8,128)(2,1)}, bf16[8,64,256]{2,1,0:T(8,128)(2,1)}, u32[]{:S(2)}, u32[]{:S(2)}) collective-permute-start(bf16[8,64,256]{2,1,0:T(8,128)(2,1)} %get-tuple-element.13), channel_id=1, source_target_pairs={{0,16},{16,32},{32,48},{48,64},{64,80},{80,96},{96,112},{1,17},{17... | collective-permute-start | bytes 786440 | tf_op jit(solution)/shard_map/ppermute | solution.py:582
  89.3 0.0 copy-done.8
  89.3 0.1 reverse
  89.4 0.1 slice.25
  89.4 2.1 %collective-permute-done.3.bottom_ref = bf16[8,64,256]{2,1,0:T(8,128)(2,1)S(1)} collective-permute-done((bf16[8,64,256]{2,1,0:T(8,128)(2,1)}, bf16[8,64,256]{2,1,0:T(8,128)(2,1)S(1)}, u32[]{:S(2)}, u32[]{:S(2)}) %collective-permute-start.3) | collective-permute-done | bytes 262176 | tf_op jit(solution)/shard_map/ppermute | solution.py:582
  91.6 1.3 collective-permute-done.2.top_ref
  92.9 33.2 %cycle_pass.3.field_ref = bf16[32,64,256]{2,1,0:T(8,128)(2,1)S(1)} custom-call(s32[48,2]{1,0:T(8,128)S(1)} %copy.14.offsets_ref, f32[32,48,256]{2,1,0:T(8,128)S(1)} %fusion.weights_ref, bf16[32,64,256]{2,1,0:T(8,128)(2,1)S(1)} %cycle_pass.2.field_ref, bf16[8,64,256]{2,1,0:T(8,128)(2,1)} %collective-permute-done.2.top_ref, ...), custom_call_target="tpu_custom_call" | custom-call | tf_op jit(solution)/shard_map/cycle_pass/pallas_call | solution.py:133
  126.0 0.0 copy-start.5
  126.0 14.3 %project.1 = (bf16[32,256,64]{2,1,0:T(8,128)(2,1)S(1)}, bf16[2,4,272,128]{3,2,1,0:T(8,128)(2,1)S(1)}) custom-call(s32[8,4]{1,0:T(8,128)S(1)} %copy.16.support_ref, s32[32]{0:T(128)S(1)} %copy-done.6, bf16[8,4,1024,128]{3,2,1,0:T(8,128)(2,1)} %bitcast.14, bf16[32,64,256]{2,1,0:T(8,128)(2,1)S(1)} %cycle_pass.3.field_ref), custom_call_target="tpu_custom_call" | custom-call | tf_op jit(solution)/shard_map/project/pallas_call | solution.py:222
  140.4 0.0 copy-done.5
  140.4 28.1 %exchange.1 = (bf16[8,256,128]{2,1,0:T(8,128)(2,1)S(1)}, bf16[32,1024]{1,0:T(8,128)(2,1)S(1)}) custom-call(f32[1,256]{1,0:T(1,128)S(1)} %bitcast.12, bf16[32,1024]{1,0:T(8,128)(2,1)S(1)} %copy-done.5, bf16[2,4,272,128]{3,2,1,0:T(8,128)(2,1)S(1)} %get-tuple-element.6.sums_ref), custom_call_target="tpu_custom_call" | custom-call | tf_op jit(solution)/shard_map/exchange/pallas_call | solution.py:555
  168.5 8.0 %final_residual.1 = bf16[32,256,64]{2,1,0:T(8,128)(2,1)S(1)} custom-call(s32[8,4]{1,0:T(8,128)S(1)} %copy.16.support_ref, s32[32]{0:T(128)S(1)} %copy-done.6, bf16[2048,128]{1,0:T(8,128)(2,1)S(1)} %bitcast.10, bf16[2048,128]{1,0:T(8,128)(2,1)S(1)} %bitcast.11, bf16[8,4,1024,128]{3,2,1,0:T(8,128)(2,1)} %bitcast.15, ...), custom_call_target="tpu_custom_call" | custom-call | tf_op jit(solution)/shard_map/final_residual/pallas_call | solution.py:277
  176.5 1.6 copy.17
  178.1 0.6 copy.22
  (3 shorter events, 0.0 us)
Async XLA Ops:
  1.4 0.8 copy-start.4
  21.9 2.1 %copy-start.6 = (s32[32]{0:T(128)S(1)}, s32[32]{0:T(128)}, u32[]{:S(2)}) copy-start(s32[32]{0:T(128)} %owner_ref.5) | copy-start | bytes 388
  23.9 20.1 %copy-start.7 = (s32[48,2]{0,1:T(2,128)S(1)}, s32[48,2]{0,1:T(2,128)}, u32[]{:S(2)}) copy-start(s32[48,2]{0,1:T(2,128)} %param.11) | copy-start | bytes 1156
  37.5 1.0 copy-start
  38.5 8.3 %collective-permute-start.1 = (bf16[8,64,256]{2,1,0:T(8,128)(2,1)S(1)}, bf16[8,64,256]{2,1,0:T(8,128)(2,1)S(1)}, u32[]{:S(2)}, u32[]{:S(2)}) collective-permute-start(bf16[8,64,256]{2,1,0:T(8,128)(2,1)S(1)} %get-tuple-element.14), channel_id=1, source_target_pairs={{16,0},{32,16},{48,32},{64,48},{80,64},{96,80},{112,96},{17,1},{33... | collective-permute-start | bytes 786440 | tf_op jit(solution)/shard_map/ppermute | solution.py:582
  40.5 6.8 %collective-permute-start = (bf16[8,64,256]{2,1,0:T(8,128)(2,1)S(1)}, bf16[8,64,256]{2,1,0:T(8,128)(2,1)S(1)}, u32[]{:S(2)}, u32[]{:S(2)}) collective-permute-start(bf16[8,64,256]{2,1,0:T(8,128)(2,1)S(1)} %get-tuple-element.15), channel_id=1, source_target_pairs={{0,16},{16,32},{32,48},{48,64},{64,80},{80,96},{96,112},{1,17},{17... | collective-permute-start | bytes 786440 | tf_op jit(solution)/shard_map/ppermute | solution.py:582
  44.2 3.8 %copy-start.1 = (bf16[32,64,256]{2,1,0:T(8,128)(2,1)S(1)}, bf16[32,64,256]{2,1,0:T(8,128)(2,1)}, u32[]{:S(2)}) copy-start(bf16[32,64,256]{2,1,0:T(8,128)(2,1)} %copy-done) | copy-start | bytes 3145732
  44.2 45.0 %copy-start.8 = (f32[129]{0:T(256)S(1)}, f32[129]{0:T(256)}, u32[]{:S(2)}) copy-start(f32[129]{0:T(256)} %param.15) | copy-start | bytes 1552
  47.3 0.7 copy-start.2
  48.0 1.0 copy-start.3
  82.9 8.6 %collective-permute-start.3 = (bf16[8,64,256]{2,1,0:T(8,128)(2,1)}, bf16[8,64,256]{2,1,0:T(8,128)(2,1)S(1)}, u32[]{:S(2)}, u32[]{:S(2)}) collective-permute-start(bf16[8,64,256]{2,1,0:T(8,128)(2,1)} %get-tuple-element.12), channel_id=1, source_target_pairs={{16,0},{32,16},{48,32},{64,48},{80,64},{96,80},{112,96},{17,1},{33... | collective-permute-start | bytes 786440 | tf_op jit(solution)/shard_map/ppermute | solution.py:582
  84.9 8.0 %collective-permute-start.2 = (bf16[8,64,256]{2,1,0:T(8,128)(2,1)}, bf16[8,64,256]{2,1,0:T(8,128)(2,1)}, u32[]{:S(2)}, u32[]{:S(2)}) collective-permute-start(bf16[8,64,256]{2,1,0:T(8,128)(2,1)} %get-tuple-element.13), channel_id=1, source_target_pairs={{0,16},{16,32},{32,48},{48,64},{64,80},{80,96},{96,112},{1,17},{17... | collective-permute-start | bytes 786440 | tf_op jit(solution)/shard_map/ppermute | solution.py:582
  126.0 14.4 %copy-start.5 = (bf16[32,1024]{1,0:T(8,128)(2,1)S(1)}, bf16[32,1024]{1,0:T(8,128)(2,1)}, u32[]{:S(2)}) copy-start(bf16[32,1024]{1,0:T(8,128)(2,1)} %old_ref.3) | copy-start | bytes 196612

commit v3 on v2

v3 whole, which is shorter than its diff:
```python
import functools

import jax
import jax.numpy as jnp
from jax import lax
from jax.experimental import pallas as pl
from jax.experimental.pallas import tpu as pltpu
from jax.sharding import PartitionSpec as P

TILE = 32
BLOCK = 128
NBLK = 32
RAD = 8
RIDGE = 1.0
GROUP = 4
LANES = 128

SMEM = pltpu.MemorySpace.SMEM


def whole(space=pltpu.MemorySpace.VMEM):
    return pl.BlockSpec(memory_space=space)


def params(limit):
    return pltpu.CompilerParams(vmem_limit_bytes=limit * 2**20)


def block_of(support_ref, owner_ref, tile, slot):
    held = support_ref[slot, tile]
    return held >= 0, owner_ref[jnp.maximum(held, 0)]


def image_kernel(sign, both, support_ref, owner_ref, *refs):
    traces_refs, (foot_ref, field_ref, out_ref, image) = refs[: 1 + both], refs[1 + both :]
    tiles, slots = foot_ref.shape[0], foot_ref.shape[1]
    rows, frames, cols = field_ref.shape
    group = LANES // TILE

    def block(tile, slot):
        live, position = block_of(support_ref, owner_ref, tile, slot)
        at = pl.ds(pl.multiple_of(position * (BLOCK // 2), BLOCK // 2), BLOCK // 2)
        if both:
            old, new = [ref[at, :].astype(jnp.float32) for ref in traces_refs]
            part = unpack(old - new)
        else:
            part = unpack(traces_refs[0][at, :])
        return jnp.where(live, part, jnp.zeros_like(part))

    def pair(tile, slot):
        return jnp.dot(
            jnp.concatenate([foot_ref[tile, slot], foot_ref[tile, slot + 1]], axis=1),
            jnp.concatenate([block(tile, slot), block(tile, slot + 1)], axis=0),
            preferred_element_type=jnp.float32,
        ).reshape(rows, TILE, frames)

    for strip in range(cols // LANES):
        lanes = slice(strip * LANES, (strip + 1) * LANES)

        def one_tile(inner, carry, strip=strip):
            tile = strip * group + inner
            columns = pl.ds(pl.multiple_of(inner * TILE, TILE), TILE)
            image[:, columns, :] = pair(tile, 0)
            for slot in range(2, slots, 2):

                @pl.when(support_ref[slot, tile] >= 0)
                def _(slot=slot):
                    image[:, columns, :] += pair(tile, slot)

            return carry

        lax.fori_loop(0, group, one_tile, 0)

        def some_rows(step, carry, lanes=lanes):
            for u in range(0, 2 * GROUP, 2):
                row = step * 2 * GROUP + u
                turned = jnp.concatenate([image[row], image[row + 1]], axis=1).T
                for k in range(2):
                    part = turned[k * frames : (k + 1) * frames]
                    out_ref[row + k, :, lanes] = (
                        field_ref[row + k, :, lanes].astype(jnp.float32) + sign * part
                    ).astype(jnp.bfloat16)
            return carry

        lax.fori_loop(0, rows // (2 * GROUP), some_rows, 0)


def add_image(sign, support, owner_map, traces, foot, field, name):
    rows, frames, cols = field.shape
    return pl.pallas_call(
        functools.partial(image_kernel, sign, len(traces) - 1),
        out_shape=jax.ShapeDtypeStruct(field.shape, jnp.bfloat16),
        in_specs=[whole(SMEM), whole(SMEM)] + [whole() for _ in range(len(traces) + 2)],
        out_specs=whole(),
        scratch_shapes=[pltpu.VMEM((rows, LANES, frames), jnp.float32)],
        compiler_params=params(20),
        name=name,
    )(support, owner_map, *traces, foot, field)


def project_kernel(
    support_ref, owner_ref, foot_ref, field_ref, packed_ref, view, sums_ref, norms_ref
):
    tiles, slots, pixels, _ = foot_ref.shape
    rows, frames, cols = field_ref.shape
    group = LANES // TILE
    sums_ref[...] = jnp.zeros_like(sums_ref)
    norms_ref[...] = jnp.zeros_like(norms_ref)
    lane = lax.broadcasted_iota(jnp.int32, (frames, LANES), 1)

    def add(tile, slot):
        both = jnp.dot(
            view[lax.rem(tile, group)],
            jnp.concatenate([foot_ref[tile, slot], foot_ref[tile, slot + 1]], axis=1),
            preferred_element_type=jnp.float32,
        )
        for k in range(2):
            live, position = block_of(support_ref, owner_ref, tile, slot + k)
            part = both[:, k * BLOCK : (k + 1) * BLOCK]
            sums_ref[position] += jnp.where(live, part, 0.0)
            wide = foot_ref[tile, slot + k].astype(jnp.float32)
            square = jnp.sum((wide * wide).reshape(pixels // 8, 8, BLOCK), axis=0)
            norms_ref[position] += jnp.where(live, square, 0.0)

    for strip in range(cols // LANES):
        lanes = slice(strip * LANES, (strip + 1) * LANES)

        def some_rows(step, carry, lanes=lanes):
            source = [
                field_ref[step * group + k, :, lanes].astype(jnp.float32) for k in range(group)
            ]
            at = pl.ds(pl.multiple_of(step * LANES, LANES), LANES)
            for t in range(group):
                line = None
                for k in range(group):
                    shift = (k - t) * TILE % LANES
                    moved = pltpu.roll(source[k], shift, 1) if shift else source[k]
                    line = moved if k == 0 else jnp.where(lane >= k * TILE, moved, line)
                view[t, :, at] = line.astype(jnp.bfloat16)
            return carry

        lax.fori_loop(0, rows // group, some_rows, 0)

        def one_tile(inner, carry, strip=strip):
            tile = strip * group + inner
            add(tile, 0)
            for slot in range(2, slots, 2):

                @pl.when(support_ref[slot, tile] >= 0)
                def _(slot=slot):
                    add(tile, slot)

            return carry

        lax.fori_loop(0, group, one_tile, 0)

    each = packed_ref.shape[2] - PACK
    per = each // (BLOCK // 2)
    for core in range(packed_ref.shape[0]):

        def one_chip(chip, carry, core=core):
            base = (2 * chip + core) * per
            for q in range(per):
                values = sums_ref[base + q].T
                for k in range(BLOCK // (2 * PACK)):
                    top = values[2 * k * PACK : (2 * k + 1) * PACK]
                    bottom = values[(2 * k + 1) * PACK : (2 * k + 2) * PACK]
                    at = q * (BLOCK // 2) + k * PACK
                    packed_ref[core, chip, at : at + PACK] = jnp.concatenate(
                        [top, bottom], axis=1
                    ).astype(jnp.bfloat16)
            lines = [jnp.sum(norms_ref[base + q], axis=0, keepdims=True) for q in range(per)]
            fill = [jnp.zeros((PACK // 2 - per, BLOCK), jnp.float32)]
            norms = jnp.concatenate(lines + fill, axis=0)
            high = norms.astype(jnp.bfloat16).astype(jnp.float32)
            packed_ref[core, chip, each : each + PACK] = jnp.concatenate(
                [high, norms - high], axis=0
            ).astype(jnp.bfloat16)
            return carry

        lax.fori_loop(0, packed_ref.shape[1], one_chip, 0)


def project(support, owner_map, foot, field, chips, times):
    rows, frames, cols = field.shape
    return pl.pallas_call(
        project_kernel,
        out_shape=jax.ShapeDtypeStruct((2, chips, times * PACK + PACK, LANES), jnp.bfloat16),
        in_specs=[whole(SMEM), whole(SMEM), whole(), whole()],
        out_specs=whole(),
        scratch_shapes=[
            pltpu.VMEM((LANES // TILE, frames, TILE * TILE), jnp.bfloat16),
            pltpu.VMEM((NBLK, frames, BLOCK), jnp.float32),
            pltpu.VMEM((NBLK, 8, BLOCK), jnp.float32),
        ],
        compiler_params=params(20),
        name="project",
    )(support, owner_map, foot, field)


MESH = pl.DeviceIdType.MESH
PACK = 16
HALF_LANES = LANES // 2


def low_lanes():
    return lax.broadcasted_iota(jnp.int32, (PACK, LANES), 1) < HALF_LANES


def join_low(left, right):
    return jnp.where(low_lanes(), left, pltpu.roll(right, HALF_LANES, 1))


def join_high(left, right):
    return jnp.where(low_lanes(), pltpu.roll(left, HALF_LANES, 1), right)


def chunks_of(top, bottom):
    return join_low(top, bottom), join_high(top, bottom)


def unpack(packed):
    wide = packed.astype(jnp.float32)
    turned = pltpu.roll(wide, HALF_LANES, 1)
    parts = []
    for k in range(packed.shape[0] // PACK):
        rows = slice(k * PACK, (k + 1) * PACK)
        parts += [wide[rows, :HALF_LANES], turned[rows, :HALF_LANES]]
    return jnp.concatenate(parts, axis=0).astype(jnp.bfloat16)


class Place:
    def __init__(self, tiles, times):
        self.chips, self.times = tiles // 2, times
        self.tile, self.time = lax.axis_index("tile"), lax.axis_index("tm")
        self.chip, self.core = self.tile // 2, lax.rem(self.tile, 2)
        self.sibling = self.chip * 2 + 1 - self.core

    def chip_at(self, step):
        return lax.rem(self.chip + step + self.chips, self.chips)

    def time_at(self, step):
        return lax.rem(self.time + step + self.times, self.times)

    def greet(self):
        barrier = pltpu.get_barrier_semaphore()
        peers = [(self.sibling, self.time)]
        peers += [(self.chip_at(d) * 2 + self.core, self.time) for d in range(1, self.chips)]
        peers += [(self.tile, self.time_at(d)) for d in range(1, self.times)]
        for peer in peers:
            pl.semaphore_signal(barrier, inc=1, device_id=peer, device_id_type=MESH)
        pl.semaphore_wait(barrier, len(peers))


def send(source, target, send_sem, recv_sem, device):
    return pltpu.make_async_remote_copy(
        src_ref=source,
        dst_ref=target,
        send_sem=send_sem,
        recv_sem=recv_sem,
        device_id=device,
        device_id_type=MESH,
    )


def spread(place, chunks, full, sems, meanwhile=None):
    (ts, tr), (xs, xr), (ss, sr) = sems
    tile, time = place.tile, place.time

    def rows(index):
        return pl.ds(pl.multiple_of(index * PACK, PACK), PACK)

    first = []
    for d in range(1, place.times):
        peer = place.time_at(d)
        copy = send(
            chunks.at[peer], full.at[tile, rows(time)], ts.at[d], tr.at[d], (tile, peer)
        )
        copy.start()
        first.append(copy)
    full[tile, rows(time)] = chunks[time]
    if meanwhile:
        meanwhile()
    for d, copy in enumerate(first, 1):
        came = place.time_at(-d)
        send(
            chunks.at[time], full.at[tile, rows(came)], ts.at[d], tr.at[d], (tile, came)
        ).wait_recv()
    second = []
    for d in range(1, place.chips):
        copy = send(
            full.at[tile],
            full.at[tile],
            xs.at[d],
            xr.at[d],
            (place.chip_at(d) * 2 + place.core, time),
        )
        copy.start()
        second.append(copy)
    third = []
    for d in range(place.chips):
        came = place.chip_at(-d) * 2 + place.core
        if d:
            send(full.at[came], full.at[came], xs.at[d], xr.at[d], (came, time)).wait_recv()
        copy = send(
            full.at[came], full.at[came], ss.at[d], sr.at[d], (place.sibling, time)
        )
        copy.start()
        third.append(copy)
    for d in range(place.chips):
        came = place.chip_at(-d) * 2 + 1 - place.core
        send(
            full.at[came], full.at[came], ss.at[d], sr.at[d], (place.sibling, time)
        ).wait_recv()
    for copy in first + second + third:
        copy.wait_send()


def pair_sems(*counts):
    return [pltpu.SemaphoreType.DMA((n,)) for n in counts for _ in range(2)]


def pairs(sems):
    return [(sems[2 * k], sems[2 * k + 1]) for k in range(len(sems) // 2)]


def old_kernel(
    tiles, times, offsets_ref, weights_ref, old_ref, full_ref, sorted_ref, chunks, *sems
):
    place = Place(tiles, times)
    for i in range(times // 2):
        part = old_ref[:, i * LANES : (i + 1) * LANES].astype(jnp.float32)
        even, odd = chunks_of(part[:PACK], part[PACK:])
        chunks[2 * i] = even.astype(jnp.bfloat16)
        chunks[2 * i + 1] = odd.astype(jnp.bfloat16)
    place.greet()
    spread(
        place,
        chunks,
        full_ref,
        pairs(sems),
        lambda: sort_weights(offsets_ref, weights_ref, sorted_ref),
    )


def remote_params(identity, limit):
    return pltpu.CompilerParams(
        vmem_limit_bytes=limit * 2**20, collective_id=identity, has_side_effects=True
    )


def spread_old(traces_old, offsets, weights):
    tiles, times = lax.axis_size("tile"), lax.axis_size("tm")
    count, rows, cols = weights.shape
    return pl.pallas_call(
        functools.partial(old_kernel, tiles, times),
        out_shape=[
            jax.ShapeDtypeStruct((tiles, times * PACK, LANES), jnp.bfloat16),
            jax.ShapeDtypeStruct((count * PLANES, rows, cols // PLANES), jnp.float32),
        ],
        in_specs=[whole(SMEM), whole(), whole()],
        out_specs=[whole()] * 2,
        scratch_shapes=[pltpu.VMEM((times, PACK, LANES), jnp.bfloat16)]
        + pair_sems(times, tiles // 2, tiles // 2),
        compiler_params=remote_params(0, 12),
        name="spread_old",
    )(offsets, weights, traces_old)


def exchange_kernel(
    tiles, times, taps_ref, old_ref, sums_ref, full_ref, fresh_ref,
    pair_buf, x_send, x_buf, owner_send, owner_buf, stacked, spare, band, chunks, *sems
):
    place = Place(tiles, times)
    (ps, pr), (xs, xr), (ts, tr), *rest = pairs(sems)
    chips, tile, time, core = place.chips, place.tile, place.time, place.core
    rows = times * PACK
    place.greet()
    to_pair = []
    for d in [*range(1, chips), 0]:
        at = place.chip_at(d)
        copy = send(
            sums_ref.at[1 - core, at], pair_buf.at[at], ps.at[d], pr.at[d], (place.sibling, time)
        )
        copy.start()
        to_pair.append((d, at, copy))
    to_chip = []
    mine = None
    for d, at, copy in to_pair:
        copy.wait_recv()
        total = sums_ref[core, at].astype(jnp.float32) + pair_buf[at].astype(jnp.float32)
        if d:
            x_send[d] = total.astype(jnp.bfloat16)
            out = send(x_send.at[d], x_buf.at[d], xs.at[d], xr.at[d], (at * 2 + core, time))
            out.start()
            to_chip.append(out)
        else:
            mine = total
    for d, copy in enumerate(to_chip, 1):
        copy.wait_recv()
        mine += x_buf[d].astype(jnp.float32)
    owner_send[...] = mine[:rows].reshape(times, PACK, LANES)
    to_owner = []
    for d in range(1, times):
        peer = place.time_at(d)
        copy = send(owner_send.at[peer], owner_buf.at[time], ts.at[d], tr.at[d], (tile, peer))
        copy.start()
        to_owner.append(copy)
    owner_buf[time] = owner_send[time]

    spare[...] = jnp.zeros_like(spare)
    spare[0:1, 0 : taps_ref.shape[1]] = taps_ref[...]
    wide = jnp.broadcast_to(spare[0:1, :], (2 * LANES, 2 * LANES))
    band[...] = pltpu.roll(wide, LANES, 1, stride=1, stride_axis=0)[:, :LANES]

    high = mine[rows : rows + PACK]
    both = high + pltpu.roll(high, PACK - PACK // 2, 0)
    block = lax.rem(time * 2 * PACK, BLOCK)
    line = lax.broadcasted_iota(jnp.int32, (PACK, LANES), 0)
    lane = lax.broadcasted_iota(jnp.int32, (PACK, LANES), 1)
    row = jnp.sum(
        jnp.where(line == time // (BLOCK // (2 * PACK)), both, 0.0), axis=0, keepdims=True
    )
    columns = [
        jnp.sum(jnp.where(lane == line + block + k * PACK, row, 0.0), axis=1, keepdims=True)
        for k in range(2)
    ]
    divisor = jnp.where(lane < HALF_LANES, columns[0], columns[1]) + RIDGE

    for d in range(1, times):
        came = place.time_at(-d)
        send(
            owner_send.at[came], owner_buf.at[came], ts.at[d], tr.at[d], (tile, came)
        ).wait_recv()
    update = [jnp.zeros((PACK, LANES), jnp.float32)]
    for i in range(times // 2):
        part = old_ref[:, i * LANES : (i + 1) * LANES].astype(jnp.float32)
        for k, old in enumerate(chunks_of(part[:PACK], part[PACK:])):
            update.append(old + owner_buf[2 * i + k] / divisor)
    update.append(jnp.zeros((PACK, LANES), jnp.float32))
    steps = times // 2
    lines = [
        (join_low(update[2 * i], update[2 * i + 1]), join_high(update[2 * i], update[2 * i + 1]))
        for i in range(steps + 1)
    ]
    for i in range(steps):
        for k in range(2):
            at = slice((2 * i + k) * PACK, (2 * i + k + 1) * PACK)
            stacked[at, :LANES] = lines[i][k]
            stacked[at, LANES:] = lines[i + 1][k]
    made = jnp.dot(
        stacked[...],
        band[...],
        precision=lax.Precision.HIGHEST,
        preferred_element_type=jnp.float32,
    )
    made = jnp.maximum(made, 0.0)
    for i in range(steps):
        part = made[2 * i * PACK : (2 * i + 2) * PACK]
        fresh_ref[:, i * LANES : (i + 1) * LANES] = part.astype(jnp.bfloat16)
        even, odd = chunks_of(part[:PACK], part[PACK:])
        chunks[2 * i] = even.astype(jnp.bfloat16)
        chunks[2 * i + 1] = odd.astype(jnp.bfloat16)
    spread(place, chunks, full_ref, rest)
    for copy in [c for _, _, c in to_pair] + to_chip + to_owner:
        copy.wait_send()


def exchange(taps, traces_old, sums):
    tiles, times = lax.axis_size("tile"), lax.axis_size("tm")
    chips = tiles // 2
    rows = times * PACK
    group = (rows + PACK, LANES)
    return pl.pallas_call(
        functools.partial(exchange_kernel, tiles, times),
        out_shape=[
            jax.ShapeDtypeStruct((tiles, rows, LANES), jnp.bfloat16),
            jax.ShapeDtypeStruct(traces_old.shape, jnp.bfloat16),
        ],
        in_specs=[whole()] * 3,
        out_specs=[whole()] * 2,
        scratch_shapes=[
            pltpu.VMEM((chips,) + group, jnp.bfloat16),
            pltpu.VMEM((chips,) + group, jnp.bfloat16),
            pltpu.VMEM((chips,) + group, jnp.bfloat16),
            pltpu.VMEM((times, PACK, LANES), jnp.float32),
            pltpu.VMEM((times, PACK, LANES), jnp.float32),
            pltpu.VMEM((times * PACK, 2 * LANES), jnp.float32),
            pltpu.VMEM((8, 2 * LANES), jnp.float32),
            pltpu.VMEM((2 * LANES, LANES), jnp.float32),
            pltpu.VMEM((times, PACK, LANES), jnp.bfloat16),
        ]
        + pair_sems(chips, chips, times, times, chips, chips),
        compiler_params=remote_params(1, 12),
        name="exchange",
    )(taps[None, :], traces_old, sums)


PLANES = 2
REACH = RAD // PLANES
ROLLS = 2 * REACH + 1


def sorting(cols, back=False):
    column = lax.broadcasted_iota(jnp.int32, (cols, cols), int(back))
    place = lax.broadcasted_iota(jnp.int32, (cols, cols), 1 - int(back))
    half = cols // PLANES
    hit = column == PLANES * lax.rem(place, half) + place // half
    return hit.astype(jnp.float32).astype(jnp.bfloat16)


def sort_weights(offsets_ref, weights_ref, sorted_ref, each=8):
    count, rows, cols = weights_ref.shape
    sort = sorting(cols)
    column = lax.broadcasted_iota(jnp.int32, (rows, cols), 1)

    def some(step, carry):
        parts = []
        for u in range(each):
            j = step * each + u
            place = column + offsets_ref[1, j]
            parts.append(jnp.where((place >= 0) & (place < cols), weights_ref[j], 0.0))
        left = jnp.concatenate(parts, axis=0)
        total = jnp.zeros((each * rows, cols), jnp.float32)
        for _ in range(3):
            piece = left.astype(jnp.bfloat16)
            total += jnp.dot(piece, sort, preferred_element_type=jnp.float32)
            left = left - piece.astype(jnp.float32)
        for u in range(each):
            for p in range(PLANES):
                sorted_ref[(step * each + u) * PLANES + p] = total[
                    u * rows : (u + 1) * rows, p * LANES : (p + 1) * LANES
                ]
        return carry

    lax.fori_loop(0, count // each, some, 0)


def clean_kernel(
    tiles, offsets_ref, weights_ref, first_ref, third_ref, copies, field, halo, table, sends, recvs
):
    rows, frames, cols = first_ref.shape
    count = offsets_ref.shape[1]
    half = frames // 2
    padded = rows + 2 * RAD
    tile, time = lax.axis_index("tile"), lax.axis_index("tm")
    below, above = lax.rem(tile + 1, tiles), lax.rem(tile + tiles - 1, tiles)
    barrier = pltpu.get_barrier_semaphore()
    for peer in (below, above):
        pl.semaphore_signal(barrier, inc=1, device_id=(peer, time), device_id_type=MESH)

    sort = sorting(cols)

    def sort_rows(base):
        wide = jnp.dot(
            first_ref[pl.ds(base, RAD)].reshape(RAD * frames, cols),
            sort,
            preferred_element_type=jnp.float32,
        ).reshape(RAD, frames, cols)
        for p in range(PLANES):
            plane = wide[:, :, p * LANES : (p + 1) * LANES]
            field[0, pl.ds(base, RAD), p] = jnp.concatenate(
                [plane[:, :half], plane[:, half:]], axis=2
            ).astype(jnp.bfloat16)

    def halo_copies(turn):
        return [
            send(
                field.at[turn, pl.ds(start, RAD)],
                halo.at[turn, side],
                sends.at[turn, side],
                recvs.at[turn, side],
                (peer, time),
            )
            for side, start, peer in ((0, rows - RAD, below), (1, 0, above))
        ]

    def roll_row(values, row):
        for p in range(PLANES):
            wide = values[p]
            low, high = wide[:, :LANES], wide[:, LANES:]
            for s in range(ROLLS):
                shift = (REACH - s) % LANES
                at = (s * padded + row) * PLANES + p
                copies[at, :, :LANES] = pltpu.roll(low, shift, 1) if shift else low
                copies[at, :, LANES:] = pltpu.roll(high, shift, 1) if shift else high

    def roll_own(turn):
        def some(step, carry):
            for u in range(GROUP):
                row = step * GROUP + u
                roll_row(field[turn, row].astype(jnp.float32), RAD + row)
            return carry

        lax.fori_loop(0, rows // GROUP, some, 0)

    def roll_halo(turn):
        for side, edge, base in ((0, tile == 0, 0), (1, tile == tiles - 1, RAD + rows)):

            def some(step, carry, side=side, edge=edge, base=base):
                for u in range(GROUP):
                    row = step * GROUP + u
                    values = halo[turn, side, row].astype(jnp.float32)
                    roll_row(jnp.where(edge, 0.0, values), base + row)
                return carry

            lax.fori_loop(0, RAD // GROUP, some, 0)

    def run_rows(turn, edges):
        def one_row(step, carry):
            row = step + RAD
            if edges:
                row = jnp.where(step < RAD, step, step + rows - 2 * RAD)
            for p in range(PLANES):
                low = jnp.zeros((half, LANES), jnp.float32)
                high = jnp.zeros((half, LANES), jnp.float32)
                for j in range(count):
                    k = j * PLANES + p
                    source = copies[table[k] + row * PLANES]
                    weight = weights_ref[k, pl.ds(row, 1), :]
                    low += weight * source[:, :LANES]
                    high += weight * source[:, LANES:]
                mine = copies[(REACH * padded + RAD + row) * PLANES + p]
                out = mine - jnp.concatenate([low, high], axis=1)
                field[1 - turn, row, p] = out.astype(jnp.bfloat16)
            return carry

        lax.fori_loop(0, 2 * RAD if edges else rows - 2 * RAD, one_row, 0)

    sort_rows(0)
    sort_rows(rows - RAD)
    pl.semaphore_wait(barrier, 2)
    for turn in range(2):
        moving = halo_copies(turn)
        for copy in moving:
            copy.start()
        if turn == 0:
            for base in range(RAD, rows - RAD, RAD):
                sort_rows(base)
            for j in range(count):
                for p in range(PLANES):
                    q = p + offsets_ref[1, j] + RAD
                    table[j * PLANES + p] = (
                        (q >> 1) * padded + RAD + offsets_ref[0, j]
                    ) * PLANES + (q & 1)
        roll_own(turn)
        run_rows(turn, False)
        for copy in moving:
            copy.wait()
        roll_halo(turn)
        run_rows(turn, True)

    unsort = sorting(cols, back=True)
    for base in range(0, rows, RAD):
        planes = []
        for p in range(PLANES):
            wide = field[0, base : base + RAD, p].astype(jnp.float32)
            planes.append(jnp.concatenate([wide[:, :, :LANES], wide[:, :, LANES:]], axis=1))
        flat = jnp.concatenate(planes, axis=2).reshape(RAD * frames, cols)
        back = jnp.dot(flat.astype(jnp.bfloat16), unsort, preferred_element_type=jnp.float32)
        third_ref[base : base + RAD] = back.astype(jnp.bfloat16).reshape(RAD, frames, cols)


def clean(offsets, weights, first):
    rows, frames, cols = first.shape
    row = (PLANES, frames // 2, cols)
    padded = rows + 2 * RAD
    return pl.pallas_call(
        functools.partial(clean_kernel, lax.axis_size("tile")),
        out_shape=jax.ShapeDtypeStruct(first.shape, jnp.bfloat16),
        in_specs=[whole(SMEM), whole(), whole()],
        out_specs=whole(),
        scratch_shapes=[
            pltpu.VMEM((ROLLS * padded * PLANES,) + row[1:], jnp.float32),
            pltpu.VMEM((2, rows) + row, jnp.bfloat16),
            pltpu.VMEM((2, 2, RAD) + row, jnp.bfloat16),
            pltpu.SMEM((PLANES * offsets.shape[1],), jnp.int32),
            pltpu.SemaphoreType.DMA((2, 2)),
            pltpu.SemaphoreType.DMA((2, 2)),
        ],
        compiler_params=remote_params(2, 40),
        name="clean",
    )(offsets, weights, first)


def body(movie, footprints, support, cycle_offsets, cycle_weights, owner_map, traces_old, taps):
    tiles, slots = support.shape
    chips, times = lax.axis_size("tile") // 2, lax.axis_size("tm")
    foot = footprints.reshape(tiles, slots, TILE * TILE, BLOCK)
    field = movie.transpose(0, 2, 1)
    blocks, offsets = support.T, cycle_offsets.T
    old_full, weights = spread_old(traces_old, offsets, cycle_weights)
    old_full = old_full.reshape(-1, LANES)
    first = add_image(-1.0, blocks, owner_map, [old_full], foot, field, "first_residual")
    third = clean(offsets, weights, first)
    sums = project(blocks, owner_map, foot, third, chips, times)
    new_full, fresh = exchange(taps, traces_old, sums)
    new_full = new_full.reshape(-1, LANES)
    residual = add_image(
        1.0, blocks, owner_map, [old_full, new_full], foot, third, "final_residual"
    )
    return (residual.transpose(0, 2, 1), fresh)


def solution(mesh):
    return jax.shard_map(
        body,
        mesh=mesh,
        in_specs=(
            P("tile", None, "tm"),
            P("tile", None, None, None, None),
            P("tile", None),
            P(),
            P(None, "tile", None),
            P(),
            P(("tile", "tm"), None),
            P(),
        ),
        out_specs=(P("tile", None, "tm"), P(("tile", "tm"), None)),
        check_vma=False,
    )
```

time: 179 us -> 108 us (0.60)
  Pallas kernels: 150 us -> 100 us
  starting transfers between devices: 11.8 us -> 0 us
  waiting for transfers between devices: 3.97 us -> 0 us
  local copies, waits for them, and re-layouts: 9.63 us -> 6.97 us
  other arithmetic: 2.59 us -> 0 us
    pallas_call x6 -> x5, Pallas kernels: 122 us -> 72.3 us  [the longest x1 30.9 us: clean(): pl.pallas_call(functools.partial(clean_kernel, lax.axis_size('tile')), ou...]
    ppermute x4 -> x0, starting transfers between devices: 11.8 us -> none  [the longest x2 7.88 us: halos(): lax.ppermute(field[-RAD:], 'tile', up)]
    ppermute x4 -> x0, waiting for transfers between devices: 3.97 us -> none  [the longest x2 2.14 us: halos(): lax.ppermute(field[:RAD], 'tile', down)]
    transpose x1 -> x0, other arithmetic: 2.51 us -> none  [body(): jnp.where(inside[:, None, :], cycle_weights, 0.0).transpose(1, 0, 2)]
    unnamed x25 -> x23, local copies, waits for them, and re-layouts: 8.77 us -> 6.97 us
  transfers between devices with their start and end apart: 4 -> 0, of which waited for: 3 -> 0; matrix products, arithmetic and copies ran while one was open for 2% -> 0% of each run, Pallas kernels for 0% -> 0%
where the time goes in v3:
time: 108 us
  Pallas kernels  100 us (93%)
  local copies, waits for them, and re-layouts  6.97 us (6%)
    pallas_call x1, Pallas kernels, clean(): pl.pallas_call(functools.partial(clean_kernel, lax.axis_size('tile')), ou...  30.9 us
    pallas_call x1, Pallas kernels, exchange(): pl.pallas_call(functools.partial(exchange_kernel, tiles, times), out_shap...  28.2 us
    pallas_call x1, Pallas kernels, spread_old(): pl.pallas_call(functools.partial(old_kernel, tiles, times), out_shape=[ja...  20.2 us
    pallas_call x2, Pallas kernels, add_image(): pl.pallas_call(functools.partial(image_kernel, sign, len(traces) - 1), ou...  13.9 us
    pallas_call x1, Pallas kernels, project(): pl.pallas_call(project_kernel, out_shape=jax.ShapeDtypeStruct((2, chips,...  7.34 us
    unnamed x23, local copies, waits for them, and re-layouts  6.97 us

profile of v3, /device:TPU:1, one launch (start us, length us, event | category | flops | bytes accessed | tf_op | source)
XLA Modules:
  0.0 108.2 jit_solution(15918326776694438169)
XLA Ops:
  0.6 0.0 copy-start.7
  0.6 0.0 copy-start.6
  0.7 0.0 copy-start.2
  0.7 1.4 %copy-done.2 = f32[48,32,256]{2,1,0:T(8,128)S(1)} copy-done((f32[48,32,256]{2,1,0:T(8,128)S(1)}, f32[48,32,256]{2,1,0:T(8,128)}, u32[]{:S(2)}) %copy-start.2) | copy-done | bytes 1572888
  2.1 0.0 copy-start.4
  2.1 0.8 copy-done.4
  2.9 0.0 copy-start.8
  2.9 0.7 copy-done.8
  3.6 0.0 copy-start.3
  3.6 20.2 %spread_old.1 = (bf16[8,256,128]{2,1,0:T(8,128)(2,1)S(1)}, f32[96,32,128]{2,1,0:T(8,128)S(1)}) custom-call(s32[2,48]{1,0:T(2,128)S(1)} %bitcast.18, f32[48,32,256]{2,1,0:T(8,128)S(1)} %copy-done.2, bf16[32,1024]{1,0:T(8,128)(2,1)S(1)} %copy-done.4), custom_call_target="tpu_custom_call" | custom-call | tf_op jit(solution)/shard_map/spread_old/pallas_call | solution.py:355
  23.8 0.0 copy-done.7
  23.8 0.0 copy-done.6
  23.8 0.0 copy-done.3
  23.8 0.0 copy-start
  23.8 3.4 %copy-done = bf16[8,4,32,32,128]{4,3,2,1,0:T(8,128)(2,1)S(1)} copy-done((bf16[8,4,32,32,128]{4,3,2,1,0:T(8,128)(2,1)S(1)}, bf16[8,4,32,32,128]{4,3,2,1,0:T(8,128)(2,1)}, u32[]{:S(2)}) %copy-start) | copy-done | bytes 8388632
  27.2 0.0 copy-start.9
  27.2 0.0 copy-start.1
  27.2 6.4 %first_residual.1.first_ref = bf16[32,64,256]{2,1,0:T(8,128)(2,1)S(1)} custom-call(s32[4,8]{1,0:T(4,128)S(1)} %bitcast.15, s32[32]{0:T(128)S(1)} %copy-done.7, bf16[2048,128]{1,0:T(8,128)(2,1)S(1)} %bitcast.11, bf16[8,4,1024,128]{3,2,1,0:T(8,128)(2,1)S(1)} %bitcast.8, bf16[32,64,256]{2,1,0:T(8,128)(2,1)S(1)} %bitcast.13), custom_call_target="tpu_custom_call" | custom-call | tf_op jit(solution)/shard_map/first_residual/pallas_call | solution.py:90
  33.6 0.0 copy-done.9
  33.6 30.9 %clean.1.field_ref.refs_3_ = bf16[32,64,256]{2,1,0:T(8,128)(2,1)S(1)} custom-call(s32[2,48]{1,0:T(2,128)S(1)} %bitcast.19, f32[96,32,128]{2,1,0:T(8,128)S(1)} %get-tuple-element.7.weights_ref, bf16[32,64,256]{2,1,0:T(8,128)(2,1)S(1)} %first_residual.1.first_ref), custom_call_target="tpu_custom_call" | custom-call | tf_op jit(solution)/shard_map/clean/pallas_call | solution.py:668
  64.5 0.0 copy-done.1
  64.6 0.0 copy-start.5
  64.6 0.0 copy-start.10
  64.6 7.3 %project.1.sums_ref = bf16[2,4,272,128]{3,2,1,0:T(8,128)(2,1)S(1)} custom-call(s32[4,8]{1,0:T(4,128)S(1)} %bitcast.16, s32[32]{0:T(128)S(1)} %copy-done.7, bf16[8,4,1024,128]{3,2,1,0:T(8,128)(2,1)S(1)} %bitcast.9, bf16[32,64,256]{2,1,0:T(8,128)(2,1)S(1)} %clean.1.field_ref.refs_3_), custom_call_target="tpu_custom_call" | custom-call | tf_op jit(solution)/shard_map/project/pallas_call | solution.py:186
  71.9 0.0 copy-done.5
  71.9 0.0 copy-done.10
  72.0 28.2 %exchange.1 = (bf16[8,256,128]{2,1,0:T(8,128)(2,1)S(1)}, bf16[32,1024]{1,0:T(8,128)(2,1)S(1)}) custom-call(f32[1,129]{1,0:T(1,128)S(1)} %bitcast.20, bf16[32,1024]{1,0:T(8,128)(2,1)S(1)} %copy-done.5, bf16[2,4,272,128]{3,2,1,0:T(8,128)(2,1)S(1)} %project.1.sums_ref), custom_call_target="tpu_custom_call" | custom-call | tf_op jit(solution)/shard_map/exchange/pallas_call | solution.py:474
  100.2 7.4 %final_residual.1 = bf16[32,64,256]{2,1,0:T(8,128)(2,1)} custom-call(s32[4,8]{1,0:T(4,128)S(1)} %bitcast.17, s32[32]{0:T(128)S(1)} %copy-done.7, bf16[2048,128]{1,0:T(8,128)(2,1)S(1)} %bitcast.12, bf16[2048,128]{1,0:T(8,128)(2,1)S(1)} %bitcast.14, bf16[8,4,1024,128]{3,2,1,0:T(8,128)(2,1)S(1)} %bitcast.10, bf16[32,64,256]{2,1,0:T(8,128)(2,1)S(1)} %clean.1.field_ref.refs_3_), custom_call_target="tpu_custom_call" | custom-call | tf_op jit(solution)/shard_map/final_residual/pallas_call | solution.py:90
  107.6 0.6 copy.11
Async XLA Ops:
  0.6 23.1 %copy-start.7 = (s32[32]{0:T(128)S(1)}, s32[32]{0:T(128)}, u32[]{:S(2)}) copy-start(s32[32]{0:T(128)} %owner_ref.5) | copy-start | bytes 388
  0.6 23.1 %copy-start.6 = (s32[8,4]{0,1:T(4,128)S(1)}, s32[8,4]{0,1:T(4,128)}, u32[]{:S(2)}) copy-start(s32[8,4]{0,1:T(4,128)} %param.10) | copy-start | bytes 388
  0.7 1.4 %copy-start.2 = (f32[48,32,256]{2,1,0:T(8,128)S(1)}, f32[48,32,256]{2,1,0:T(8,128)}, u32[]{:S(2)}) copy-start(f32[48,32,256]{2,1,0:T(8,128)} %weights_ref.1) | copy-start | bytes 4718596
  2.1 0.8 copy-start.4
  2.9 0.7 copy-start.8
  3.6 20.2 %copy-start.3 = (bf16[32,256,64]{1,2,0:T(8,128)(2,1)S(1)}, bf16[32,256,64]{1,2,0:T(8,128)(2,1)}, u32[]{:S(2)}) copy-start(bf16[32,256,64]{1,2,0:T(8,128)(2,1)} %param.8) | copy-start | bytes 3145732
  23.8 3.4 %copy-start = (bf16[8,4,32,32,128]{4,3,2,1,0:T(8,128)(2,1)S(1)}, bf16[8,4,32,32,128]{4,3,2,1,0:T(8,128)(2,1)}, u32[]{:S(2)}) copy-start(bf16[8,4,32,32,128]{4,3,2,1,0:T(8,128)(2,1)} %param.9) | copy-start | bytes 25165828
  27.2 6.5 %copy-start.9 = (s32[48,2]{0,1:T(2,128)S(1)}, s32[48,2]{0,1:T(2,128)}, u32[]{:S(2)}) copy-start(s32[48,2]{0,1:T(2,128)} %param.11) | copy-start | bytes 1156
  27.2 37.4 %copy-start.1 = (bf16[8,4,32,32,128]{4,3,2,1,0:T(8,128)(2,1)S(1)}, bf16[8,4,32,32,128]{4,3,2,1,0:T(8,128)(2,1)}, u32[]{:S(2)}) copy-start(bf16[8,4,32,32,128]{4,3,2,1,0:T(8,128)(2,1)} %param.9) | copy-start | bytes 25165828
  64.6 7.4 %copy-start.5 = (bf16[32,1024]{1,0:T(8,128)(2,1)S(1)}, bf16[32,1024]{1,0:T(8,128)(2,1)}, u32[]{:S(2)}) copy-start(bf16[32,1024]{1,0:T(8,128)(2,1)} %old_ref.3) | copy-start | bytes 196612
  64.6 7.4 %copy-start.10 = (f32[129]{0:T(256)S(1)}, f32[129]{0:T(256)}, u32[]{:S(2)}) copy-start(f32[129]{0:T(256)} %param.15) | copy-start | bytes 1552

commit v4 on v3

v4 whole, which is shorter than its diff:
```python
import functools
import math

import jax
import jax.numpy as jnp
from jax import lax
from jax.experimental import pallas as pl
from jax.experimental.pallas import tpu as pltpu
from jax.sharding import PartitionSpec as P

TILE = 32
BLOCK = 128
NBLK = 32
RAD = 8
RIDGE = 1.0
GROUP = 4
LANES = 128

SMEM = pltpu.MemorySpace.SMEM


def whole(space=pltpu.MemorySpace.VMEM):
    return pl.BlockSpec(memory_space=space)


def params(limit):
    return pltpu.CompilerParams(vmem_limit_bytes=limit * 2**20)


def cost(microseconds):
    return pl.CostEstimate(
        flops=microseconds * 10**9, bytes_accessed=microseconds * 10**6, transcendentals=0
    )


def block_of(support_ref, owner_ref, tile, slot):
    held = support_ref[slot, tile]
    return held >= 0, owner_ref[jnp.maximum(held, 0)]


def image_kernel(sign, both, support_ref, owner_ref, *refs):
    traces_refs, refs = refs[: 1 + both], refs[1 + both :]
    if both:
        foot_ref, field_ref, fresh_ref, out_ref, fresh_out, images = refs
        fresh_out[...] = fresh_ref[...]
    else:
        foot_ref, field_ref, out_ref, images = refs
    tiles, slots = foot_ref.shape[0], foot_ref.shape[1]
    rows, frames, cols = field_ref.shape
    group = LANES // TILE

    def block(tile, slot):
        live, position = block_of(support_ref, owner_ref, tile, slot)
        at = pl.ds(pl.multiple_of(position * (BLOCK // 2), BLOCK // 2), BLOCK // 2)
        if both:
            old, new = [ref[at, :].astype(jnp.float32) for ref in traces_refs]
            part = unpack(old - new)
        else:
            part = unpack(traces_refs[0][at, :])
        return jnp.where(live, part, jnp.zeros_like(part))

    for strip in range(cols // LANES):
        for inner in range(group):
            tile = strip * group + inner
            images[strip, :, inner * TILE : (inner + 1) * TILE, :] = jnp.dot(
                jnp.concatenate([foot_ref[tile, slot] for slot in range(slots)], axis=1),
                jnp.concatenate([block(tile, slot) for slot in range(slots)], axis=0),
                preferred_element_type=jnp.float32,
            ).reshape(rows, TILE, frames)
        lanes = slice(strip * LANES, (strip + 1) * LANES)
        for row in range(0, rows, 2):
            turned = jnp.concatenate([images[strip, row], images[strip, row + 1]], axis=1).T
            for k in range(2):
                part = turned[k * frames : (k + 1) * frames]
                out_ref[row + k, :, lanes] = (
                    field_ref[row + k, :, lanes].astype(jnp.float32) + sign * part
                ).astype(jnp.bfloat16)


def add_image(sign, support, owner_map, traces, foot, field, name, fresh=()):
    rows, frames, cols = field.shape
    made = pl.pallas_call(
        functools.partial(image_kernel, sign, len(traces) - 1),
        out_shape=[jax.ShapeDtypeStruct(x.shape, jnp.bfloat16) for x in (field, *fresh)],
        in_specs=[whole(SMEM), whole(SMEM)]
        + [whole() for _ in range(len(traces) + 2 + len(fresh))],
        out_specs=[whole() for _ in range(1 + len(fresh))],
        scratch_shapes=[pltpu.VMEM((cols // LANES, rows, LANES, frames), jnp.float32)],
        compiler_params=params(20),
        cost_estimate=cost(5),
        name=name,
    )(support, owner_map, *traces, foot, field, *fresh)
    return made if fresh else made[0]


def project_kernel(
    support_ref, owner_ref, foot_ref, field_ref, packed_ref, view, sums_ref, norms_ref
):
    tiles, slots, pixels, _ = foot_ref.shape
    rows, frames, cols = field_ref.shape
    group = LANES // TILE
    sums_ref[...] = jnp.zeros_like(sums_ref)
    norms_ref[...] = jnp.zeros_like(norms_ref)
    lane = lax.broadcasted_iota(jnp.int32, (frames, LANES), 1)

    def add(tile, slot):
        both = jnp.dot(
            view[tile],
            jnp.concatenate([foot_ref[tile, slot], foot_ref[tile, slot + 1]], axis=1),
            preferred_element_type=jnp.float32,
        )
        for k in range(2):
            live, position = block_of(support_ref, owner_ref, tile, slot + k)
            part = both[:, k * BLOCK : (k + 1) * BLOCK]
            sums_ref[position] += jnp.where(live, part, 0.0)
            wide = foot_ref[tile, slot + k].astype(jnp.float32)
            square = jnp.sum((wide * wide).reshape(pixels // 8, 8, BLOCK), axis=0)
            norms_ref[position] += jnp.where(live, square, 0.0)

    for strip in range(cols // LANES):
        lanes = slice(strip * LANES, (strip + 1) * LANES)

        for step in range(rows // group):
            source = [
                field_ref[step * group + k, :, lanes].astype(jnp.float32) for k in range(group)
            ]
            at = slice(step * LANES, (step + 1) * LANES)
            for t in range(group):
                line = None
                for k in range(group):
                    shift = (k - t) * TILE % LANES
                    moved = pltpu.roll(source[k], shift, 1) if shift else source[k]
                    line = moved if k == 0 else jnp.where(lane >= k * TILE, moved, line)
                view[strip * group + t, :, at] = line.astype(jnp.bfloat16)

        for inner in range(group):
            add(strip * group + inner, 0)

    for tile in range(tiles):
        for slot in range(2, slots, 2):

            @pl.when(support_ref[slot, tile] >= 0)
            def _(tile=tile, slot=slot):
                add(tile, slot)

    groups, each = packed_ref.shape[0], packed_ref.shape[1] - PACK
    per = each // frames
    for tile in range(groups):
        base = tile * per
        packed_ref[tile, :each] = (
            sums_ref[base : base + per].reshape(each, BLOCK).astype(jnp.bfloat16)
        )
        lines = [jnp.sum(norms_ref[base + q], axis=0, keepdims=True) for q in range(per)]
        fill = [jnp.zeros((PACK // 2 - per, BLOCK), jnp.float32)]
        norms = jnp.concatenate(lines + fill, axis=0)
        high = norms.astype(jnp.bfloat16).astype(jnp.float32)
        packed_ref[tile, each : each + PACK] = jnp.concatenate(
            [high, norms - high], axis=0
        ).astype(jnp.bfloat16)


def project(support, owner_map, foot, field, times):
    rows, frames, cols = field.shape
    return pl.pallas_call(
        project_kernel,
        out_shape=jax.ShapeDtypeStruct((lax.axis_size("tile"), times * PACK + PACK, LANES), jnp.bfloat16),
        in_specs=[whole(SMEM), whole(SMEM), whole(), whole()],
        out_specs=whole(),
        scratch_shapes=[
            pltpu.VMEM((foot.shape[0], frames, TILE * TILE), jnp.bfloat16),
            pltpu.VMEM((NBLK, frames, BLOCK), jnp.float32),
            pltpu.VMEM((NBLK, 8, BLOCK), jnp.float32),
        ],
        compiler_params=params(20),
        cost_estimate=cost(7),
        name="project",
    )(support, owner_map, foot, field)


MESH = pl.DeviceIdType.MESH
PACK = 16
HALF_LANES = LANES // 2


def low_lanes():
    return lax.broadcasted_iota(jnp.int32, (PACK, LANES), 1) < HALF_LANES


def join_low(left, right):
    return jnp.where(low_lanes(), left, pltpu.roll(right, HALF_LANES, 1))


def join_high(left, right):
    return jnp.where(low_lanes(), pltpu.roll(left, HALF_LANES, 1), right)


def chunks_of(top, bottom):
    return join_low(top, bottom), join_high(top, bottom)


def unpack(packed):
    wide = packed.astype(jnp.float32)
    turned = pltpu.roll(wide, HALF_LANES, 1)
    parts = []
    for k in range(packed.shape[0] // PACK):
        rows = slice(k * PACK, (k + 1) * PACK)
        parts += [wide[rows, :HALF_LANES], turned[rows, :HALF_LANES]]
    return jnp.concatenate(parts, axis=0).astype(jnp.bfloat16)


def far_first(peers, square):
    side = math.isqrt(peers) if square else peers
    if square and side * side != peers:
        side = peers
    steps = [(a, b) for a in range(peers // side) for b in range(side)][1:]

    def hops(step):
        return min(step[0], peers // side - step[0]) + min(step[1], side - step[1])

    return side, sorted(steps, key=hops, reverse=True)


class Place:
    def __init__(self, tiles, times):
        self.chips, self.times = tiles // 2, times
        self.tile, self.time = lax.axis_index("tile"), lax.axis_index("tm")
        self.chip, self.core = self.tile // 2, lax.rem(self.tile, 2)
        self.side, self.time_steps = far_first(times, True)
        chip_steps = [b for _, b in far_first(self.chips, False)[1]]
        self.tile_steps = [(b, k) for b in chip_steps for k in range(2)] + [(0, 1)]

    def tile_at(self, step, sign=1):
        core = 1 - self.core if step[1] else self.core
        return lax.rem(self.chip + sign * step[0] + self.chips, self.chips) * 2 + core

    def time_at(self, d, sign=1):
        a, b = self.time_steps[d - 1]
        rings = self.times // self.side
        return lax.rem(self.time // self.side + sign * a + rings, rings) * self.side + lax.rem(
            lax.rem(self.time, self.side) + sign * b + self.side, self.side
        )

    def signal(self):
        barrier = pltpu.get_barrier_semaphore()
        peers = [(self.tile, self.time_at(d)) for d in range(1, self.times)]
        peers += [(self.tile_at(step), self.time) for step in self.tile_steps]
        for peer in peers:
            pl.semaphore_signal(barrier, inc=1, device_id=peer, device_id_type=MESH)
        self.peers = len(peers)

    def wait(self):
        pl.semaphore_wait(pltpu.get_barrier_semaphore(), self.peers)


def send(source, target, send_sem, recv_sem, device):
    return pltpu.make_async_remote_copy(
        src_ref=source,
        dst_ref=target,
        send_sem=send_sem,
        recv_sem=recv_sem,
        device_id=device,
        device_id_type=MESH,
    )


def spread(place, chunks, full, sems, meanwhile=None):
    (ts, tr), (xs, xr) = sems
    tile, time = place.tile, place.time

    def rows(index):
        return pl.ds(pl.multiple_of(index * PACK, PACK), PACK)

    first = []
    for d in range(1, place.times):
        peer = place.time_at(d)
        copy = send(
            chunks.at[peer], full.at[tile, rows(time)], ts.at[d], tr.at[d], (tile, peer)
        )
        copy.start()
        first.append(copy)
    full[tile, rows(time)] = chunks[time]
    if meanwhile:
        meanwhile()
    for d, copy in enumerate(first, 1):
        came = place.time_at(d, -1)
        send(
            chunks.at[time], full.at[tile, rows(came)], ts.at[d], tr.at[d], (tile, came)
        ).wait_recv()
    second = []
    for i, step in enumerate(place.tile_steps):
        copy = send(
            full.at[tile], full.at[tile], xs.at[i], xr.at[i], (place.tile_at(step), time)
        )
        copy.start()
        second.append(copy)
    for i, step in enumerate(place.tile_steps):
        came = place.tile_at(step, -1)
        send(full.at[came], full.at[came], xs.at[i], xr.at[i], (came, time)).wait_recv()
    for copy in first + second:
        copy.wait_send()


def pair_sems(*counts):
    return [pltpu.SemaphoreType.DMA((n,)) for n in counts for _ in range(2)]


def pairs(sems):
    return [(sems[2 * k], sems[2 * k + 1]) for k in range(len(sems) // 2)]


def old_kernel(
    tiles, times, offsets_ref, weights_hbm, old_hbm, full_ref, sorted_ref,
    weights, old, chunks, local, *sems
):
    place = Place(tiles, times)
    fetch_old = pltpu.make_async_copy(old_hbm, old, local.at[0])
    fetch_old.start()
    fetch_weights = pltpu.make_async_copy(weights_hbm, weights, local.at[1])
    fetch_weights.start()
    place.signal()
    fetch_old.wait()
    for i in range(times // 2):
        part = old[:, i * LANES : (i + 1) * LANES].astype(jnp.float32)
        even, odd = chunks_of(part[:PACK], part[PACK:])
        chunks[2 * i] = even.astype(jnp.bfloat16)
        chunks[2 * i + 1] = odd.astype(jnp.bfloat16)
    place.wait()

    def meanwhile():
        fetch_weights.wait()
        sort_weights(offsets_ref, weights, sorted_ref)

    spread(place, chunks, full_ref, pairs(sems), meanwhile)


def remote_params(identity, limit):
    return pltpu.CompilerParams(
        vmem_limit_bytes=limit * 2**20, collective_id=identity, has_side_effects=True
    )


def spread_old(traces_old, offsets, weights):
    tiles, times = lax.axis_size("tile"), lax.axis_size("tm")
    count, rows, cols = weights.shape
    return pl.pallas_call(
        functools.partial(old_kernel, tiles, times),
        out_shape=[
            jax.ShapeDtypeStruct((tiles, times * PACK, LANES), jnp.bfloat16),
            jax.ShapeDtypeStruct((count * PLANES, rows, LANES), jnp.float32),
        ],
        in_specs=[whole(SMEM), whole(pltpu.MemorySpace.HBM), whole(pltpu.MemorySpace.HBM)],
        out_specs=[whole()] * 2,
        scratch_shapes=[
            pltpu.VMEM(weights.shape, weights.dtype),
            pltpu.VMEM(traces_old.shape, traces_old.dtype),
            pltpu.VMEM((times, PACK, LANES), jnp.bfloat16),
            pltpu.SemaphoreType.DMA((2,)),
        ]
        + pair_sems(times, tiles - 1),
        compiler_params=remote_params(0, 54),
        cost_estimate=cost(15),
        name="spread_old",
    )(offsets, weights, traces_old)


def exchange_kernel(
    tiles, times, taps_ref, old_ref, sums_ref, full_ref, fresh_ref,
    group_buf, owner_send, owner_buf, stacked, spare, band, chunks, *sems
):
    place = Place(tiles, times)
    (gs, gr), (ts, tr), *rest = pairs(sems)
    tile, time = place.tile, place.time
    rows = times * PACK
    place.signal()
    place.wait()
    to_group = []
    for i, step in enumerate(place.tile_steps):
        peer = place.tile_at(step)
        copy = send(sums_ref.at[peer], group_buf.at[i], gs.at[i], gr.at[i], (peer, time))
        copy.start()
        to_group.append(copy)
    mine = sums_ref[tile].astype(jnp.float32)
    for i, copy in reversed(list(enumerate(to_group))):
        copy.wait_recv()
        mine += group_buf[i].astype(jnp.float32)
    frames = rows * LANES // (2 * PACK * times)
    each = BLOCK // (2 * PACK)
    for q in range(rows // frames):
        turned = mine[q * frames : (q + 1) * frames].T
        for k in range(each):
            top = turned[2 * k * PACK : (2 * k + 1) * PACK]
            bottom = turned[(2 * k + 1) * PACK : (2 * k + 2) * PACK]
            owner_send[q * each + k] = jnp.concatenate([top, bottom], axis=1)
    to_owner = []
    for d in range(1, times):
        peer = place.time_at(d)
        copy = send(owner_send.at[peer], owner_buf.at[time], ts.at[d], tr.at[d], (tile, peer))
        copy.start()
        to_owner.append(copy)
    owner_buf[time] = owner_send[time]

    spare[...] = jnp.zeros_like(spare)
    spare[0:1, 0 : taps_ref.shape[1]] = taps_ref[...]
    wide = jnp.broadcast_to(spare[0:1, :], (2 * LANES, 2 * LANES))
    band[...] = pltpu.roll(wide, LANES, 1, stride=1, stride_axis=0)[:, :LANES]

    high = mine[rows : rows + PACK]
    both = high + pltpu.roll(high, PACK - PACK // 2, 0)
    block = lax.rem(time * 2 * PACK, BLOCK)
    line = lax.broadcasted_iota(jnp.int32, (PACK, LANES), 0)
    lane = lax.broadcasted_iota(jnp.int32, (PACK, LANES), 1)
    row = jnp.sum(
        jnp.where(line == time // (BLOCK // (2 * PACK)), both, 0.0), axis=0, keepdims=True
    )
    columns = [
        jnp.sum(jnp.where(lane == line + block + k * PACK, row, 0.0), axis=1, keepdims=True)
        for k in range(2)
    ]
    divisor = jnp.where(lane < HALF_LANES, columns[0], columns[1]) + RIDGE

    for d in range(1, times):
        came = place.time_at(d, -1)
        send(
            owner_send.at[came], owner_buf.at[came], ts.at[d], tr.at[d], (tile, came)
        ).wait_recv()
    update = [jnp.zeros((PACK, LANES), jnp.float32)]
    for i in range(times // 2):
        part = old_ref[:, i * LANES : (i + 1) * LANES].astype(jnp.float32)
        for k, old in enumerate(chunks_of(part[:PACK], part[PACK:])):
            update.append(old + owner_buf[2 * i + k] / divisor)
    update.append(jnp.zeros((PACK, LANES), jnp.float32))
    steps = times // 2
    lines = [
        (join_low(update[2 * i], update[2 * i + 1]), join_high(update[2 * i], update[2 * i + 1]))
        for i in range(steps + 1)
    ]
    for i in range(steps):
        for k in range(2):
            at = slice((2 * i + k) * PACK, (2 * i + k + 1) * PACK)
            stacked[at, :LANES] = lines[i][k]
            stacked[at, LANES:] = lines[i + 1][k]
    made = jnp.dot(
        stacked[...],
        band[...],
        precision=lax.Precision.HIGHEST,
        preferred_element_type=jnp.float32,
    )
    made = jnp.maximum(made, 0.0)
    for i in range(steps):
        part = made[2 * i * PACK : (2 * i + 2) * PACK]
        fresh_ref[:, i * LANES : (i + 1) * LANES] = part.astype(jnp.bfloat16)
        even, odd = chunks_of(part[:PACK], part[PACK:])
        chunks[2 * i] = even.astype(jnp.bfloat16)
        chunks[2 * i + 1] = odd.astype(jnp.bfloat16)
    spread(place, chunks, full_ref, rest)
    for copy in to_group + to_owner:
        copy.wait_send()


def exchange(taps, traces_old, sums):
    tiles, times = lax.axis_size("tile"), lax.axis_size("tm")
    rows = times * PACK
    return pl.pallas_call(
        functools.partial(exchange_kernel, tiles, times),
        out_shape=[
            jax.ShapeDtypeStruct((tiles, rows, LANES), jnp.bfloat16),
            jax.ShapeDtypeStruct(traces_old.shape, jnp.bfloat16),
        ],
        in_specs=[whole()] * 3,
        out_specs=[whole()] * 2,
        scratch_shapes=[
            pltpu.VMEM((tiles - 1, rows + PACK, LANES), jnp.bfloat16),
            pltpu.VMEM((times, PACK, LANES), jnp.float32),
            pltpu.VMEM((times, PACK, LANES), jnp.float32),
            pltpu.VMEM((times * PACK, 2 * LANES), jnp.float32),
            pltpu.VMEM((8, 2 * LANES), jnp.float32),
            pltpu.VMEM((2 * LANES, LANES), jnp.float32),
            pltpu.VMEM((times, PACK, LANES), jnp.bfloat16),
        ]
        + pair_sems(tiles - 1, times, times, tiles - 1),
        compiler_params=remote_params(1, 12),
        cost_estimate=cost(25),
        name="exchange",
    )(taps[None, :], traces_old, sums)


PLANES = 4
REACH = RAD // PLANES
ROLLS = 2 * REACH + 1


def sorting(cols):
    shape = (cols, PLANES * LANES)
    column = lax.broadcasted_iota(jnp.int32, shape, 0)
    place = lax.broadcasted_iota(jnp.int32, shape, 1)
    hit = column == PLANES * lax.rem(place, LANES // 2) + place // LANES
    return hit.astype(jnp.float32).astype(jnp.bfloat16)


def unsorting(cols):
    shape = (PLANES * LANES, 2 * cols)
    place = lax.broadcasted_iota(jnp.int32, shape, 0)
    target = lax.broadcasted_iota(jnp.int32, shape, 1)
    hit = target == lax.rem(place, LANES) // (LANES // 2) * cols + (
        PLANES * lax.rem(place, LANES // 2) + place // LANES
    )
    return hit.astype(jnp.float32).astype(jnp.bfloat16)


def sort_weights(offsets_ref, weights_ref, sorted_ref, each=8):
    count, rows, cols = weights_ref.shape
    sort = sorting(cols)
    column = lax.broadcasted_iota(jnp.int32, (rows, cols), 1)

    def some(step, carry):
        parts = []
        for u in range(each):
            j = step * each + u
            place = column + offsets_ref[1, j]
            parts.append(jnp.where((place >= 0) & (place < cols), weights_ref[j], 0.0))
        left = jnp.concatenate(parts, axis=0)
        total = jnp.zeros((each * rows, PLANES * LANES), jnp.float32)
        for _ in range(3):
            piece = left.astype(jnp.bfloat16)
            total += jnp.dot(piece, sort, preferred_element_type=jnp.float32)
            left = left - piece.astype(jnp.float32)
        for u in range(each):
            for p in range(PLANES):
                sorted_ref[(step * each + u) * PLANES + p] = total[
                    u * rows : (u + 1) * rows, p * LANES : (p + 1) * LANES
                ]
        return carry

    lax.fori_loop(0, count // each, some, 0)


def clean_kernel(
    tiles, offsets_ref, weights_ref, first_ref, third_ref,
    copies_0, copies_1, field, halo, table, sends, recvs
):
    rows, frames, cols = first_ref.shape
    count = offsets_ref.shape[1]
    half = frames // 2
    padded = rows + 2 * RAD
    copies = (copies_0, copies_1)
    tile, time = lax.axis_index("tile"), lax.axis_index("tm")
    below, above = lax.rem(tile + 1, tiles), lax.rem(tile + tiles - 1, tiles)
    barrier = pltpu.get_barrier_semaphore()
    for peer in (below, above):
        pl.semaphore_signal(barrier, inc=1, device_id=(peer, time), device_id_type=MESH)

    sort = sorting(cols)
    lower = lax.broadcasted_iota(jnp.int32, (RAD, half, LANES), 2) < LANES // 2

    def sort_rows(base):
        wide = jnp.dot(
            first_ref[pl.ds(base, RAD)].reshape(RAD * frames, cols),
            sort,
            preferred_element_type=jnp.float32,
        ).reshape(RAD, frames, PLANES * LANES)
        for p in range(PLANES):
            plane = wide[:, :, p * LANES : (p + 1) * LANES]
            field[0, pl.ds(base, RAD), p] = jnp.where(
                lower, plane[:, :half], plane[:, half:]
            ).astype(jnp.bfloat16)

    def halo_copies(turn):
        return [
            send(
                field.at[turn, pl.ds(start, RAD)],
                halo.at[turn, side],
                sends.at[turn, side],
                recvs.at[turn, side],
                (peer, time),
            )
            for side, start, peer in ((0, rows - RAD, below), (1, 0, above))
        ]

    def roll_plane(turn, p, values, row):
        for s in range(ROLLS):
            shift = (REACH - s) % LANES
            copies[turn][(s * PLANES + p) * padded + row] = (
                pltpu.roll(values, shift, 1) if shift else values
            )

    def roll_own():
        def some(step, carry):
            for u in range(2 * RAD):
                row = step * 2 * RAD + u
                for p in range(PLANES):
                    roll_plane(0, p, field[0, row, p].astype(jnp.float32), RAD + row)
            return carry

        lax.fori_loop(0, rows // (2 * RAD), some, 0)

    def roll_halo(turn):
        for side, edge, base in ((0, tile == 0, 0), (1, tile == tiles - 1, RAD + rows)):
            for row in range(RAD):
                for p in range(PLANES):
                    values = halo[turn, side, row, p].astype(jnp.float32)
                    roll_plane(turn, p, jnp.where(edge, 0.0, values), base + row)

    def run_rows(turn, edges):
        def some(step, carry):
            row = step * RAD + RAD
            if edges:
                row = jnp.where(step < RAD // RAD, step * RAD, step * RAD + rows - 2 * RAD)
            for p in range(PLANES):
                total = [jnp.zeros((half, LANES), jnp.float32) for _ in range(RAD)]
                for j in range(count):
                    k = j * PLANES + p
                    source = copies[turn][pl.ds(table[k] + row, RAD)]
                    for r in range(RAD):
                        total[r] += weights_ref[k, pl.ds(row + r, 1), :] * source[r]
                mine = copies[turn][pl.ds((REACH * PLANES + p) * padded + RAD + row, RAD)]
                for r in range(RAD):
                    out = (mine[r] - total[r]).astype(jnp.bfloat16)
                    field[1 - turn, row + r, p] = out
                    if turn == 0:
                        roll_plane(1, p, out.astype(jnp.float32), RAD + row + r)
            return carry

        lax.fori_loop(0, (2 * RAD if edges else rows - 2 * RAD) // RAD, some, 0)

    sort_rows(0)
    sort_rows(rows - RAD)
    pl.semaphore_wait(barrier, 2)
    for turn in range(2):
        moving = halo_copies(turn)
        for copy in moving:
            copy.start()
        if turn == 0:
            for base in range(RAD, rows - RAD, RAD):
                sort_rows(base)
            for j in range(count):
                for p in range(PLANES):
                    q = p + offsets_ref[1, j] + RAD
                    table[j * PLANES + p] = q * padded + RAD + offsets_ref[0, j]
            roll_own()
        run_rows(turn, False)
        for copy in moving:
            copy.wait()
        roll_halo(turn)
        run_rows(turn, True)

    unsort = unsorting(cols)
    for base in range(0, rows, RAD):
        planes = [field[0, base : base + RAD, p].astype(jnp.float32) for p in range(PLANES)]
        flat = jnp.concatenate(planes, axis=2).reshape(RAD * half, PLANES * LANES)
        back = jnp.dot(flat.astype(jnp.bfloat16), unsort, preferred_element_type=jnp.float32)
        back = back.astype(jnp.bfloat16).reshape(RAD, half, 2 * cols)
        for k in range(2):
            third_ref[base : base + RAD, k * half : (k + 1) * half] = back[
                :, :, k * cols : (k + 1) * cols
            ]


def clean(offsets, weights, first):
    rows, frames, cols = first.shape
    row = (PLANES, frames // 2, LANES)
    copies = pltpu.VMEM((ROLLS * PLANES * (rows + 2 * RAD),) + row[1:], jnp.float32)
    return pl.pallas_call(
        functools.partial(clean_kernel, lax.axis_size("tile")),
        out_shape=jax.ShapeDtypeStruct(first.shape, jnp.bfloat16),
        in_specs=[whole(SMEM), whole(), whole()],
        out_specs=whole(),
        scratch_shapes=[
            copies,
            copies,
            pltpu.VMEM((2, rows) + row, jnp.bfloat16),
            pltpu.VMEM((2, 2, RAD) + row, jnp.bfloat16),
            pltpu.SMEM((PLANES * offsets.shape[1],), jnp.int32),
            pltpu.SemaphoreType.DMA((2, 2)),
            pltpu.SemaphoreType.DMA((2, 2)),
        ],
        compiler_params=remote_params(2, 42),
        cost_estimate=cost(25),
        name="clean",
    )(offsets, weights, first)


def body(movie, footprints, support, cycle_offsets, cycle_weights, owner_map, traces_old, taps):
    tiles, slots = support.shape
    times = lax.axis_size("tm")
    foot = footprints.reshape(tiles, slots, TILE * TILE, BLOCK)
    field = movie.transpose(0, 2, 1)
    blocks, offsets = support.T, cycle_offsets.T
    old_full, weights = spread_old(traces_old, offsets, cycle_weights)
    old_full = old_full.reshape(-1, LANES)
    first = add_image(-1.0, blocks, owner_map, [old_full], foot, field, "first_residual")
    third = clean(offsets, weights, first)
    sums = project(blocks, owner_map, foot, third, times)
    new_full, fresh = exchange(taps, traces_old, sums)
    new_full = new_full.reshape(-1, LANES)
    residual, fresh = add_image(
        1.0, blocks, owner_map, [old_full, new_full], foot, third, "final_residual", (fresh,)
    )
    return (residual.transpose(0, 2, 1), fresh)


def solution(mesh):
    return jax.shard_map(
        body,
        mesh=mesh,
        in_specs=(
            P("tile", None, "tm"),
            P("tile", None, None, None, None),
            P("tile", None),
            P(),
            P(None, "tile", None),
            P(),
            P(("tile", "tm"), None),
            P(),
        ),
        out_specs=(P("tile", None, "tm"), P(("tile", "tm"), None)),
        check_vma=False,
    )
```

time: 108 us -> 90.4 us (0.84)
  Pallas kernels: 100 us -> 88.3 us
  local copies, waits for them, and re-layouts: 6.97 us -> 1.08 us
    pallas_call x1, Pallas kernels: 30.9 us -> 24.8 us  [clean(): pl.pallas_call(functools.partial(clean_kernel, lax.axis_size('tile')), ou...]
    pallas_call x2, Pallas kernels: 13.9 us -> 7.92 us  [add_image(): pl.pallas_call(functools.partial(image_kernel, sign, len(traces) - 1), ou...]
    unnamed x23 -> x20, local copies, waits for them, and re-layouts: 6.97 us -> 1.08 us
    pallas_call x1, Pallas kernels: 7.34 us -> 4.13 us  [project(): pl.pallas_call(project_kernel, out_shape=jax.ShapeDtypeStruct((lax.axis_s...]
    pallas_call x1, Pallas kernels: 20.2 us -> 22.5 us  [spread_old(): pl.pallas_call(functools.partial(old_kernel, tiles, times), out_shape=[ja...]
where the time goes in v4:
time: 90.4 us; the launch traced here: 90.2 us
  Pallas kernels  88.3 us (98%)
  local copies, waits for them, and re-layouts  1.08 us (1%)
    pallas_call x1, Pallas kernels, exchange(): pl.pallas_call(functools.partial(exchange_kernel, tiles, times), out_shap...  29 us
    pallas_call x1, Pallas kernels, clean(): pl.pallas_call(functools.partial(clean_kernel, lax.axis_size('tile')), ou...  24.8 us
    pallas_call x1, Pallas kernels, spread_old(): pl.pallas_call(functools.partial(old_kernel, tiles, times), out_shape=[ja...  22.5 us
    pallas_call x2, Pallas kernels, add_image(): pl.pallas_call(functools.partial(image_kernel, sign, len(traces) - 1), ou...  7.92 us
    pallas_call x1, Pallas kernels, project(): pl.pallas_call(project_kernel, out_shape=jax.ShapeDtypeStruct((lax.axis_s...  4.13 us

profile of v4, /device:TPU:1, one launch (start us, length us, event | category | flops | bytes accessed | tf_op | source)
XLA Modules:
  0.0 90.2 jit_solution(13501377095203004297)
XLA Ops:
  0.6 0.0 copy-start
  0.6 0.0 copy-start.1
  0.7 0.0 copy-start.3
  0.7 0.0 copy-start.6
  0.7 22.5 %spread_old.1 = (bf16[8,256,128]{2,1,0:T(8,128)(2,1)}, f32[192,32,128]{2,1,0:T(8,128)}) custom-call(s32[2,48]{1,0:T(2,128)} %bitcast.15, f32[48,32,256]{2,1,0:T(8,128)} %weights_hbm.1, bf16[32,1024]{1,0:T(8,128)(2,1)} %old_ref.1), custom_call_target="tpu_custom_call" | custom-call | flops 15000000512 | bytes 15000000 | tf_op jit(solution)/shard_map/spread_old/pallas_call | solution.py:345
  23.1 0.0 copy-done
  23.1 0.0 copy-done.1
  23.2 0.0 copy-done.3
  23.2 0.0 copy-done.6
  23.2 0.0 copy-start.7
  23.2 1.0 %copy-done.7 = bf16[8,256,128]{2,1,0:T(8,128)(2,1)S(1)} copy-done((bf16[8,256,128]{2,1,0:T(8,128)(2,1)S(1)}, bf16[8,256,128]{2,1,0:T(8,128)(2,1)}, u32[]{:S(2)}) %copy-start.7) | copy-done | bytes 524312
  24.2 0.0 copy-start.4
  24.2 0.0 copy-start.9
  24.2 3.5 %first_residual.1.first_ref = bf16[32,64,256]{2,1,0:T(8,128)(2,1)S(1)} custom-call(s32[4,8]{1,0:T(4,128)S(1)} %bitcast.12, s32[32]{0:T(128)S(1)} %copy-done.6, bf16[2048,128]{1,0:T(8,128)(2,1)S(1)} %bitcast.18, bf16[8,4,1024,128]{3,2,1,0:T(8,128)(2,1)S(1)} %bitcast.8, bf16[32,64,256]{2,1,0:T(8,128)(2,1)S(1)} %bitcast.11), custom_call_target="tpu_custom_call" | custom-call | flops 5000000000 | bytes 5000000 | tf_op jit(solution)/shard_map/first_residual/pallas_call | solution.py:82
  27.7 0.0 copy-done.4
  27.7 0.0 copy-done.9
  27.7 24.8 %clean.1.field_ref.refs_3_ = bf16[32,64,256]{2,1,0:T(8,128)(2,1)S(1)} custom-call(s32[2,48]{1,0:T(2,128)S(1)} %bitcast.16, f32[192,32,128]{2,1,0:T(8,128)S(1)} %copy-done.9, bf16[32,64,256]{2,1,0:T(8,128)(2,1)S(1)} %first_residual.1.first_ref), custom_call_target="tpu_custom_call" | custom-call | flops 24999999488 | bytes 25000000 | tf_op jit(solution)/shard_map/clean/pallas_call | solution.py:662
  52.6 0.0 copy-start.2
  52.6 0.0 copy-start.5
  52.6 4.1 %project.1.sums_ref = bf16[8,272,128]{2,1,0:T(8,128)(2,1)S(1)} custom-call(s32[4,8]{1,0:T(4,128)S(1)} %bitcast.13, s32[32]{0:T(128)S(1)} %copy-done.6, bf16[8,4,1024,128]{3,2,1,0:T(8,128)(2,1)S(1)} %bitcast.9, bf16[32,64,256]{2,1,0:T(8,128)(2,1)S(1)} %clean.1.field_ref.refs_3_), custom_call_target="tpu_custom_call" | custom-call | flops 7000000000 | bytes 7000000 | tf_op jit(solution)/shard_map/project/pallas_call | solution.py:164
  56.7 0.0 copy-done.2
  56.7 0.0 copy-done.5
  56.7 0.0 copy-start.8
  56.8 29.0 %exchange.1 = (bf16[8,256,128]{2,1,0:T(8,128)(2,1)S(1)}, bf16[32,1024]{1,0:T(8,128)(2,1)S(1)}) custom-call(f32[1,129]{1,0:T(1,128)S(1)} %bitcast.17, bf16[32,1024]{1,0:T(8,128)(2,1)S(1)} %copy-done.2, bf16[8,272,128]{2,1,0:T(8,128)(2,1)S(1)} %project.1.sums_ref), custom_call_target="tpu_custom_call" | custom-call | flops 24999999488 | bytes 25000000 | tf_op jit(solution)/shard_map/exchange/pallas_call | solution.py:463
  85.7 0.0 copy-done.8
  85.7 4.5 %final_residual.1 = (bf16[32,64,256]{2,1,0:T(8,128)(2,1)}, bf16[32,1024]{1,0:T(8,128)(2,1)}) custom-call(s32[4,8]{1,0:T(4,128)S(1)} %bitcast.14, s32[32]{0:T(128)S(1)} %copy-done.6, bf16[2048,128]{1,0:T(8,128)(2,1)S(1)} %bitcast.19, bf16[2048,128]{1,0:T(8,128)(2,1)S(1)} %bitcast.20, bf16[8,4,1024,128]{3,2,1,0:T(8,128)(2,1)S(1)} %bitcast.10, ...), custom_call_target="tpu_custom_call" | custom-call | flops 5000000000 | bytes 5000000 | tf_op jit(solution)/shard_map/final_residual/pallas_call | solution.py:82
Async XLA Ops:
  0.6 22.5 %copy-start = (bf16[8,4,32,32,128]{4,3,2,1,0:T(8,128)(2,1)S(1)}, bf16[8,4,32,32,128]{4,3,2,1,0:T(8,128)(2,1)}, u32[]{:S(2)}) copy-start(bf16[8,4,32,32,128]{4,3,2,1,0:T(8,128)(2,1)} %param.9) | copy-start | bytes 25165828
  0.6 22.5 %copy-start.1 = (bf16[32,256,64]{1,2,0:T(8,128)(2,1)S(1)}, bf16[32,256,64]{1,2,0:T(8,128)(2,1)}, u32[]{:S(2)}) copy-start(bf16[32,256,64]{1,2,0:T(8,128)(2,1)} %param.8) | copy-start | bytes 3145732
  0.7 22.5 %copy-start.3 = (s32[8,4]{0,1:T(4,128)S(1)}, s32[8,4]{0,1:T(4,128)}, u32[]{:S(2)}) copy-start(s32[8,4]{0,1:T(4,128)} %param.10) | copy-start | bytes 388
  0.7 22.5 %copy-start.6 = (s32[32]{0:T(128)S(1)}, s32[32]{0:T(128)}, u32[]{:S(2)}) copy-start(s32[32]{0:T(128)} %owner_ref.5) | copy-start | bytes 388
  23.2 1.0 %copy-start.7 = (bf16[8,256,128]{2,1,0:T(8,128)(2,1)S(1)}, bf16[8,256,128]{2,1,0:T(8,128)(2,1)}, u32[]{:S(2)}) copy-start(bf16[8,256,128]{2,1,0:T(8,128)(2,1)} %get-tuple-element.8) | copy-start | bytes 1572868
  24.2 3.5 %copy-start.4 = (s32[48,2]{0,1:T(2,128)S(1)}, s32[48,2]{0,1:T(2,128)}, u32[]{:S(2)}) copy-start(s32[48,2]{0,1:T(2,128)} %param.11) | copy-start | bytes 1156
  24.2 3.5 %copy-start.9 = (f32[192,32,128]{2,1,0:T(8,128)S(1)}, f32[192,32,128]{2,1,0:T(8,128)}, u32[]{:S(2)}) copy-start(f32[192,32,128]{2,1,0:T(8,128)} %get-tuple-element.9.weights_ref) | copy-start | bytes 9437188
  52.6 4.2 %copy-start.2 = (bf16[32,1024]{1,0:T(8,128)(2,1)S(1)}, bf16[32,1024]{1,0:T(8,128)(2,1)}, u32[]{:S(2)}) copy-start(bf16[32,1024]{1,0:T(8,128)(2,1)} %old_ref.1) | copy-start | bytes 196612
  52.6 4.2 %copy-start.5 = (f32[129]{0:T(256)S(1)}, f32[129]{0:T(256)}, u32[]{:S(2)}) copy-start(f32[129]{0:T(256)} %param.15) | copy-start | bytes 1552
  56.7 29.0 %copy-start.8 = (bf16[8,256,128]{2,1,0:T(8,128)(2,1)S(1)}, bf16[8,256,128]{2,1,0:T(8,128)(2,1)}, u32[]{:S(2)}) copy-start(bf16[8,256,128]{2,1,0:T(8,128)(2,1)} %get-tuple-element.8) | copy-start | bytes 1572868

commit v5 on v4

--- a/solution.py
+++ b/solution.py
@@ -143,27 +143,28 @@
             def _(tile=tile, slot=slot):
                 add(tile, slot)
 
-    groups, each = packed_ref.shape[0], packed_ref.shape[1] - PACK
+    each = packed_ref.shape[2] - PACK
     per = each // frames
-    for tile in range(groups):
-        base = tile * per
-        packed_ref[tile, :each] = (
-            sums_ref[base : base + per].reshape(each, BLOCK).astype(jnp.bfloat16)
-        )
-        lines = [jnp.sum(norms_ref[base + q], axis=0, keepdims=True) for q in range(per)]
-        fill = [jnp.zeros((PACK // 2 - per, BLOCK), jnp.float32)]
-        norms = jnp.concatenate(lines + fill, axis=0)
-        high = norms.astype(jnp.bfloat16).astype(jnp.float32)
-        packed_ref[tile, each : each + PACK] = jnp.concatenate(
-            [high, norms - high], axis=0
-        ).astype(jnp.bfloat16)
-
-
-def project(support, owner_map, foot, field, times):
+    for core in range(packed_ref.shape[0]):
+        for chip in range(packed_ref.shape[1]):
+            base = (2 * chip + core) * per
+            packed_ref[core, chip, :each] = (
+                sums_ref[base : base + per].reshape(each, BLOCK).astype(jnp.bfloat16)
+            )
+            lines = [jnp.sum(norms_ref[base + q], axis=0, keepdims=True) for q in range(per)]
+            fill = [jnp.zeros((PACK // 2 - per, BLOCK), jnp.float32)]
+            norms = jnp.concatenate(lines + fill, axis=0)
+            high = norms.astype(jnp.bfloat16).astype(jnp.float32)
+            packed_ref[core, chip, each : each + PACK] = jnp.concatenate(
+                [high, norms - high], axis=0
+            ).astype(jnp.bfloat16)
+
+
+def project(support, owner_map, foot, field, chips, times):
     rows, frames, cols = field.shape
     return pl.pallas_call(
         project_kernel,
-        out_shape=jax.ShapeDtypeStruct((lax.axis_size("tile"), times * PACK + PACK, LANES), jnp.bfloat16),
+        out_shape=jax.ShapeDtypeStruct((2, chips, times * PACK + PACK, LANES), jnp.bfloat16),
         in_specs=[whole(SMEM), whole(SMEM), whole(), whole()],
         out_specs=whole(),
         scratch_shapes=[
@@ -225,13 +226,12 @@
         self.chips, self.times = tiles // 2, times
         self.tile, self.time = lax.axis_index("tile"), lax.axis_index("tm")
         self.chip, self.core = self.tile // 2, lax.rem(self.tile, 2)
+        self.sibling = self.chip * 2 + 1 - self.core
         self.side, self.time_steps = far_first(times, True)
-        chip_steps = [b for _, b in far_first(self.chips, False)[1]]
-        self.tile_steps = [(b, k) for b in chip_steps for k in range(2)] + [(0, 1)]
-
-    def tile_at(self, step, sign=1):
-        core = 1 - self.core if step[1] else self.core
-        return lax.rem(self.chip + sign * step[0] + self.chips, self.chips) * 2 + core
+        self.chip_steps = [b for _, b in far_first(self.chips, False)[1]]
+
+    def chip_at(self, step):
+        return lax.rem(self.chip + step + self.chips, self.chips)
 
     def time_at(self, d, sign=1):
         a, b = self.time_steps[d - 1]
@@ -243,7 +243,8 @@
     def signal(self):
         barrier = pltpu.get_barrier_semaphore()
         peers = [(self.tile, self.time_at(d)) for d in range(1, self.times)]
-        peers += [(self.tile_at(step), self.time) for step in self.tile_steps]
+        peers += [(self.chip_at(d) * 2 + self.core, self.time) for d in self.chip_steps]
+        peers += [(self.sibling, self.time)]
         for peer in peers:
             pl.semaphore_signal(barrier, inc=1, device_id=peer, device_id_type=MESH)
         self.peers = len(peers)
@@ -264,7 +265,7 @@
 
 
 def spread(place, chunks, full, sems, meanwhile=None):
-    (ts, tr), (xs, xr) = sems
+    (ts, tr), (xs, xr), (ss, sr) = sems
     tile, time = place.tile, place.time
 
     def rows(index):
@@ -287,16 +288,32 @@
             chunks.at[time], full.at[tile, rows(came)], ts.at[d], tr.at[d], (tile, came)
         ).wait_recv()
     second = []
-    for i, step in enumerate(place.tile_steps):
+    for d in place.chip_steps:
         copy = send(
-            full.at[tile], full.at[tile], xs.at[i], xr.at[i], (place.tile_at(step), time)
+            full.at[tile],
+            full.at[tile],
+            xs.at[d],
+            xr.at[d],
+            (place.chip_at(d) * 2 + place.core, time),
         )
         copy.start()
         second.append(copy)
-    for i, step in enumerate(place.tile_steps):
-        came = place.tile_at(step, -1)
-        send(full.at[came], full.at[came], xs.at[i], xr.at[i], (came, time)).wait_recv()
-    for copy in first + second:
+    third = []
+    for d in [0, *reversed(place.chip_steps)]:
+        came = place.chip_at(-d) * 2 + place.core
+        if d:
+            send(full.at[came], full.at[came], xs.at[d], xr.at[d], (came, time)).wait_recv()
+        copy = send(
+            full.at[came], full.at[came], ss.at[d], sr.at[d], (place.sibling, time)
+        )
+        copy.start()
+        third.append(copy)
+    for d in range(place.chips):
+        came = place.chip_at(-d) * 2 + 1 - place.core
+        send(
+            full.at[came], full.at[came], ss.at[d], sr.at[d], (place.sibling, time)
+        ).wait_recv()
+    for copy in first + second + third:
         copy.wait_send()
 
 
@@ -356,7 +373,7 @@
             pltpu.VMEM((times, PACK, LANES), jnp.bfloat16),
             pltpu.SemaphoreType.DMA((2,)),
         ]
-        + pair_sems(times, tiles - 1),
+        + pair_sems(times, tiles // 2, tiles // 2),
         compiler_params=remote_params(0, 54),
         cost_estimate=cost(15),
         name="spread_old",
@@ -365,24 +382,37 @@
 
 def exchange_kernel(
     tiles, times, taps_ref, old_ref, sums_ref, full_ref, fresh_ref,
-    group_buf, owner_send, owner_buf, stacked, spare, band, chunks, *sems
+    pair_buf, x_send, x_buf, owner_send, owner_buf, stacked, spare, band, chunks, *sems
 ):
     place = Place(tiles, times)
-    (gs, gr), (ts, tr), *rest = pairs(sems)
-    tile, time = place.tile, place.time
+    (ps, pr), (xs, xr), (ts, tr), *rest = pairs(sems)
+    chips, tile, time, core = place.chips, place.tile, place.time, place.core
     rows = times * PACK
     place.signal()
     place.wait()
-    to_group = []
-    for i, step in enumerate(place.tile_steps):
-        peer = place.tile_at(step)
-        copy = send(sums_ref.at[peer], group_buf.at[i], gs.at[i], gr.at[i], (peer, time))
+    to_pair = []
+    for d in [*place.chip_steps, 0]:
+        at = place.chip_at(d)
+        copy = send(
+            sums_ref.at[1 - core, at], pair_buf.at[at], ps.at[d], pr.at[d], (place.sibling, time)
+        )
         copy.start()
-        to_group.append(copy)
-    mine = sums_ref[tile].astype(jnp.float32)
-    for i, copy in reversed(list(enumerate(to_group))):
+        to_pair.append((d, at, copy))
+    to_chip = []
+    mine = None
+    for d, at, copy in to_pair:
         copy.wait_recv()
-        mine += group_buf[i].astype(jnp.float32)
+        total = sums_ref[core, at].astype(jnp.float32) + pair_buf[at].astype(jnp.float32)
+        if d:
+            x_send[d] = total.astype(jnp.bfloat16)
+            out = send(x_send.at[d], x_buf.at[d], xs.at[d], xr.at[d], (at * 2 + core, time))
+            out.start()
+            to_chip.append(out)
+        else:
+            mine = total
+    for d, copy in reversed(list(zip(place.chip_steps, to_chip))):
+        copy.wait_recv()
+        mine += x_buf[d].astype(jnp.float32)
     frames = rows * LANES // (2 * PACK * times)
     each = BLOCK // (2 * PACK)
     for q in range(rows // frames):
@@ -453,13 +483,15 @@
         chunks[2 * i] = even.astype(jnp.bfloat16)
         chunks[2 * i + 1] = odd.astype(jnp.bfloat16)
     spread(place, chunks, full_ref, rest)
-    for copy in to_group + to_owner:
+    for copy in [c for _, _, c in to_pair] + to_chip + to_owner:
         copy.wait_send()
 
 
 def exchange(taps, traces_old, sums):
     tiles, times = lax.axis_size("tile"), lax.axis_size("tm")
+    chips = tiles // 2
     rows = times * PACK
+    group = (rows + PACK, LANES)
     return pl.pallas_call(
         functools.partial(exchange_kernel, tiles, times),
         out_shape=[
@@ -469,7 +501,9 @@
         in_specs=[whole()] * 3,
         out_specs=[whole()] * 2,
         scratch_shapes=[
-            pltpu.VMEM((tiles - 1, rows + PACK, LANES), jnp.bfloat16),
+            pltpu.VMEM((chips,) + group, jnp.bfloat16),
+            pltpu.VMEM((chips,) + group, jnp.bfloat16),
+            pltpu.VMEM((chips,) + group, jnp.bfloat16),
             pltpu.VMEM((times, PACK, LANES), jnp.float32),
             pltpu.VMEM((times, PACK, LANES), jnp.float32),
             pltpu.VMEM((times * PACK, 2 * LANES), jnp.float32),
@@ -477,7 +511,7 @@
             pltpu.VMEM((2 * LANES, LANES), jnp.float32),
             pltpu.VMEM((times, PACK, LANES), jnp.bfloat16),
         ]
-        + pair_sems(tiles - 1, times, times, tiles - 1),
+        + pair_sems(chips, chips, times, times, chips, chips),
         compiler_params=remote_params(1, 12),
         cost_estimate=cost(25),
         name="exchange",
@@ -681,7 +715,7 @@
 
 def body(movie, footprints, support, cycle_offsets, cycle_weights, owner_map, traces_old, taps):
     tiles, slots = support.shape
-    times = lax.axis_size("tm")
+    chips, times = lax.axis_size("tile") // 2, lax.axis_size("tm")
     foot = footprints.reshape(tiles, slots, TILE * TILE, BLOCK)
     field = movie.transpose(0, 2, 1)
     blocks, offsets = support.T, cycle_offsets.T
@@ -689,7 +723,7 @@
     old_full = old_full.reshape(-1, LANES)
     first = add_image(-1.0, blocks, owner_map, [old_full], foot, field, "first_residual")
     third = clean(offsets, weights, first)
-    sums = project(blocks, owner_map, foot, third, times)
+    sums = project(blocks, owner_map, foot, third, chips, times)
     new_full, fresh = exchange(taps, traces_old, sums)
     new_full = new_full.reshape(-1, LANES)
     residual, fresh = add_image(

time: 90.4 us -> 87.2 us (0.965)
  Pallas kernels: 88.3 us -> 85 us
    pallas_call x1, Pallas kernels: 29 us -> 26.6 us  [exchange(): pl.pallas_call(functools.partial(exchange_kernel, tiles, times), out_shap...]
where the time goes in v5:
time: 87.2 us; the launch traced here: 86.9 us
  Pallas kernels  85 us (97%)
  local copies, waits for them, and re-layouts  1.08 us (1%)
    pallas_call x1, Pallas kernels, exchange(): pl.pallas_call(functools.partial(exchange_kernel, tiles, times), out_shap...  26.6 us
    pallas_call x1, Pallas kernels, clean(): pl.pallas_call(functools.partial(clean_kernel, lax.axis_size('tile')), ou...  24.8 us
    pallas_call x1, Pallas kernels, spread_old(): pl.pallas_call(functools.partial(old_kernel, tiles, times), out_shape=[ja...  21.8 us
    pallas_call x2, Pallas kernels, add_image(): pl.pallas_call(functools.partial(image_kernel, sign, len(traces) - 1), ou...  7.93 us
    pallas_call x1, Pallas kernels, project(): pl.pallas_call(project_kernel, out_shape=jax.ShapeDtypeStruct((2, chips,...  3.85 us

profile of v5, /device:TPU:1, one launch (start us, length us, event | category | flops | bytes accessed | tf_op | source)
XLA Modules:
  0.0 86.9 jit_solution(17009074480013579596)
XLA Ops:
  0.6 0.0 copy-start
  0.6 0.0 copy-start.1
  0.7 0.0 copy-start.3
  0.7 0.0 copy-start.6
  0.7 21.8 %spread_old.1 = (bf16[8,256,128]{2,1,0:T(8,128)(2,1)}, f32[192,32,128]{2,1,0:T(8,128)}) custom-call(s32[2,48]{1,0:T(2,128)} %bitcast.15, f32[48,32,256]{2,1,0:T(8,128)} %weights_hbm.1, bf16[32,1024]{1,0:T(8,128)(2,1)} %old_ref.1), custom_call_target="tpu_custom_call" | custom-call | flops 15000000512 | bytes 15000000 | tf_op jit(solution)/shard_map/spread_old/pallas_call | solution.py:362
  22.5 0.0 copy-done
  22.5 0.0 copy-done.1
  22.5 0.0 copy-done.3
  22.5 0.0 copy-done.6
  22.5 0.0 copy-start.7
  22.5 1.0 %copy-done.7 = bf16[8,256,128]{2,1,0:T(8,128)(2,1)S(1)} copy-done((bf16[8,256,128]{2,1,0:T(8,128)(2,1)S(1)}, bf16[8,256,128]{2,1,0:T(8,128)(2,1)}, u32[]{:S(2)}) %copy-start.7) | copy-done | bytes 524312
  23.5 0.0 copy-start.4
  23.5 0.0 copy-start.9
  23.5 3.5 %first_residual.1.first_ref = bf16[32,64,256]{2,1,0:T(8,128)(2,1)S(1)} custom-call(s32[4,8]{1,0:T(4,128)S(1)} %bitcast.12, s32[32]{0:T(128)S(1)} %copy-done.6, bf16[2048,128]{1,0:T(8,128)(2,1)S(1)} %bitcast.18, bf16[8,4,1024,128]{3,2,1,0:T(8,128)(2,1)S(1)} %bitcast.8, bf16[32,64,256]{2,1,0:T(8,128)(2,1)S(1)} %bitcast.11), custom_call_target="tpu_custom_call" | custom-call | flops 5000000000 | bytes 5000000 | tf_op jit(solution)/shard_map/first_residual/pallas_call | solution.py:82
  27.0 0.0 copy-done.4
  27.0 0.0 copy-done.9
  27.0 24.8 %clean.1.field_ref.refs_3_ = bf16[32,64,256]{2,1,0:T(8,128)(2,1)S(1)} custom-call(s32[2,48]{1,0:T(2,128)S(1)} %bitcast.16, f32[192,32,128]{2,1,0:T(8,128)S(1)} %copy-done.9, bf16[32,64,256]{2,1,0:T(8,128)(2,1)S(1)} %first_residual.1.first_ref), custom_call_target="tpu_custom_call" | custom-call | flops 24999999488 | bytes 25000000 | tf_op jit(solution)/shard_map/clean/pallas_call | solution.py:696
  51.9 0.0 copy-start.2
  51.9 0.0 copy-start.5
  51.9 3.9 %project.1.sums_ref = bf16[2,4,272,128]{3,2,1,0:T(8,128)(2,1)S(1)} custom-call(s32[4,8]{1,0:T(4,128)S(1)} %bitcast.13, s32[32]{0:T(128)S(1)} %copy-done.6, bf16[8,4,1024,128]{3,2,1,0:T(8,128)(2,1)S(1)} %bitcast.9, bf16[32,64,256]{2,1,0:T(8,128)(2,1)S(1)} %clean.1.field_ref.refs_3_), custom_call_target="tpu_custom_call" | custom-call | flops 7000000000 | bytes 7000000 | tf_op jit(solution)/shard_map/project/pallas_call | solution.py:165
  55.8 0.0 copy-done.2
  55.8 0.0 copy-done.5
  55.8 0.0 copy-start.8
  55.8 26.6 %exchange.1 = (bf16[8,256,128]{2,1,0:T(8,128)(2,1)S(1)}, bf16[32,1024]{1,0:T(8,128)(2,1)S(1)}) custom-call(f32[1,129]{1,0:T(1,128)S(1)} %bitcast.17, bf16[32,1024]{1,0:T(8,128)(2,1)S(1)} %copy-done.2, bf16[2,4,272,128]{3,2,1,0:T(8,128)(2,1)S(1)} %project.1.sums_ref), custom_call_target="tpu_custom_call" | custom-call | flops 24999999488 | bytes 25000000 | tf_op jit(solution)/shard_map/exchange/pallas_call | solution.py:495
  82.4 0.0 copy-done.8
  82.4 4.5 %final_residual.1 = (bf16[32,64,256]{2,1,0:T(8,128)(2,1)}, bf16[32,1024]{1,0:T(8,128)(2,1)}) custom-call(s32[4,8]{1,0:T(4,128)S(1)} %bitcast.14, s32[32]{0:T(128)S(1)} %copy-done.6, bf16[2048,128]{1,0:T(8,128)(2,1)S(1)} %bitcast.19, bf16[2048,128]{1,0:T(8,128)(2,1)S(1)} %bitcast.20, bf16[8,4,1024,128]{3,2,1,0:T(8,128)(2,1)S(1)} %bitcast.10, ...), custom_call_target="tpu_custom_call" | custom-call | flops 5000000000 | bytes 5000000 | tf_op jit(solution)/shard_map/final_residual/pallas_call | solution.py:82
Async XLA Ops:
  0.6 21.8 %copy-start = (bf16[8,4,32,32,128]{4,3,2,1,0:T(8,128)(2,1)S(1)}, bf16[8,4,32,32,128]{4,3,2,1,0:T(8,128)(2,1)}, u32[]{:S(2)}) copy-start(bf16[8,4,32,32,128]{4,3,2,1,0:T(8,128)(2,1)} %param.9) | copy-start | bytes 25165828
  0.6 21.8 %copy-start.1 = (bf16[32,256,64]{1,2,0:T(8,128)(2,1)S(1)}, bf16[32,256,64]{1,2,0:T(8,128)(2,1)}, u32[]{:S(2)}) copy-start(bf16[32,256,64]{1,2,0:T(8,128)(2,1)} %param.8) | copy-start | bytes 3145732
  0.7 21.8 %copy-start.3 = (s32[8,4]{0,1:T(4,128)S(1)}, s32[8,4]{0,1:T(4,128)}, u32[]{:S(2)}) copy-start(s32[8,4]{0,1:T(4,128)} %param.10) | copy-start | bytes 388
  0.7 21.8 %copy-start.6 = (s32[32]{0:T(128)S(1)}, s32[32]{0:T(128)}, u32[]{:S(2)}) copy-start(s32[32]{0:T(128)} %owner_ref.5) | copy-start | bytes 388
  22.5 1.0 %copy-start.7 = (bf16[8,256,128]{2,1,0:T(8,128)(2,1)S(1)}, bf16[8,256,128]{2,1,0:T(8,128)(2,1)}, u32[]{:S(2)}) copy-start(bf16[8,256,128]{2,1,0:T(8,128)(2,1)} %get-tuple-element.8) | copy-start | bytes 1572868
  23.5 3.5 %copy-start.4 = (s32[48,2]{0,1:T(2,128)S(1)}, s32[48,2]{0,1:T(2,128)}, u32[]{:S(2)}) copy-start(s32[48,2]{0,1:T(2,128)} %param.11) | copy-start | bytes 1156
  23.5 3.5 %copy-start.9 = (f32[192,32,128]{2,1,0:T(8,128)S(1)}, f32[192,32,128]{2,1,0:T(8,128)}, u32[]{:S(2)}) copy-start(f32[192,32,128]{2,1,0:T(8,128)} %get-tuple-element.9.weights_ref) | copy-start | bytes 9437188
  51.9 3.9 %copy-start.2 = (bf16[32,1024]{1,0:T(8,128)(2,1)S(1)}, bf16[32,1024]{1,0:T(8,128)(2,1)}, u32[]{:S(2)}) copy-start(bf16[32,1024]{1,0:T(8,128)(2,1)} %old_ref.1) | copy-start | bytes 196612
  51.9 3.9 %copy-start.5 = (f32[129]{0:T(256)S(1)}, f32[129]{0:T(256)}, u32[]{:S(2)}) copy-start(f32[129]{0:T(256)} %param.15) | copy-start | bytes 1552
  55.8 26.6 %copy-start.8 = (bf16[8,256,128]{2,1,0:T(8,128)(2,1)S(1)}, bf16[8,256,128]{2,1,0:T(8,128)(2,1)}, u32[]{:S(2)}) copy-start(bf16[8,256,128]{2,1,0:T(8,128)(2,1)} %get-tuple-element.8) | copy-start | bytes 1572868

commit v6 on v5

--- a/solution.py
+++ b/solution.py
@@ -420,7 +420,8 @@
         for k in range(each):
             top = turned[2 * k * PACK : (2 * k + 1) * PACK]
             bottom = turned[(2 * k + 1) * PACK : (2 * k + 2) * PACK]
-            owner_send[q * each + k] = jnp.concatenate([top, bottom], axis=1)
+            both = jnp.concatenate([top, bottom], axis=1)
+            owner_send[q * each + k] = both.astype(jnp.bfloat16)
     to_owner = []
     for d in range(1, times):
         peer = place.time_at(d)
@@ -457,7 +458,7 @@
     for i in range(times // 2):
         part = old_ref[:, i * LANES : (i + 1) * LANES].astype(jnp.float32)
         for k, old in enumerate(chunks_of(part[:PACK], part[PACK:])):
-            update.append(old + owner_buf[2 * i + k] / divisor)
+            update.append(old + owner_buf[2 * i + k].astype(jnp.float32) / divisor)
     update.append(jnp.zeros((PACK, LANES), jnp.float32))
     steps = times // 2
     lines = [
@@ -504,8 +505,8 @@
             pltpu.VMEM((chips,) + group, jnp.bfloat16),
             pltpu.VMEM((chips,) + group, jnp.bfloat16),
             pltpu.VMEM((chips,) + group, jnp.bfloat16),
-            pltpu.VMEM((times, PACK, LANES), jnp.float32),
-            pltpu.VMEM((times, PACK, LANES), jnp.float32),
+            pltpu.VMEM((times, PACK, LANES), jnp.bfloat16),
+            pltpu.VMEM((times, PACK, LANES), jnp.bfloat16),
             pltpu.VMEM((times * PACK, 2 * LANES), jnp.float32),
             pltpu.VMEM((8, 2 * LANES), jnp.float32),
             pltpu.VMEM((2 * LANES, LANES), jnp.float32),

time: 87.2 us -> 86.5 us (level)
  no operation moved by 1% of the time
where the time goes in v6:
time: 86.5 us; the launch traced here: 86.3 us
  Pallas kernels  84.4 us (98%)
  local copies, waits for them, and re-layouts  1.08 us (1%)
    pallas_call x1, Pallas kernels, exchange(): pl.pallas_call(functools.partial(exchange_kernel, tiles, times), out_shap...  26.3 us
    pallas_call x1, Pallas kernels, clean(): pl.pallas_call(functools.partial(clean_kernel, lax.axis_size('tile')), ou...  24.8 us
    pallas_call x1, Pallas kernels, spread_old(): pl.pallas_call(functools.partial(old_kernel, tiles, times), out_shape=[ja...  21.8 us
    pallas_call x2, Pallas kernels, add_image(): pl.pallas_call(functools.partial(image_kernel, sign, len(traces) - 1), ou...  7.93 us
    pallas_call x1, Pallas kernels, project(): pl.pallas_call(project_kernel, out_shape=jax.ShapeDtypeStruct((2, chips,...  3.6 us

profile of v6, /device:TPU:1, one launch (start us, length us, event | category | flops | bytes accessed | tf_op | source)
XLA Modules:
  0.0 86.3 jit_solution(11083870833538942643)
XLA Ops:
  0.6 0.0 copy-start
  0.6 0.0 copy-start.1
  0.7 0.0 copy-start.3
  0.7 0.0 copy-start.6
  0.7 21.8 %spread_old.1 = (bf16[8,256,128]{2,1,0:T(8,128)(2,1)}, f32[192,32,128]{2,1,0:T(8,128)}) custom-call(s32[2,48]{1,0:T(2,128)} %bitcast.15, f32[48,32,256]{2,1,0:T(8,128)} %weights_hbm.1, bf16[32,1024]{1,0:T(8,128)(2,1)} %old_ref.1), custom_call_target="tpu_custom_call" | custom-call | flops 15000000512 | bytes 15000000 | tf_op jit(solution)/shard_map/spread_old/pallas_call | solution.py:362
  22.5 0.0 copy-done
  22.5 0.0 copy-done.1
  22.5 0.0 copy-done.3
  22.5 0.0 copy-done.6
  22.5 0.0 copy-start.7
  22.5 1.0 %copy-done.7 = bf16[8,256,128]{2,1,0:T(8,128)(2,1)S(1)} copy-done((bf16[8,256,128]{2,1,0:T(8,128)(2,1)S(1)}, bf16[8,256,128]{2,1,0:T(8,128)(2,1)}, u32[]{:S(2)}) %copy-start.7) | copy-done | bytes 524312
  23.5 0.0 copy-start.4
  23.5 0.0 copy-start.9
  23.5 3.5 %first_residual.1.first_ref = bf16[32,64,256]{2,1,0:T(8,128)(2,1)S(1)} custom-call(s32[4,8]{1,0:T(4,128)S(1)} %bitcast.12, s32[32]{0:T(128)S(1)} %copy-done.6, bf16[2048,128]{1,0:T(8,128)(2,1)S(1)} %bitcast.18, bf16[8,4,1024,128]{3,2,1,0:T(8,128)(2,1)S(1)} %bitcast.8, bf16[32,64,256]{2,1,0:T(8,128)(2,1)S(1)} %bitcast.11), custom_call_target="tpu_custom_call" | custom-call | flops 5000000000 | bytes 5000000 | tf_op jit(solution)/shard_map/first_residual/pallas_call | solution.py:82
  27.0 0.0 copy-done.4
  27.0 0.0 copy-done.9
  27.0 24.8 %clean.1.field_ref.refs_3_ = bf16[32,64,256]{2,1,0:T(8,128)(2,1)S(1)} custom-call(s32[2,48]{1,0:T(2,128)S(1)} %bitcast.16, f32[192,32,128]{2,1,0:T(8,128)S(1)} %copy-done.9, bf16[32,64,256]{2,1,0:T(8,128)(2,1)S(1)} %first_residual.1.first_ref), custom_call_target="tpu_custom_call" | custom-call | flops 24999999488 | bytes 25000000 | tf_op jit(solution)/shard_map/clean/pallas_call | solution.py:697
  51.9 0.0 copy-start.2
  51.9 0.0 copy-start.5
  51.9 3.6 %project.1.sums_ref = bf16[2,4,272,128]{3,2,1,0:T(8,128)(2,1)S(1)} custom-call(s32[4,8]{1,0:T(4,128)S(1)} %bitcast.13, s32[32]{0:T(128)S(1)} %copy-done.6, bf16[8,4,1024,128]{3,2,1,0:T(8,128)(2,1)S(1)} %bitcast.9, bf16[32,64,256]{2,1,0:T(8,128)(2,1)S(1)} %clean.1.field_ref.refs_3_), custom_call_target="tpu_custom_call" | custom-call | flops 7000000000 | bytes 7000000 | tf_op jit(solution)/shard_map/project/pallas_call | solution.py:165
  55.5 0.0 copy-done.2
  55.5 0.0 copy-done.5
  55.5 0.0 copy-start.8
  55.5 26.3 %exchange.1 = (bf16[8,256,128]{2,1,0:T(8,128)(2,1)S(1)}, bf16[32,1024]{1,0:T(8,128)(2,1)S(1)}) custom-call(f32[1,129]{1,0:T(1,128)S(1)} %bitcast.17, bf16[32,1024]{1,0:T(8,128)(2,1)S(1)} %copy-done.2, bf16[2,4,272,128]{3,2,1,0:T(8,128)(2,1)S(1)} %project.1.sums_ref), custom_call_target="tpu_custom_call" | custom-call | flops 24999999488 | bytes 25000000 | tf_op jit(solution)/shard_map/exchange/pallas_call | solution.py:496
  81.8 0.0 copy-done.8
  81.8 4.5 %final_residual.1 = (bf16[32,64,256]{2,1,0:T(8,128)(2,1)}, bf16[32,1024]{1,0:T(8,128)(2,1)}) custom-call(s32[4,8]{1,0:T(4,128)S(1)} %bitcast.14, s32[32]{0:T(128)S(1)} %copy-done.6, bf16[2048,128]{1,0:T(8,128)(2,1)S(1)} %bitcast.19, bf16[2048,128]{1,0:T(8,128)(2,1)S(1)} %bitcast.20, bf16[8,4,1024,128]{3,2,1,0:T(8,128)(2,1)S(1)} %bitcast.10, ...), custom_call_target="tpu_custom_call" | custom-call | flops 5000000000 | bytes 5000000 | tf_op jit(solution)/shard_map/final_residual/pallas_call | solution.py:82
Async XLA Ops:
  0.6 21.8 %copy-start = (bf16[8,4,32,32,128]{4,3,2,1,0:T(8,128)(2,1)S(1)}, bf16[8,4,32,32,128]{4,3,2,1,0:T(8,128)(2,1)}, u32[]{:S(2)}) copy-start(bf16[8,4,32,32,128]{4,3,2,1,0:T(8,128)(2,1)} %param.9) | copy-start | bytes 25165828
  0.6 21.8 %copy-start.1 = (bf16[32,256,64]{1,2,0:T(8,128)(2,1)S(1)}, bf16[32,256,64]{1,2,0:T(8,128)(2,1)}, u32[]{:S(2)}) copy-start(bf16[32,256,64]{1,2,0:T(8,128)(2,1)} %param.8) | copy-start | bytes 3145732
  0.7 21.8 %copy-start.3 = (s32[8,4]{0,1:T(4,128)S(1)}, s32[8,4]{0,1:T(4,128)}, u32[]{:S(2)}) copy-start(s32[8,4]{0,1:T(4,128)} %param.10) | copy-start | bytes 388
  0.7 21.8 %copy-start.6 = (s32[32]{0:T(128)S(1)}, s32[32]{0:T(128)}, u32[]{:S(2)}) copy-start(s32[32]{0:T(128)} %owner_ref.5) | copy-start | bytes 388
  22.5 1.0 %copy-start.7 = (bf16[8,256,128]{2,1,0:T(8,128)(2,1)S(1)}, bf16[8,256,128]{2,1,0:T(8,128)(2,1)}, u32[]{:S(2)}) copy-start(bf16[8,256,128]{2,1,0:T(8,128)(2,1)} %get-tuple-element.8) | copy-start | bytes 1572868
  23.5 3.5 %copy-start.4 = (s32[48,2]{0,1:T(2,128)S(1)}, s32[48,2]{0,1:T(2,128)}, u32[]{:S(2)}) copy-start(s32[48,2]{0,1:T(2,128)} %param.11) | copy-start | bytes 1156
  23.5 3.5 %copy-start.9 = (f32[192,32,128]{2,1,0:T(8,128)S(1)}, f32[192,32,128]{2,1,0:T(8,128)}, u32[]{:S(2)}) copy-start(f32[192,32,128]{2,1,0:T(8,128)} %get-tuple-element.9.weights_ref) | copy-start | bytes 9437188
  51.9 3.6 %copy-start.2 = (bf16[32,1024]{1,0:T(8,128)(2,1)S(1)}, bf16[32,1024]{1,0:T(8,128)(2,1)}, u32[]{:S(2)}) copy-start(bf16[32,1024]{1,0:T(8,128)(2,1)} %old_ref.1) | copy-start | bytes 196612
  51.9 3.6 %copy-start.5 = (f32[129]{0:T(256)S(1)}, f32[129]{0:T(256)}, u32[]{:S(2)}) copy-start(f32[129]{0:T(256)} %param.15) | copy-start | bytes 1552
  55.5 26.3 %copy-start.8 = (bf16[8,256,128]{2,1,0:T(8,128)(2,1)S(1)}, bf16[8,256,128]{2,1,0:T(8,128)(2,1)}, u32[]{:S(2)}) copy-start(bf16[8,256,128]{2,1,0:T(8,128)(2,1)} %get-tuple-element.8) | copy-start | bytes 1572868
